TPU v7x, 128 devices: a whole 4x4x4 slice. The times are simulated.
128 devices in a mesh: fsdp: 16 (over z, x), seq: 8 (over y, core).
Axes of the slice: x: 4, y: 4, z: 4, core: 2. Of those that a mesh axis runs over, the one named last changes fastest.
Arguments:
- tokens: bfloat16 [16384, 768], P(('fsdp', 'seq')), may hold values from -6 to 6
- segments: int32 [16, 1024], P('fsdp'), may hold values from 0 to 2, as said below
- routes: int32 [16384, 1], P(('fsdp', 'seq')), may hold values from 0 to 127; in each aligned block of 128 rows (0 to 127, 128 to 255, ...) at most 2 rows name the same one
- gain_attn: bfloat16 [768], P(('fsdp', 'seq')), may hold values from 0.25 to 1.75
- w_query: bfloat16 [768, 768], P(('fsdp', 'seq')), may hold values from -0.21875 to 0.21875
- w_key: bfloat16 [768, 768], P(('fsdp', 'seq')), may hold values from -0.21875 to 0.21875
- w_value: bfloat16 [768, 768], P(('fsdp', 'seq')), may hold values from -0.21875 to 0.21875
- w_output: bfloat16 [768, 768], P(('fsdp', 'seq')), may hold values from -0.875 to 0.875
- rel_table: bfloat16 [384], P(('fsdp', 'seq')), may hold values from -6 to 6
- gain_moe: bfloat16 [768], P(('fsdp', 'seq')), may hold values from 0.25 to 1.75
- w_router: bfloat16 [768, 128], P(('fsdp', 'seq')), may hold values from -0.15625 to 0.15625
- w_inner: bfloat16 [128, 768, 3072], P(('fsdp', 'seq')), may hold values from -0.21875 to 0.21875
- w_outer: bfloat16 [128, 3072, 768], P(('fsdp', 'seq')), may hold values from -12 to 12
- cotangent: bfloat16 [16384, 768], P(('fsdp', 'seq')), may hold values from -6 to 6
Outputs:
- layer_out: bfloat16 [16384, 768], P(('fsdp', 'seq'))
- tokens_grad: float32 [16384, 768], P(('fsdp', 'seq'))
- gain_attn_grad: bfloat16 [768], P(('fsdp', 'seq'))
- w_query_grad: bfloat16 [768, 768], P(('fsdp', 'seq'))
- w_key_grad: bfloat16 [768, 768], P(('fsdp', 'seq'))
- w_value_grad: bfloat16 [768, 768], P(('fsdp', 'seq'))
- w_output_grad: bfloat16 [768, 768], P(('fsdp', 'seq'))
- rel_table_grad: bfloat16 [384], P(('fsdp', 'seq'))
- gain_moe_grad: bfloat16 [768], P(('fsdp', 'seq'))
- w_router_grad: bfloat16 [768, 128], P(('fsdp', 'seq'))
- w_inner_grad: bfloat16 [128, 768, 3072], P(('fsdp', 'seq'))
- w_outer_grad: bfloat16 [128, 3072, 768], P(('fsdp', 'seq'))
Inputs may be any that keep to these rules, and one draw needn't show every extreme that they name: `routes`: among the 128 rows of one device no expert is named more than 2 times; some expert is named exactly 2 times in some device's rows. `segments`: document numbers never fall along a sequence and every sequence has all three. Document 0 fills the first 96 to 127 positions, document 2 the last 96 to 127 positions, and document 1 the rest.
All inputs are finite; a program needn't handle non-finite values.
Results may differ from a plain program's by a relative error of at most 0.03.
Values may be sent and summed in bfloat16 or wider, within the bound.
No kernel may reach another device: no remote copies, remote signals or barrier semaphores. Data moves between devices by JAX's collectives and lax.ppermute only.
A program may use at most 128 MiB of HBM per device.

v0:
```python
import jax
import jax.numpy as jnp
from jax import lax
from jax.sharding import PartitionSpec as P

HEADS = 12
HEAD_DIM = 64
BUCKETS = 32


eps = 1e-06
bucket_edges = (12, 16, 23, 32, 46, 64, 91)


def normed(values, gain):
    return values * lax.rsqrt(jnp.mean(values * values, axis=-1, keepdims=True) + eps) * gain


def bucket_of(offsets):
    spread = jnp.abs(offsets)
    bucket_ids = (offsets > 0).astype(jnp.int32) * 16 + jnp.minimum(spread, 8)
    for border in bucket_edges:
        bucket_ids = bucket_ids + (spread >= border).astype(jnp.int32)
    return bucket_ids


def inner_rows(left, right):
    return lax.dot_general(
        left, right, (((0,), (0,)), ((), ())), preferred_element_type=jnp.float32
    )


def times_trans(left, right):
    return lax.dot_general(
        left, right, (((1,), (1,)), ((), ())), preferred_element_type=jnp.float32
    )


def bucket_table(offsets, bucket_count):
    bucket_ids = bucket_of(offsets).reshape(1, -1)
    return (bucket_ids == jnp.arange(bucket_count, dtype=jnp.int32)[:, None]).astype(jnp.bfloat16)


def bias_from(table_low, bucket_hot, rows, cols):
    flat_bias = jnp.dot(table_low, bucket_hot, preferred_element_type=jnp.float32)
    return flat_bias.reshape(table_low.shape[0], rows, cols)


def masked_scores(query_part, key_part, bias, same_doc):
    scale = query_part.shape[-1] ** (-0.5)
    scores = (
        jnp.einsum("rgd,kgd->grk", query_part, key_part, preferred_element_type=jnp.float32) * scale
        + bias
    )
    return jnp.where(same_doc[None], scores, -1e30)


def attend_forward(query_part, key_part, value_part, bias, same_doc):
    scores = masked_scores(query_part, key_part, bias, same_doc)
    top_score = jnp.max(scores, axis=-1, keepdims=True)
    exp_scores = jnp.exp(scores - top_score)
    exp_total = jnp.sum(exp_scores, axis=-1, keepdims=True)
    soft_low = (exp_scores / exp_total).astype(jnp.bfloat16)
    mixed_part = jnp.einsum(
        "grk,kgd->rgd", soft_low, value_part, preferred_element_type=jnp.float32
    )
    return (mixed_part, top_score + jnp.log(exp_total))


def attend_backward(
    query_part, key_part, value_part, bias, bucket_hot, same_doc, logsum, grad_mixed
):
    scale = query_part.shape[-1] ** (-0.5)
    scores = masked_scores(query_part, key_part, bias, same_doc)
    soft_full = jnp.exp(scores - logsum)
    soft_low = soft_full.astype(jnp.bfloat16)
    grad_soft = jnp.einsum(
        "rgd,kgd->grk", grad_mixed, value_part, preferred_element_type=jnp.float32
    )
    row_inner = jnp.sum(soft_full * grad_soft, axis=-1, keepdims=True)
    grad_scores = (soft_full * (grad_soft - row_inner)).astype(jnp.bfloat16)
    grad_query = (
        jnp.einsum("grk,kgd->rgd", grad_scores, key_part, preferred_element_type=jnp.float32)
        * scale
    )
    grad_key = (
        jnp.einsum("grk,rgd->kgd", grad_scores, query_part, preferred_element_type=jnp.float32)
        * scale
    )
    grad_value = jnp.einsum(
        "grk,rgd->kgd", soft_low, grad_mixed, preferred_element_type=jnp.float32
    )
    flat_scores = grad_scores.reshape(grad_scores.shape[0], -1)
    grad_table = times_trans(flat_scores, bucket_hot)
    return (grad_query, grad_key, grad_value, grad_table, row_inner)


def on_device(
    tokens,
    segments,
    routes,
    gain_attn,
    w_query,
    w_key,
    w_value,
    w_output,
    rel_table,
    gain_moe,
    w_router,
    w_inner,
    w_outer,
    cotangent,
):
    row_count, model_width = tokens.shape
    length = segments.shape[1]
    head_count = HEADS
    head_dim = HEAD_DIM
    bucket_count = BUCKETS
    gathered = (
        lax.all_gather(gain_attn, ("fsdp", "seq"), axis=0, tiled=True),
        lax.all_gather(w_query, ("fsdp", "seq"), axis=0, tiled=True),
        lax.all_gather(w_key, ("fsdp", "seq"), axis=0, tiled=True),
        lax.all_gather(w_value, ("fsdp", "seq"), axis=0, tiled=True),
        lax.all_gather(w_output, ("fsdp", "seq"), axis=0, tiled=True),
        lax.all_gather(rel_table, ("fsdp", "seq"), axis=0, tiled=True),
        lax.all_gather(gain_moe, ("fsdp", "seq"), axis=0, tiled=True),
        lax.all_gather(w_router, ("fsdp", "seq"), axis=0, tiled=True),
    )
    gain_one, query_w, key_w, value_w, output_w, table_flat, gain_two, router_w = gathered
    seq_index = lax.axis_index("seq")
    positions = seq_index * row_count + jnp.arange(row_count, dtype=jnp.int32)
    key_places = jnp.arange(length, dtype=jnp.int32)
    bucket_hot = bucket_table(key_places[None, :] - positions[:, None], bucket_count)
    doc_ids = segments[0]
    own_docs = lax.dynamic_slice_in_dim(doc_ids, seq_index * row_count, row_count)
    same_doc = own_docs[:, None] == doc_ids[None, :]
    inputs = tokens.astype(jnp.float32)
    normed_low = normed(inputs, gain_one.astype(jnp.float32)).astype(jnp.bfloat16)
    query_low = jnp.dot(normed_low, query_w, preferred_element_type=jnp.float32).astype(
        jnp.bfloat16
    )
    key_low = jnp.dot(normed_low, key_w, preferred_element_type=jnp.float32).astype(jnp.bfloat16)
    value_low = jnp.dot(normed_low, value_w, preferred_element_type=jnp.float32).astype(
        jnp.bfloat16
    )
    key_all, value_all = (
        lax.all_gather(key_low, "seq", axis=0, tiled=True),
        lax.all_gather(value_low, "seq", axis=0, tiled=True),
    )
    heads_query = query_low.reshape(row_count, head_count, head_dim)
    heads_key = key_all.reshape(length, head_count, head_dim)
    heads_value = value_all.reshape(length, head_count, head_dim)
    bias_fwd = bias_from(
        table_flat.reshape(head_count, bucket_count), bucket_hot, row_count, length
    )
    mixed_part, logsum = attend_forward(heads_query, heads_key, heads_value, bias_fwd, same_doc)
    mixed_low = mixed_part.reshape(row_count, model_width).astype(jnp.bfloat16)
    hidden = inputs + jnp.dot(mixed_low, output_w, preferred_element_type=jnp.float32)
    second_low = normed(hidden, gain_two.astype(jnp.float32)).astype(jnp.bfloat16)
    logits = jnp.dot(second_low, router_w, preferred_element_type=jnp.float32)
    exp_logits = jnp.exp(logits - jnp.max(logits, axis=-1, keepdims=True))
    router_prob = exp_logits / jnp.sum(exp_logits, axis=-1, keepdims=True)
    experts_all = router_w.shape[1]
    capacity = max(2, 2 * row_count // experts_all)
    route_col = routes[:, 0]
    picked = (route_col[:, None] == jnp.arange(experts_all, dtype=jnp.int32)[None, :]).astype(
        jnp.float32
    )
    gate_prob = jnp.sum(router_prob * picked, axis=-1, keepdims=True)
    earlier = (jnp.arange(row_count)[:, None] > jnp.arange(row_count)[None, :]).astype(jnp.float32)
    ranks = jnp.dot(earlier, picked, precision=lax.Precision.HIGHEST)
    slot_index = jnp.sum(ranks * picked, axis=-1).astype(jnp.int32)
    send_rows = (
        jnp.zeros((experts_all, capacity, model_width), jnp.bfloat16)
        .at[route_col, slot_index]
        .set(second_low)
    )
    inner_own = w_inner[0]
    outer_own = w_outer[0]
    arrived = lax.all_to_all(send_rows, ("fsdp", "seq"), split_axis=0, concat_axis=0, tiled=True)
    sources = arrived.shape[0]
    slots = arrived.shape[1]
    flat_in = arrived.reshape(sources * slots, model_width)
    pre_act = jnp.dot(flat_in, inner_own, preferred_element_type=jnp.float32)
    act_low = jax.nn.gelu(pre_act).astype(jnp.bfloat16)
    result = jnp.dot(act_low, outer_own, preferred_element_type=jnp.float32).astype(jnp.bfloat16)
    expert_out = result.reshape(sources, slots, model_width)
    pre_kept = pre_act.reshape(sources, slots, -1)
    came_back = lax.all_to_all(expert_out, ("fsdp", "seq"), split_axis=0, concat_axis=0, tiled=True)
    returned = came_back[route_col, slot_index].astype(jnp.float32)
    layer_out = (hidden + gate_prob * returned).astype(jnp.bfloat16)
    regathered = (
        lax.all_gather(gain_attn, ("fsdp", "seq"), axis=0, tiled=True),
        lax.all_gather(w_query, ("fsdp", "seq"), axis=0, tiled=True),
        lax.all_gather(w_key, ("fsdp", "seq"), axis=0, tiled=True),
        lax.all_gather(w_value, ("fsdp", "seq"), axis=0, tiled=True),
        lax.all_gather(w_output, ("fsdp", "seq"), axis=0, tiled=True),
        lax.all_gather(rel_table, ("fsdp", "seq"), axis=0, tiled=True),
        lax.all_gather(gain_moe, ("fsdp", "seq"), axis=0, tiled=True),
        lax.all_gather(w_router, ("fsdp", "seq"), axis=0, tiled=True),
    )
    (
        gain_back,
        query_back,
        key_back,
        value_back,
        output_back,
        table_back,
        gain_later,
        router_back,
    ) = regathered
    keys_back, values_back = (
        lax.all_gather(key_low, "seq", axis=0, tiled=True),
        lax.all_gather(value_low, "seq", axis=0, tiled=True),
    )
    table_low = table_back.reshape(head_count, bucket_count)
    upstream = cotangent.astype(jnp.float32)
    grad_returned = (gate_prob * upstream).astype(jnp.bfloat16)
    grad_gate = jnp.sum(upstream * returned, axis=-1, keepdims=True)
    grad_logits = (grad_gate * gate_prob * (picked - router_prob)).astype(jnp.bfloat16)
    grad_send = (
        jnp.zeros((experts_all, capacity, model_width), jnp.bfloat16)
        .at[route_col, slot_index]
        .set(grad_returned)
    )
    arrived_grad = lax.all_to_all(
        grad_send, ("fsdp", "seq"), split_axis=0, concat_axis=0, tiled=True
    )
    flat_grad = arrived_grad.reshape(-1, model_width)
    pre_flat = pre_kept.reshape(flat_grad.shape[0], -1)
    arrived_flat = arrived.reshape(-1, model_width)
    act_low = jax.nn.gelu(pre_flat).astype(jnp.bfloat16)
    grad_outer = inner_rows(act_low, flat_grad)
    grad_act = times_trans(flat_grad, outer_own)
    _, pull_gelu = jax.vjp(jax.nn.gelu, pre_flat)
    (grad_pre,) = pull_gelu(grad_act)
    grad_pre_low = grad_pre.astype(jnp.bfloat16)
    grad_inner = inner_rows(arrived_flat, grad_pre_low)
    grad_arrived = (
        times_trans(grad_pre_low, inner_own).astype(jnp.bfloat16).reshape(arrived_grad.shape)
    )
    token_back = lax.all_to_all(
        grad_arrived, ("fsdp", "seq"), split_axis=0, concat_axis=0, tiled=True
    )
    grad_second = token_back[route_col, slot_index].astype(jnp.float32) + times_trans(
        grad_logits, router_back
    )
    grad_router = inner_rows(second_low, grad_logits)
    _, pull_second = jax.vjp(normed, hidden, gain_later.astype(jnp.float32))
    grad_hidden_part, grad_gain_two = pull_second(grad_second)
    grad_hidden = upstream + grad_hidden_part
    grad_attn_low = grad_hidden.astype(jnp.bfloat16)
    grad_output_w = inner_rows(mixed_low, grad_attn_low)
    grad_mixed = (
        times_trans(grad_attn_low, output_back)
        .astype(jnp.bfloat16)
        .reshape(row_count, head_count, head_dim)
    )
    heads_key_back = keys_back.reshape(length, head_count, head_dim)
    heads_value_back = values_back.reshape(length, head_count, head_dim)
    bias_back = bias_from(table_low, bucket_hot, row_count, length)
    grad_query, key_terms, value_terms, grad_table, row_inner = attend_backward(
        heads_query,
        heads_key_back,
        heads_value_back,
        bias_back,
        bucket_hot,
        same_doc,
        logsum,
        grad_mixed,
    )
    query_grad_low = grad_query.reshape(row_count, model_width).astype(jnp.bfloat16)
    key_flat = key_terms.reshape(length, model_width)
    value_flat = value_terms.reshape(length, model_width)
    key_grad, value_grad = (
        lax.psum_scatter(
            key_flat.astype(jnp.bfloat16), "seq", scatter_dimension=0, tiled=True
        ).astype(jnp.float32),
        lax.psum_scatter(
            value_flat.astype(jnp.bfloat16), "seq", scatter_dimension=0, tiled=True
        ).astype(jnp.float32),
    )
    key_grad_low = key_grad.astype(jnp.bfloat16)
    value_grad_low = value_grad.astype(jnp.bfloat16)
    grad_query_w = inner_rows(normed_low, query_grad_low)
    grad_key_w = inner_rows(normed_low, key_grad_low)
    grad_value_w = inner_rows(normed_low, value_grad_low)
    grad_first = (
        times_trans(query_grad_low, query_back)
        + times_trans(key_grad_low, key_back)
        + times_trans(value_grad_low, value_back)
    )
    _, pull_first = jax.vjp(normed, inputs, gain_back.astype(jnp.float32))
    grad_inputs_part, grad_gain_one = pull_first(grad_first)
    tokens_grad = grad_hidden + grad_inputs_part
    table_grad_all = grad_table.reshape(-1)
    summed = (
        lax.psum_scatter(grad_gain_one, ("fsdp", "seq"), scatter_dimension=0, tiled=True),
        lax.psum_scatter(grad_query_w, ("fsdp", "seq"), scatter_dimension=0, tiled=True),
        lax.psum_scatter(grad_key_w, ("fsdp", "seq"), scatter_dimension=0, tiled=True),
        lax.psum_scatter(grad_value_w, ("fsdp", "seq"), scatter_dimension=0, tiled=True),
        lax.psum_scatter(grad_output_w, ("fsdp", "seq"), scatter_dimension=0, tiled=True),
        lax.psum_scatter(table_grad_all, ("fsdp", "seq"), scatter_dimension=0, tiled=True),
        lax.psum_scatter(grad_gain_two, ("fsdp", "seq"), scatter_dimension=0, tiled=True),
        lax.psum_scatter(grad_router, ("fsdp", "seq"), scatter_dimension=0, tiled=True),
    )
    return (
        layer_out,
        tokens_grad,
        summed[0].astype(jnp.bfloat16),
        summed[1].astype(jnp.bfloat16),
        summed[2].astype(jnp.bfloat16),
        summed[3].astype(jnp.bfloat16),
        summed[4].astype(jnp.bfloat16),
        summed[5].astype(jnp.bfloat16),
        summed[6].astype(jnp.bfloat16),
        summed[7].astype(jnp.bfloat16),
        grad_inner[None].astype(jnp.bfloat16),
        grad_outer[None].astype(jnp.bfloat16),
    )


def solution(mesh):
    placed = (
        P(("fsdp", "seq"), None),
        P("fsdp", None),
        P(("fsdp", "seq"), None),
        P(("fsdp", "seq")),
        P(("fsdp", "seq"), None),
        P(("fsdp", "seq"), None),
        P(("fsdp", "seq"), None),
        P(("fsdp", "seq"), None),
        P(("fsdp", "seq")),
        P(("fsdp", "seq")),
        P(("fsdp", "seq"), None),
        P(("fsdp", "seq"), None, None),
        P(("fsdp", "seq"), None, None),
        P(("fsdp", "seq"), None),
    )
    return jax.shard_map(
        on_device,
        mesh=mesh,
        in_specs=placed,
        out_specs=(
            P(("fsdp", "seq"), None),
            P(("fsdp", "seq"), None),
            P(("fsdp", "seq")),
            P(("fsdp", "seq"), None),
            P(("fsdp", "seq"), None),
            P(("fsdp", "seq"), None),
            P(("fsdp", "seq"), None),
            P(("fsdp", "seq")),
            P(("fsdp", "seq")),
            P(("fsdp", "seq"), None),
            P(("fsdp", "seq"), None, None),
            P(("fsdp", "seq"), None, None),
        ),
        check_vma=False,
    )
```

profile of v0, /device:TPU:1, one launch (start us, length us, event | category | flops | bytes accessed | tf_op | source)
XLA Modules:
  0.0 1425.0 jit_solution(1437046093933562896)
XLA Ops:
  12.6 69.2 %all-reduce.16 = (bf16[768]{0:T(1024)(128)(2,1)S(1)}, bf16[384]{0:T(512)(128)(2,1)S(1)}, bf16[768]{0:T(1024)(128)(2,1)S(1)}) all-reduce(bf16[768]{0:T(1024)(128)(2,1)S(1)} %dynamic-update-slice, bf16[384]{0:T(512)(128)(2,1)S(1)} %dynamic-update-slice.1, ...), channel_id=1, replica_groups=mesh['fsdp'=16,'seq'=8] {'fsdp','seq'}, use_global_device_ids=true, to_apply=%add | all-reduce | flops 1920 | bytes 7680
  86.6 56.7 %all-gather.16.cloned.1.call-done = bf16[128,6,768]{2,1,0:T(8,128)(2,1)} async-done(((bf16[1,6,768]{2,1,0:T(8,128)(2,1)}), bf16[128,6,768]{2,1,0:T(8,128)(2,1)}) %all-gather.16.cloned.1.call-update) | async-done | bytes 1179664 | tf_op jit(solution)/shard_map/all_gather | solution.py:123
  150.1 8.1 copy.47
  158.6 49.1 %all-gather.18.cloned.1.call-done = bf16[128,6,768]{2,1,0:T(8,128)(2,1)} async-done(((bf16[1,6,768]{2,1,0:T(8,128)(2,1)}), bf16[128,6,768]{2,1,0:T(8,128)(2,1)}) %all-gather.18.cloned.1.call-update) | async-done | bytes 1179664 | tf_op jit(solution)/shard_map/all_gather | solution.py:121
  210.6 61.4 %all-gather.22.cloned.1.call-done = bf16[128,6,768]{2,1,0:T(8,128)(2,1)} async-done(((bf16[1,6,768]{2,1,0:T(8,128)(2,1)}), bf16[128,6,768]{2,1,0:T(8,128)(2,1)}) %all-gather.22.cloned.1.call-update) | async-done | bytes 1179664 | tf_op jit(solution)/shard_map/all_gather | solution.py:124
  274.4 21.6 %all-gather.14.cloned.1.call-done = bf16[1024,768]{1,0:T(8,128)(2,1)} async-done(((bf16[128,768]{1,0:T(8,128)(2,1)}), bf16[1024,768]{1,0:T(8,128)(2,1)}) %all-gather.14.cloned.1.call-update) | async-done | bytes 1572880 | tf_op jit(solution)/shard_map/all_gather | solution.py:147
  298.2 4.9 fusion.92
  307.2 15.4 %all-gather.12.cloned.1.call-done = bf16[1024,768]{1,0:T(8,128)(2,1)} async-done(((bf16[128,768]{1,0:T(8,128)(2,1)}), bf16[1024,768]{1,0:T(8,128)(2,1)}) %all-gather.12.cloned.1.call-update) | async-done | bytes 1572880 | tf_op jit(solution)/shard_map/all_gather | solution.py:148
  324.3 4.8 fusion.44
  330.9 17.0 %scatter_fusion = bf16[128,2,768]{2,1,0:T(2,128)(2,1)} fusion(bf16[128,2,768]{2,1,0:T(2,128)(2,1)} %broadcast.214.clone, s32[128]{0:T(128)S(1)} %get-tuple-element.31, bf16[128,768]{1,0:T(8,128)(2,1)S(1)} %multiply_convert_fusion.3), kind=kCustom, calls=%fused_computation.2 | custom fusion | bytes 590848 | tf_op jit(solution)/shard_map/scatter | solution.py:176
  347.9 8.1 all-to-all-start
  356.0 37.0 %all-gather.4 = bf16[128,6,128]{2,1,0:T(8,128)(2,1)S(1)} all-gather(bf16[1,6,128]{2,1,0:T(8,128)(2,1)S(1)} %bitcast.137), channel_id=1, replica_groups=mesh['fsdp'=16,'seq'=8] {'fsdp','seq'}, dimensions={0}, use_global_device_ids=true | all-gather | bytes 198144 | tf_op jit(solution)/shard_map/all_gather | solution.py:127
  393.2 3.9 fusion.17
  398.8 4.3 fusion.40
  404.1 6.1 all-to-all-start.1
  410.5 11.8 all-to-all-done.1
  423.9 7.8 scatter_fusion.1
  431.8 16.4 %all_to_all.20 = bf16[128,2,768]{2,1,0:T(2,128)(2,1)S(1)} all-to-all(bf16[128,2,768]{2,1,0:T(2,128)(2,1)S(1)} %scatter_fusion.1), channel_id=1, replica_groups=mesh['fsdp'=16,'seq'=8] {'fsdp','seq'}, dimensions={0} | all-to-all | bytes 786432 | tf_op jit(solution)/shard_map/all_to_all | solution.py:226
  448.3 6.8 fusion.27
  460.9 4.6 all-to-all-start.3
  465.6 12.0 all-to-all-done.3
  483.9 4.4 multiply_reduce_fusion
  494.4 5.3 fusion.34
  509.8 10.9 reduce-scatter.15.cloned.1.call-done
  523.7 31.0 %reduce-scatter.17.cloned.1.call-done = bf16[128,768]{1,0:T(8,128)(2,1)} async-done(((bf16[1024,768]{1,0:T(8,128)(2,1)}), bf16[128,768]{1,0:T(8,128)(2,1)}) %reduce-scatter.17.cloned.1.call-update) | async-done | bytes 196624
  557.6 368.2 %fusion.86 = (f32[8,768]{1,0:T(8,128)}, f32[8,768]{1,0:T(8,128)}, f32[8,768]{1,0:T(8,128)}, f32[8,768]{1,0:T(8,128)}) fusion(f32[768,768]{1,0:T(8,128)} %fusion.81, f32[768,768]{1,0:T(8,128)} %fusion.79, f32[768,768]{1,0:T(8,128)} %fusion.77, f32[768,768]{1,0:T(8,128)} %fusion.66), kind=kCustom, calls=%all-reduce-scatter.4 | all-reduce-scatter fusion | flops 3145729 | bytes 9535488
  934.0 5.7 collective-permute-start.29
  952.4 11.4 collective-permute-start.22
  986.6 4.3 collective-permute-start.12
  1039.0 4.2 collective-permute-start.53
  1068.1 4.1 collective-permute-start.42
  1080.4 4.0 collective-permute-start.37
  1112.0 6.4 fusion.20
  1157.8 4.1 collective-permute-start.74
  1182.5 4.0 collective-permute-start.66
  1212.3 66.6 %all-reduce.19 = (bf16[768]{0:T(1024)(128)(2,1)S(1)}, bf16[384]{0:T(512)(128)(2,1)S(1)}, bf16[768]{0:T(1024)(128)(2,1)S(1)}, bf16[768,128]{1,0:T(8,128)(2,1)S(1)}) all-reduce(f32[768]{0:T(1024)S(1)} %get-tuple-element.14, f32[384]{0:T(512)S(1)} %copy-done.128, ...), channel_id=4, replica_groups=mesh['fsdp'=16,'seq'=8] {'fsdp','seq'}, use_global_device_ids=true, to_apply=%region_17.18.clone | all-reduce | flops 100224 | bytes 601344
  1279.0 4.7 collective-permute-start.115
  1286.9 4.7 collective-permute-start.113
  1291.6 4.1 collective-permute-start.112
  1295.7 4.4 collective-permute-start.111
  1302.5 27.3 %concatenate.15 = bf16[262,768]{1,0:T(8,128)(2,1)S(1)} concatenate(bf16[6,768]{1,0:T(8,128)(2,1)} %copy-done.42, bf16[8,768]{1,0:T(8,128)(2,1)} %copy-done.43, bf16[8,768]{1,0:T(8,128)(2,1)} %copy-done.44, bf16[8,768]{1,0:T(8,128)(2,1)} %copy-done.45, bf16[8,768]{1,0:T(8,128)(2,1)} %copy-done.46, bf16[8,768]{1,0:T(8,128)(2,1)} %copy-done.47, bf16[8,768]{1,0:T(8,128)(2,1)} %copy-done.48, ...), dimensions={0} | concatenate | bytes 817152
  1332.6 3.9 collective-permute-start.109
  1336.6 4.4 collective-permute-start.108
  1344.5 4.0 collective-permute-start.106
  1349.1 27.3 %concatenate.16 = bf16[262,768]{1,0:T(8,128)(2,1)S(1)} concatenate(bf16[6,768]{1,0:T(8,128)(2,1)} %copy-done.41, bf16[8,768]{1,0:T(8,128)(2,1)} %copy-done.68, bf16[8,768]{1,0:T(8,128)(2,1)} %copy-done.70, bf16[8,768]{1,0:T(8,128)(2,1)} %copy-done.72, bf16[8,768]{1,0:T(8,128)(2,1)} %copy-done.74, bf16[8,768]{1,0:T(8,128)(2,1)} %copy-done.76, bf16[8,768]{1,0:T(8,128)(2,1)} %copy-done.77, ...), dimensions={0} | concatenate | bytes 817152
  1388.4 8.9 concatenate.17
  1403.9 3.9 collective-permute-start.98
  1413.4 4.0 concatenate.18
  (621 shorter events, 343.9 us)
Async XLA Ops:
  7.2 75.6 %all-gather.20.cloned.1.call-start = ((), (), s32[]{:S(2)}) async-start(), calls=%async_computation.10 | async-start | bytes 1585152 | tf_op jit(solution)/shard_map/all_gather | solution.py:122
  7.9 135.4 %all-gather.16.cloned.1.call-start = ((), (), s32[]{:S(2)}) async-start(), calls=%async_computation.8 | async-start | bytes 1585152 | tf_op jit(solution)/shard_map/all_gather | solution.py:123
  8.7 199.1 %all-gather.18.cloned.1.call-start = ((), (), s32[]{:S(2)}) async-start(), calls=%async_computation.9 | async-start | bytes 1585152 | tf_op jit(solution)/shard_map/all_gather | solution.py:121
  9.4 262.6 %all-gather.22.cloned.1.call-start = ((), (), s32[]{:S(2)}) async-start(), calls=%async_computation.11 | async-start | bytes 1585152 | tf_op jit(solution)/shard_map/all_gather | solution.py:124
  10.0 286.0 %all-gather.14.cloned.1.call-start = ((), (), s32[]{:S(2)}) async-start(), calls=%async_computation.7 | async-start | bytes 1769472 | tf_op jit(solution)/shard_map/all_gather | solution.py:147
  86.3 236.4 %all-gather.12.cloned.1.call-start = ((), (), s32[]{:S(2)}) async-start(), calls=%async_computation.6 | async-start | bytes 1769472 | tf_op jit(solution)/shard_map/all_gather | solution.py:148
  347.9 45.1 %all-to-all-start = ((bf16[128,2,768]{2,1,0:T(2,128)(2,1)}), bf16[128,2,768]{2,1,0:T(2,128)(2,1)S(1)}, u32[]{:S(2)}, u32[]{:S(2)}) async-start(bf16[128,2,768]{2,1,0:T(2,128)(2,1)} %scatter_fusion), calls=%async_computation | async-start | bytes 786432 | tf_op jit(solution)/shard_map/all_to_all | solution.py:180
  404.1 18.2 %all-to-all-start.1 = ((bf16[128,2,768]{2,1,0:T(2,128)(2,1)}), bf16[128,2,768]{2,1,0:T(2,128)(2,1)S(1)}, u32[]{:S(2)}, u32[]{:S(2)}) async-start(bf16[128,2,768]{2,1,0:T(2,128)(2,1)} %reshape.272), calls=%async_computation.1 | async-start | bytes 786432 | tf_op jit(solution)/shard_map/all_to_all | solution.py:189
  460.9 16.8 %all-to-all-start.3 = ((bf16[128,2,768]{2,1,0:T(2,128)(2,1)}), bf16[128,2,768]{2,1,0:T(2,128)(2,1)S(1)}, u32[]{:S(2)}, u32[]{:S(2)}) async-start(bf16[128,2,768]{2,1,0:T(2,128)(2,1)} %reshape.274), calls=%async_computation.3 | async-start | bytes 786432 | tf_op jit(solution)/shard_map/all_to_all | solution.py:242
  465.6 55.2 %reduce-scatter.15.cloned.1.call-start = ((), (), s32[]{:S(2)}) async-start(), calls=%async_computation.12 | async-start | bytes 1769472
  494.4 60.3 %reduce-scatter.17.cloned.1.call-start = ((), (), s32[]{:S(2)}) async-start(), calls=%async_computation.13 | async-start | bytes 1769472
  947.1 16.6 %collective-permute-start.26 = (bf16[8,768]{1,0:T(8,128)(2,1)S(1)}, bf16[8,768]{1,0:T(8,128)(2,1)S(1)}, u32[]{:S(2)}, u32[]{:S(2)}) collective-permute-start(bf16[8,768]{1,0:T(8,128)(2,1)S(1)} %convert.258), channel_id=1, source_target_pairs={{0,27},{1,28},{2,29},{3,30},{4,31},{5,32},{6,33},{7,34},{8,35},{9,... | collective-permute-start | bytes 36872
  948.4 18.8 %collective-permute-start.25 = (bf16[8,768]{1,0:T(8,128)(2,1)S(1)}, bf16[8,768]{1,0:T(8,128)(2,1)S(1)}, u32[]{:S(2)}, u32[]{:S(2)}) collective-permute-start(bf16[8,768]{1,0:T(8,128)(2,1)S(1)} %convert.258), channel_id=1, source_target_pairs={{0,26},{1,27},{2,28},{3,29},{4,30},{5,31},{6,32},{7,33},{8,34},{9,... | collective-permute-start | bytes 36872
  949.7 20.7 %collective-permute-start.24 = (bf16[8,768]{1,0:T(8,128)(2,1)S(1)}, bf16[8,768]{1,0:T(8,128)(2,1)S(1)}, u32[]{:S(2)}, u32[]{:S(2)}) collective-permute-start(bf16[8,768]{1,0:T(8,128)(2,1)S(1)} %convert.258), channel_id=1, source_target_pairs={{0,25},{1,26},{2,27},{3,28},{4,29},{5,30},{6,31},{7,32},{8,33},{9,... | collective-permute-start | bytes 36872
  951.1 21.6 %collective-permute-start.23 = (bf16[8,768]{1,0:T(8,128)(2,1)S(1)}, bf16[8,768]{1,0:T(8,128)(2,1)S(1)}, u32[]{:S(2)}, u32[]{:S(2)}) collective-permute-start(bf16[8,768]{1,0:T(8,128)(2,1)S(1)} %convert.258), channel_id=1, source_target_pairs={{0,24},{1,25},{2,26},{3,27},{4,28},{5,29},{6,30},{7,31},{8,32},{9,... | collective-permute-start | bytes 36872
  952.4 23.1 %collective-permute-start.22 = (bf16[8,768]{1,0:T(8,128)(2,1)S(1)}, bf16[8,768]{1,0:T(8,128)(2,1)S(1)}, u32[]{:S(2)}, u32[]{:S(2)}) collective-permute-start(bf16[8,768]{1,0:T(8,128)(2,1)S(1)} %convert.258), channel_id=1, source_target_pairs={{0,23},{1,24},{2,25},{3,26},{4,27},{5,28},{6,29},{7,30},{8,31},{9,... | collective-permute-start | bytes 36872
  1002.9 17.6 %collective-permute-start.6 = (bf16[8,768]{1,0:T(8,128)(2,1)S(1)}, bf16[8,768]{1,0:T(8,128)(2,1)S(1)}, u32[]{:S(2)}, u32[]{:S(2)}) collective-permute-start(bf16[8,768]{1,0:T(8,128)(2,1)S(1)} %convert.258), channel_id=1, source_target_pairs={{0,7},{1,8},{2,9},{3,10},{4,11},{5,12},{6,13},{7,14},{8,15},{9,16}... | collective-permute-start | bytes 36872
  1005.6 17.7 %collective-permute-start.5 = (bf16[8,768]{1,0:T(8,128)(2,1)S(1)}, bf16[8,768]{1,0:T(8,128)(2,1)S(1)}, u32[]{:S(2)}, u32[]{:S(2)}) collective-permute-start(bf16[8,768]{1,0:T(8,128)(2,1)S(1)} %convert.258), channel_id=1, source_target_pairs={{0,6},{1,7},{2,8},{3,9},{4,10},{5,11},{6,12},{7,13},{8,14},{9,15},... | collective-permute-start | bytes 36872
  1009.1 16.9 %collective-permute-start.4 = (bf16[8,768]{1,0:T(8,128)(2,1)S(1)}, bf16[8,768]{1,0:T(8,128)(2,1)S(1)}, u32[]{:S(2)}, u32[]{:S(2)}) collective-permute-start(bf16[8,768]{1,0:T(8,128)(2,1)S(1)} %convert.258), channel_id=1, source_target_pairs={{0,5},{1,6},{2,7},{3,8},{4,9},{5,10},{6,11},{7,12},{8,13},{9,14},{... | collective-permute-start | bytes 36872
  1077.9 16.7 %collective-permute-start.38 = (bf16[8,768]{1,0:T(8,128)(2,1)}, bf16[8,768]{1,0:T(8,128)(2,1)}, u32[]{:S(2)}, u32[]{:S(2)}) collective-permute-start(bf16[8,768]{1,0:T(8,128)(2,1)} %convert.257), channel_id=1, source_target_pairs={{0,7},{1,8},{2,9},{3,10},{4,11},{5,12},{6,13},{7,14},{8,15},{9,16}... | collective-permute-start | bytes 36872
  1118.4 18.0 %collective-permute-start.87 = (bf16[8,768]{1,0:T(8,128)(2,1)}, bf16[8,768]{1,0:T(8,128)(2,1)S(1)}, u32[]{:S(2)}, u32[]{:S(2)}) collective-permute-start(bf16[8,768]{1,0:T(8,128)(2,1)} %convert.256), channel_id=1, source_target_pairs={{0,24},{1,25},{2,26},{3,27},{4,28},{5,29},{6,30},{7,31},{8,32},{9,... | collective-permute-start | bytes 36872
  1119.7 19.0 %collective-permute-start.86 = (bf16[8,768]{1,0:T(8,128)(2,1)}, bf16[8,768]{1,0:T(8,128)(2,1)S(1)}, u32[]{:S(2)}, u32[]{:S(2)}) collective-permute-start(bf16[8,768]{1,0:T(8,128)(2,1)} %convert.256), channel_id=1, source_target_pairs={{0,23},{1,24},{2,25},{3,26},{4,27},{5,28},{6,29},{7,30},{8,31},{9,... | collective-permute-start | bytes 36872
  1121.0 19.1 %collective-permute-start.85 = (bf16[8,768]{1,0:T(8,128)(2,1)}, bf16[8,768]{1,0:T(8,128)(2,1)S(1)}, u32[]{:S(2)}, u32[]{:S(2)}) collective-permute-start(bf16[8,768]{1,0:T(8,128)(2,1)} %convert.256), channel_id=1, source_target_pairs={{0,22},{1,23},{2,24},{3,25},{4,26},{5,27},{6,28},{7,29},{8,30},{9,... | collective-permute-start | bytes 36872
  1123.8 18.5 %collective-permute-start.84 = (bf16[8,768]{1,0:T(8,128)(2,1)}, bf16[8,768]{1,0:T(8,128)(2,1)S(1)}, u32[]{:S(2)}, u32[]{:S(2)}) collective-permute-start(bf16[8,768]{1,0:T(8,128)(2,1)} %convert.256), channel_id=1, source_target_pairs={{0,21},{1,22},{2,23},{3,24},{4,25},{5,26},{6,27},{7,28},{8,29},{9,... | collective-permute-start | bytes 36872
  1126.7 17.2 %collective-permute-start.83 = (bf16[8,768]{1,0:T(8,128)(2,1)}, bf16[8,768]{1,0:T(8,128)(2,1)S(1)}, u32[]{:S(2)}, u32[]{:S(2)}) collective-permute-start(bf16[8,768]{1,0:T(8,128)(2,1)} %convert.256), channel_id=1, source_target_pairs={{0,20},{1,21},{2,22},{3,23},{4,24},{5,25},{6,26},{7,27},{8,28},{9,... | collective-permute-start | bytes 36872
  1143.9 17.9 %collective-permute-start.78 = (bf16[8,768]{1,0:T(8,128)(2,1)}, bf16[8,768]{1,0:T(8,128)(2,1)S(1)}, u32[]{:S(2)}, u32[]{:S(2)}) collective-permute-start(bf16[8,768]{1,0:T(8,128)(2,1)} %convert.256), channel_id=1, source_target_pairs={{0,15},{1,16},{2,17},{3,18},{4,19},{5,20},{6,21},{7,22},{8,23},{9,... | collective-permute-start | bytes 36872
  1169.2 17.4 %collective-permute-start.70 = (bf16[8,768]{1,0:T(8,128)(2,1)}, bf16[8,768]{1,0:T(8,128)(2,1)S(1)}, u32[]{:S(2)}, u32[]{:S(2)}) collective-permute-start(bf16[8,768]{1,0:T(8,128)(2,1)} %convert.256), channel_id=1, source_target_pairs={{0,7},{1,8},{2,9},{3,10},{4,11},{5,12},{6,13},{7,14},{8,15},{9,16}... | collective-permute-start | bytes 36872
  1171.2 17.8 %collective-permute-start.69 = (bf16[8,768]{1,0:T(8,128)(2,1)}, bf16[8,768]{1,0:T(8,128)(2,1)S(1)}, u32[]{:S(2)}, u32[]{:S(2)}) collective-permute-start(bf16[8,768]{1,0:T(8,128)(2,1)} %convert.256), channel_id=1, source_target_pairs={{0,6},{1,7},{2,8},{3,9},{4,10},{5,11},{6,12},{7,13},{8,14},{9,15},... | collective-permute-start | bytes 36872
  1201.1 77.9 %collective-permute-start.120 = (bf16[8,768]{1,0:T(8,128)(2,1)S(1)}, bf16[8,768]{1,0:T(8,128)(2,1)S(1)}, u32[]{:S(2)}, u32[]{:S(2)}) collective-permute-start(bf16[8,768]{1,0:T(8,128)(2,1)S(1)} %convert.255), channel_id=1, source_target_pairs={{0,25},{1,26},{2,27},{3,28},{4,29},{5,30},{6,31},{7,32},{8,33},{9,... | collective-permute-start | bytes 36872
  1202.4 81.3 %collective-permute-start.119 = (bf16[8,768]{1,0:T(8,128)(2,1)S(1)}, bf16[8,768]{1,0:T(8,128)(2,1)S(1)}, u32[]{:S(2)}, u32[]{:S(2)}) collective-permute-start(bf16[8,768]{1,0:T(8,128)(2,1)S(1)} %convert.255), channel_id=1, source_target_pairs={{0,24},{1,25},{2,26},{3,27},{4,28},{5,29},{6,30},{7,31},{8,32},{9,... | collective-permute-start | bytes 36872
  1203.7 83.2 %collective-permute-start.118 = (bf16[8,768]{1,0:T(8,128)(2,1)S(1)}, bf16[8,768]{1,0:T(8,128)(2,1)S(1)}, u32[]{:S(2)}, u32[]{:S(2)}) collective-permute-start(bf16[8,768]{1,0:T(8,128)(2,1)S(1)} %convert.255), channel_id=1, source_target_pairs={{0,23},{1,24},{2,25},{3,26},{4,27},{5,28},{6,29},{7,30},{8,31},{9,... | collective-permute-start | bytes 36872
  1205.0 86.6 %collective-permute-start.117 = (bf16[8,768]{1,0:T(8,128)(2,1)S(1)}, bf16[8,768]{1,0:T(8,128)(2,1)S(1)}, u32[]{:S(2)}, u32[]{:S(2)}) collective-permute-start(bf16[8,768]{1,0:T(8,128)(2,1)S(1)} %convert.255), channel_id=1, source_target_pairs={{0,22},{1,23},{2,24},{3,25},{4,26},{5,27},{6,28},{7,29},{8,30},{9,... | collective-permute-start | bytes 36872
  1208.5 87.2 %collective-permute-start.116 = (bf16[8,768]{1,0:T(8,128)(2,1)S(1)}, bf16[8,768]{1,0:T(8,128)(2,1)S(1)}, u32[]{:S(2)}, u32[]{:S(2)}) collective-permute-start(bf16[8,768]{1,0:T(8,128)(2,1)S(1)} %convert.255), channel_id=1, source_target_pairs={{0,21},{1,22},{2,23},{3,24},{4,25},{5,26},{6,27},{7,28},{8,29},{9,... | collective-permute-start | bytes 36872
  1279.0 50.8 %collective-permute-start.115 = (bf16[8,768]{1,0:T(8,128)(2,1)S(1)}, bf16[8,768]{1,0:T(8,128)(2,1)S(1)}, u32[]{:S(2)}, u32[]{:S(2)}) collective-permute-start(bf16[8,768]{1,0:T(8,128)(2,1)S(1)} %convert.255), channel_id=1, source_target_pairs={{0,20},{1,21},{2,22},{3,23},{4,24},{5,25},{6,26},{7,27},{8,28},{9,... | collective-permute-start | bytes 36872
  1283.7 49.0 %collective-permute-start.114 = (bf16[8,768]{1,0:T(8,128)(2,1)S(1)}, bf16[8,768]{1,0:T(8,128)(2,1)S(1)}, u32[]{:S(2)}, u32[]{:S(2)}) collective-permute-start(bf16[8,768]{1,0:T(8,128)(2,1)S(1)} %convert.255), channel_id=1, source_target_pairs={{0,19},{1,20},{2,21},{3,22},{4,23},{5,24},{6,25},{7,26},{8,27},{9,... | collective-permute-start | bytes 36872
  1286.9 49.7 %collective-permute-start.113 = (bf16[8,768]{1,0:T(8,128)(2,1)S(1)}, bf16[8,768]{1,0:T(8,128)(2,1)S(1)}, u32[]{:S(2)}, u32[]{:S(2)}) collective-permute-start(bf16[8,768]{1,0:T(8,128)(2,1)S(1)} %convert.255), channel_id=1, source_target_pairs={{0,18},{1,19},{2,20},{3,21},{4,22},{5,23},{6,24},{7,25},{8,26},{9,... | collective-permute-start | bytes 36872
  1291.6 49.4 %collective-permute-start.112 = (bf16[8,768]{1,0:T(8,128)(2,1)S(1)}, bf16[8,768]{1,0:T(8,128)(2,1)S(1)}, u32[]{:S(2)}, u32[]{:S(2)}) collective-permute-start(bf16[8,768]{1,0:T(8,128)(2,1)S(1)} %convert.255), channel_id=1, source_target_pairs={{0,17},{1,18},{2,19},{3,20},{4,21},{5,22},{6,23},{7,24},{8,25},{9,... | collective-permute-start | bytes 36872
  1295.7 48.8 %collective-permute-start.111 = (bf16[8,768]{1,0:T(8,128)(2,1)S(1)}, bf16[8,768]{1,0:T(8,128)(2,1)S(1)}, u32[]{:S(2)}, u32[]{:S(2)}) collective-permute-start(bf16[8,768]{1,0:T(8,128)(2,1)S(1)} %convert.255), channel_id=1, source_target_pairs={{0,16},{1,17},{2,18},{3,19},{4,20},{5,21},{6,22},{7,23},{8,24},{9,... | collective-permute-start | bytes 36872
  1329.8 46.6 %collective-permute-start.110 = (bf16[8,768]{1,0:T(8,128)(2,1)S(1)}, bf16[8,768]{1,0:T(8,128)(2,1)S(1)}, u32[]{:S(2)}, u32[]{:S(2)}) collective-permute-start(bf16[8,768]{1,0:T(8,128)(2,1)S(1)} %convert.255), channel_id=1, source_target_pairs={{0,15},{1,16},{2,17},{3,18},{4,19},{5,20},{6,21},{7,22},{8,23},{9,... | collective-permute-start | bytes 36872
  1332.6 45.1 %collective-permute-start.109 = (bf16[8,768]{1,0:T(8,128)(2,1)S(1)}, bf16[8,768]{1,0:T(8,128)(2,1)S(1)}, u32[]{:S(2)}, u32[]{:S(2)}) collective-permute-start(bf16[8,768]{1,0:T(8,128)(2,1)S(1)} %convert.255), channel_id=1, source_target_pairs={{0,14},{1,15},{2,16},{3,17},{4,18},{5,19},{6,20},{7,21},{8,22},{9,... | collective-permute-start | bytes 36872
  1336.6 44.0 %collective-permute-start.108 = (bf16[8,768]{1,0:T(8,128)(2,1)S(1)}, bf16[8,768]{1,0:T(8,128)(2,1)S(1)}, u32[]{:S(2)}, u32[]{:S(2)}) collective-permute-start(bf16[8,768]{1,0:T(8,128)(2,1)S(1)} %convert.255), channel_id=1, source_target_pairs={{0,13},{1,14},{2,15},{3,16},{4,17},{5,18},{6,19},{7,20},{8,21},{9,... | collective-permute-start | bytes 36872
  1341.1 41.2 %collective-permute-start.107 = (bf16[8,768]{1,0:T(8,128)(2,1)S(1)}, bf16[8,768]{1,0:T(8,128)(2,1)S(1)}, u32[]{:S(2)}, u32[]{:S(2)}) collective-permute-start(bf16[8,768]{1,0:T(8,128)(2,1)S(1)} %convert.255), channel_id=1, source_target_pairs={{0,12},{1,13},{2,14},{3,15},{4,16},{5,17},{6,18},{7,19},{8,20},{9,... | collective-permute-start | bytes 36872
  1344.5 39.7 %collective-permute-start.106 = (bf16[8,768]{1,0:T(8,128)(2,1)S(1)}, bf16[8,768]{1,0:T(8,128)(2,1)S(1)}, u32[]{:S(2)}, u32[]{:S(2)}) collective-permute-start(bf16[8,768]{1,0:T(8,128)(2,1)S(1)} %convert.255), channel_id=1, source_target_pairs={{0,11},{1,12},{2,13},{3,14},{4,15},{5,16},{6,17},{7,18},{8,19},{9,... | collective-permute-start | bytes 36872
  1376.4 21.0 %collective-permute-start.105 = (bf16[8,768]{1,0:T(8,128)(2,1)S(1)}, bf16[8,768]{1,0:T(8,128)(2,1)S(1)}, u32[]{:S(2)}, u32[]{:S(2)}) collective-permute-start(bf16[8,768]{1,0:T(8,128)(2,1)S(1)} %convert.255), channel_id=1, source_target_pairs={{0,10},{1,11},{2,12},{3,13},{4,14},{5,15},{6,16},{7,17},{8,18},{9,... | collective-permute-start | bytes 36872
  1377.7 23.5 %collective-permute-start.104 = (bf16[8,768]{1,0:T(8,128)(2,1)S(1)}, bf16[8,768]{1,0:T(8,128)(2,1)S(1)}, u32[]{:S(2)}, u32[]{:S(2)}) collective-permute-start(bf16[8,768]{1,0:T(8,128)(2,1)S(1)} %convert.255), channel_id=1, source_target_pairs={{0,9},{1,10},{2,11},{3,12},{4,13},{5,14},{6,15},{7,16},{8,17},{9,1... | collective-permute-start | bytes 36872
  1380.6 23.2 %collective-permute-start.103 = (bf16[8,768]{1,0:T(8,128)(2,1)S(1)}, bf16[8,768]{1,0:T(8,128)(2,1)S(1)}, u32[]{:S(2)}, u32[]{:S(2)}) collective-permute-start(bf16[8,768]{1,0:T(8,128)(2,1)S(1)} %convert.255), channel_id=1, source_target_pairs={{0,8},{1,9},{2,10},{3,11},{4,12},{5,13},{6,14},{7,15},{8,16},{9,17... | collective-permute-start | bytes 36872
  1382.2 25.6 %collective-permute-start.102 = (bf16[8,768]{1,0:T(8,128)(2,1)S(1)}, bf16[8,768]{1,0:T(8,128)(2,1)S(1)}, u32[]{:S(2)}, u32[]{:S(2)}) collective-permute-start(bf16[8,768]{1,0:T(8,128)(2,1)S(1)} %convert.255), channel_id=1, source_target_pairs={{0,7},{1,8},{2,9},{3,10},{4,11},{5,12},{6,13},{7,14},{8,15},{9,16}... | collective-permute-start | bytes 36872
  1384.2 25.3 %collective-permute-start.101 = (bf16[8,768]{1,0:T(8,128)(2,1)S(1)}, bf16[8,768]{1,0:T(8,128)(2,1)S(1)}, u32[]{:S(2)}, u32[]{:S(2)}) collective-permute-start(bf16[8,768]{1,0:T(8,128)(2,1)S(1)} %convert.255), channel_id=1, source_target_pairs={{0,6},{1,7},{2,8},{3,9},{4,10},{5,11},{6,12},{7,13},{8,14},{9,15},... | collective-permute-start | bytes 36872
  (227 other events, 9790.7 us)
Sparse Core Ops, SparseCore 0:
  10.8 67.8 all-gather.19
  81.5 61.6 all-gather.15
  146.1 61.5 all-gather.17
  210.4 61.5 all-gather.21
  274.1 21.7 all-gather.13
  298.1 24.5 all-gather.11
  494.5 26.1 reduce-scatter.14
  523.2 31.4 reduce-scatter.16
where the time goes:
time: 1440 us; the launch traced here: 1430 us
  blocking collectives  557 us (39%)
  starting transfers between devices  334 us (23%)
  waiting for transfers between devices  274 us (19%)
  local copies, waits for them, and re-layouts  151 us (10%)
  matrix products  79.2 us (6%)
  between operations  17.9 us (1%)
    unnamed x3, blocking collectives  504 us
    unnamed x130, starting transfers between devices  315 us
    unnamed x300, local copies, waits for them, and re-layouts  110 us
    all_gather x1, waiting for transfers between devices, on_device(): lax.all_gather(w_output, ('fsdp', 'seq'), axis=0, tiled=True)  61.4 us
    all_gather x1, waiting for transfers between devices, on_device(): lax.all_gather(w_value, ('fsdp', 'seq'), axis=0, tiled=True)  56.7 us
    all_gather x1, waiting for transfers between devices, on_device(): lax.all_gather(w_query, ('fsdp', 'seq'), axis=0, tiled=True)  49.1 us
    unnamed x138, waiting for transfers between devices  45.8 us
    all_gather x1, blocking collectives, on_device(): lax.all_gather(w_router, ('fsdp', 'seq'), axis=0, tiled=True)  37 us
  transfers between devices with their start and end apart: 139, of which 11 were waited for; matrix products, arithmetic and copies ran while one was open for 11% of the time, Pallas kernels for 0%

commit v1 on v0

v1 whole, which is shorter than its diff:
```python
import functools

import jax
import jax.numpy as jnp
from jax import lax
from jax.experimental import pallas as pl
from jax.experimental.pallas import tpu as pltpu
from jax.sharding import PartitionSpec as P

bf16 = jnp.bfloat16
f32 = jnp.float32

WIDTH = 768
TOK = 128
LEN = 1024
FF = 3072
GROUP = 3
HD = 64
COLS = GROUP * HD
BAND = 15 * TOK
PACK = 1152
HALF = WIDTH // 2
FF_TILE = 512
eps = 1e-06
bucket_edges = (12, 16, 23, 32, 46, 64, 91)
BOTH = ("fsdp", "seq")

params = pltpu.CompilerParams(vmem_limit_bytes=56 << 20)
smem = pl.BlockSpec(memory_space=pltpu.SMEM)
vmem = pl.BlockSpec(memory_space=pltpu.VMEM)


def iota(shape, dim):
    return lax.broadcasted_iota(jnp.int32, shape, dim)


def sixth(n):
    return (n * 10923) >> 16


def third(n):
    return (n * 21846) >> 16


def bucket_of(offsets):
    spread = jnp.abs(offsets)
    ids = (offsets > 0).astype(jnp.int32) * 16 + jnp.minimum(spread, 8)
    for border in bucket_edges:
        ids = ids + (spread >= border).astype(jnp.int32)
    return ids


def mm(a, b):
    return jnp.dot(a, b, preferred_element_type=f32)


def mm_nt(a, b):
    return lax.dot_general(a, b, (((1,), (1,)), ((), ())), preferred_element_type=f32)


def mm_tn(a, b):
    return lax.dot_general(a, b, (((0,), (0,)), ((), ())), preferred_element_type=f32)


def exact(a, b):
    return lax.dot_general(
        a,
        b,
        (((1,), (0,)), ((), ())),
        precision=lax.Precision.HIGHEST,
        preferred_element_type=f32,
    )


def call(kernel, outs, ins, scratch=(), **kw):
    return pl.pallas_call(
        kernel,
        out_shape=outs,
        in_specs=ins,
        out_specs=jax.tree.map(lambda _: vmem, outs),
        scratch_shapes=list(scratch),
        compiler_params=params,
        **kw,
    )


def load_rows(ref, start, stride):
    return jnp.concatenate(
        [ref[j, pl.ds(start, 128, stride=stride), :] for j in range(ref.shape[0])], axis=1
    )


def store_rows(ref, start, stride, value):
    for j in range(value.shape[1] // 128):
        ref[j, pl.ds(start, 128, stride=stride), :] = value[:, 128 * j : 128 * j + 128]


def whole(ref, first, last):
    return jnp.concatenate([ref[j] for j in range(first, last)], axis=1)


def fill(ref, value):
    for j in range(ref.shape[0]):
        ref[j] = value[:, 128 * j : 128 * j + 128].astype(f32)


def sds(*shape, dtype=bf16):
    return jax.ShapeDtypeStruct(shape, dtype)


def attend_kernel(
    idx_ref, x_ref, pack_ref, seg_ref,
    o0_ref, o1_ref, o2_ref, o3_ref, h_ref, wqkv_ref, wo_ref, router_ref, gain_ref,
    qe_ref, ke_ref, v_ref, band_ref, lse_ref,
    pf_ref, wf_ref, tail_ref, rf_ref, os_ref,
):
    y, c = idx_ref[0], idx_ref[1]
    fill(pf_ref, pack_ref)
    for r in range(6):
        store_rows(wf_ref, r, 6, load_rows(pf_ref, r, 8))
    row6 = load_rows(pf_ref, 6, 8)
    row7 = load_rows(pf_ref, 7, 8)
    blank = jnp.zeros((128, 64), f32)
    for r in range(6):
        tail = jnp.concatenate([row6[:, 192 * r : 192 * r + 192], blank], axis=1)
        store_rows(tail_ref, r, 6, tail)
        rf_ref[pl.ds(r, 128, stride=6), :] = row7[:, 128 * r : 128 * r + 128]
    wqkv_ref[...] = whole(wf_ref, 0, 5)[:, : 3 * COLS].astype(bf16)
    left = whole(wf_ref, 4, 9)[:, 64:]
    wo_ref[...] = jnp.concatenate([left, whole(tail_ref, 0, 2)[:, :COLS]], axis=1).astype(bf16)
    router_ref[...] = rf_ref[...].astype(bf16)
    small = row7[:, WIDTH : WIDTH + 128].astype(bf16)

    lanes = iota((128, WIDTH), 1)
    rows = iota((128, WIDTH), 0)
    own = sixth(lanes) == rows
    within = lanes - 6 * sixth(lanes)
    gains = []
    for base in (0, 6):
        spread = mm(small, (rows == within + base).astype(bf16))
        gains.append(jnp.sum(jnp.where(own, spread, 0.0), axis=0, keepdims=True))
    gain_ref[...] = jnp.concatenate([gains[0], gains[1], jnp.zeros((6, WIDTH), f32)], axis=0)
    lanes = iota((128, 384), 1)
    rows = iota((128, 384), 0)
    spread = mm(small, (rows == lanes - 3 * third(lanes) + 12).astype(bf16))
    table = jnp.sum(jnp.where(third(lanes) == rows, spread, 0.0), axis=0, keepdims=True)
    table = jnp.broadcast_to(table, (8, 384)).astype(bf16)
    ids = bucket_of(iota((384, 512), 1) - 255)
    entry = iota((384, 512), 0)
    for h in range(GROUP):
        hot = (entry == ids + 32 * (3 * y + h)).astype(bf16)
        line = mm(table, hot)[:1]
        wide = pltpu.roll(
            jnp.broadcast_to(line, (TOK, 512)), 385, 1, stride=1, stride_axis=0
        )
        band_ref[h, :, : 6 * TOK] = jnp.broadcast_to(line[:, :1], (TOK, 6 * TOK))
        band_ref[h, :, 6 * TOK : 9 * TOK] = wide[:, : 3 * TOK]
        band_ref[h, :, 9 * TOK :] = jnp.broadcast_to(line[:, 511:], (TOK, 6 * TOK))

    gain = gains[0]

    def project(i, _):
        at = pl.ds(pl.multiple_of(i * TOK, TOK), TOK)
        x = x_ref[at, :].astype(f32)
        hb = (x * lax.rsqrt(jnp.mean(x * x, axis=-1, keepdims=True) + eps) * gain).astype(bf16)
        h_ref[at, :] = hb
        qkv = mm(hb, wqkv_ref[...])
        doc = seg_ref[at, :]
        lane = iota((TOK, HD), 1)
        same = lane == doc
        q_mark = jnp.where(same, -1e30, 0.0)
        k_mark = jnp.where((lane < 3) & jnp.logical_not(same), 1.0, 0.0)
        q_parts, k_parts = [], []
        for h in range(GROUP):
            q = qkv[:, HD * h : HD * h + HD]
            k = qkv[:, COLS + HD * h : COLS + HD * h + HD]
            q_parts += [q.astype(bf16).astype(f32) * 0.125, q_mark]
            k_parts += [k, k_mark]
        qe_ref[at, :] = jnp.concatenate(q_parts, axis=1).astype(bf16)
        ke_ref[at, :] = jnp.concatenate(k_parts, axis=1).astype(bf16)
        v_ref[at, :] = qkv[:, 2 * COLS :].astype(bf16)
        return 0

    lax.fori_loop(0, 8, project, 0)

    def attend(k, _):
        yq = lax.rem(y + k, 4)
        pq = 2 * yq + c
        at = pl.ds(pl.multiple_of(pq * TOK, TOK), TOK)
        shift = pl.ds(pl.multiple_of((7 - pq) * TOK, TOK), LEN)
        lane = iota((TOK, 128), 1)
        lse_all = jnp.zeros((TOK, 128), f32)
        outs = []
        for h in range(GROUP):
            s = mm_nt(qe_ref[at, 128 * h : 128 * h + 128], ke_ref[:, 128 * h : 128 * h + 128])
            s = s + band_ref[h, :, shift]
            top = jnp.max(s, axis=-1, keepdims=True)
            e = jnp.exp(s - top)
            total = jnp.sum(e, axis=-1, keepdims=True)
            p = (e * (1.0 / total)).astype(bf16)
            outs.append(mm(p, v_ref[:, HD * h : HD * h + HD]))
            lse_all = jnp.where(lane == h, top + jnp.log(total), lse_all)
        os_ref[k] = jnp.concatenate(outs, axis=1).astype(bf16)
        lse_ref[yq] = lse_all
        return 0

    lax.fori_loop(0, 4, attend, 0)
    o0_ref[...] = os_ref[0]
    o1_ref[...] = os_ref[1]
    o2_ref[...] = os_ref[2]
    o3_ref[...] = os_ref[3]


def attend(idx, x_all, pack, seg_col):
    outs = (
        [sds(TOK, COLS)] * 4
        + [sds(LEN, WIDTH), sds(WIDTH, 3 * COLS), sds(WIDTH, WIDTH), sds(WIDTH, 128)]
        + [sds(8, WIDTH, dtype=f32), sds(LEN, 384), sds(LEN, 384), sds(LEN, COLS)]
        + [sds(GROUP, TOK, BAND, dtype=f32), sds(4, TOK, 128, dtype=f32)]
    )
    return call(
        attend_kernel,
        outs,
        [smem, vmem, vmem, vmem],
        [
            pltpu.VMEM((9, LEN, 128), f32),
            pltpu.VMEM((9, WIDTH, 128), f32),
            pltpu.VMEM((2, WIDTH, 128), f32),
            pltpu.VMEM((WIDTH, 128), f32),
            pltpu.VMEM((4, TOK, COLS), bf16),
        ],
        name="attend",
    )(idx, x_all, pack, seg_col)


def dispatch_kernel(
    idx_ref, x_ref, o0_ref, o1_ref, o2_ref, o3_ref, wo_ref, router_ref, gain_ref,
    route_ref, cot_ref,
    x1_ref, h2_ref, prob_ref, hot_ref, send_ref,
    sf_ref,
):
    y = idx_ref[0]
    x1 = x_ref[...].astype(f32)
    for k, o_ref in enumerate((o0_ref, o1_ref, o2_ref, o3_ref)):
        src = lax.rem(y + 4 - k, 4)
        x1 = x1 + mm(o_ref[...], wo_ref[pl.ds(pl.multiple_of(src * COLS, COLS), COLS), :])
    x1_ref[...] = x1
    r2 = lax.rsqrt(jnp.mean(x1 * x1, axis=-1, keepdims=True) + eps)
    h2 = (x1 * r2 * gain_ref[1:2, :]).astype(bf16)
    h2_ref[...] = h2
    logits = mm(h2, router_ref[...])
    e = jnp.exp(logits - jnp.max(logits, axis=-1, keepdims=True))
    prob = e / jnp.sum(e, axis=-1, keepdims=True)
    prob_ref[...] = prob
    expert = iota((TOK, 128), 1)
    picked = (route_ref[...] == expert).astype(f32)
    gate = jnp.sum(prob * picked, axis=-1, keepdims=True)
    earlier = (iota((TOK, TOK), 0) > iota((TOK, TOK), 1)).astype(bf16)
    slot = jnp.sum(mm(earlier, picked.astype(bf16)) * picked, axis=-1, keepdims=True)
    geo = (gate * cot_ref[...].astype(f32)).astype(bf16)
    for s in range(2):
        hot = jnp.where((slot > 0.5) == (s == 1), picked, 0.0).astype(bf16)
        hot_ref[s] = hot
        for kind, src in enumerate((h2, geo)):
            placed = mm_tn(hot, src)
            for half in range(2):
                part = placed[:, HALF * half : HALF * half + HALF]
                store_rows(sf_ref, kind * 4 + s * 2 + half, 8, part)
    send_ref[...] = whole(sf_ref, 0, 3).astype(bf16)


def dispatch(idx, x_own, o_parts, wo, router, gains, route_col, cot):
    outs = [
        sds(TOK, WIDTH, dtype=f32), sds(TOK, WIDTH), sds(TOK, 128, dtype=f32),
        sds(2, TOK, 128), sds(LEN, HALF),
    ]
    return call(
        dispatch_kernel,
        outs,
        [smem] + [vmem] * 10,
        [pltpu.VMEM((3, LEN, 128), f32)],
        name="dispatch",
    )(idx, x_own, *o_parts, wo, router, gains, route_col, cot)


def expert_kernel(
    recv_ref, wi_ref, wo_ref, ret_ref, gi_ref, go_ref, rf_ref, x_ref, xt_ref, g_ref, eo_ref, gx_ref
):
    step = pl.program_id(0)

    @pl.when(step == 0)
    def _():
        fill(rf_ref, recv_ref)
        for kind, dst in enumerate((x_ref, g_ref)):
            for s in range(2):
                for half in range(2):
                    dst[TOK * s : TOK * s + TOK, HALF * half : HALF * half + HALF] = load_rows(
                        rf_ref, kind * 4 + s * 2 + half, 8
                    ).astype(bf16)
        xt_ref[...] = x_ref[...].T
        eo_ref[...] = jnp.zeros_like(eo_ref)
        gx_ref[...] = jnp.zeros_like(gx_ref)

    wi = wi_ref[...]
    wo = wo_ref[...]
    g = g_ref[...]
    a = mm(x_ref[...], wi)
    cc = 0.7978845608028654
    sq = a * a
    t = jnp.tanh(cc * (a + 0.044715 * (sq * a)))
    u = (0.5 * a * (1.0 + t)).astype(bf16)
    slope = 0.5 * (1.0 + t) + (0.5 * cc) * a * (1.0 - t * t) * (1.0 + 0.134145 * sq)
    eo_ref[...] += mm(u, wo)
    ga = (mm_nt(g, wo) * slope).astype(bf16)
    go_ref[...] = mm_tn(u, g).astype(bf16)
    gi_ref[...] = mm(xt_ref[...], ga).astype(bf16)
    gx_ref[...] += mm_nt(ga, wi)

    @pl.when(step == FF // FF_TILE - 1)
    def _():
        for kind, src in enumerate((eo_ref, gx_ref)):
            for s in range(2):
                for half in range(2):
                    part = src[TOK * s : TOK * s + TOK, HALF * half : HALF * half + HALF]
                    store_rows(rf_ref, kind * 4 + s * 2 + half, 8, part)
        ret_ref[...] = whole(rf_ref, 0, 3).astype(bf16)


def experts(recv, w_inner, w_outer):
    return pl.pallas_call(
        expert_kernel,
        grid=(FF // FF_TILE,),
        out_shape=[sds(LEN, HALF), sds(1, WIDTH, FF), sds(1, FF, WIDTH)],
        in_specs=[
            pl.BlockSpec((LEN, HALF), lambda i: (0, 0)),
            pl.BlockSpec((None, WIDTH, FF_TILE), lambda i: (0, 0, i)),
            pl.BlockSpec((None, FF_TILE, WIDTH), lambda i: (0, i, 0)),
        ],
        out_specs=[
            pl.BlockSpec((LEN, HALF), lambda i: (0, 0)),
            pl.BlockSpec((None, WIDTH, FF_TILE), lambda i: (0, 0, i)),
            pl.BlockSpec((None, FF_TILE, WIDTH), lambda i: (0, i, 0)),
        ],
        scratch_shapes=[
            pltpu.VMEM((3, LEN, 128), f32),
            pltpu.VMEM((2 * TOK, WIDTH), bf16),
            pltpu.VMEM((WIDTH, 2 * TOK), bf16),
            pltpu.VMEM((2 * TOK, WIDTH), bf16),
            pltpu.VMEM((2 * TOK, WIDTH), f32),
            pltpu.VMEM((2 * TOK, WIDTH), f32),
        ],
        compiler_params=params,
        name="experts",
    )(recv, w_inner, w_outer)


def return_kernel(
    idx_ref, back_ref, x1_ref, h2_ref, prob_ref, hot_ref, cot_ref, router_ref, gain_ref, wo_ref,
    o0_ref, o1_ref, o2_ref, o3_ref,
    out_ref, dx1_ref, g0_ref, g1_ref, g2_ref, g3_ref, dwo_ref, drouter_ref, dgain_ref,
    bf_ref,
):
    y = idx_ref[0]
    fill(bf_ref, back_ref)
    parts = []
    for kind in range(2):
        halves = []
        for half in range(2):
            got = jnp.zeros((TOK, HALF), f32)
            for s in range(2):
                rows = load_rows(bf_ref, kind * 4 + s * 2 + half, 8).astype(bf16)
                got = got + mm(hot_ref[s], rows)
            halves.append(got)
        parts.append(jnp.concatenate(halves, axis=1))
    eo, gx = parts
    x1 = x1_ref[...]
    prob = prob_ref[...]
    picked = hot_ref[0].astype(f32) + hot_ref[1].astype(f32)
    gate = jnp.sum(prob * picked, axis=-1, keepdims=True)
    out_ref[...] = (x1 + gate * eo).astype(bf16)
    dy = cot_ref[...].astype(f32)
    dgate = jnp.sum(dy * eo, axis=-1, keepdims=True)
    gz = (dgate * gate * (picked - prob)).astype(bf16)
    dh2 = gx + mm_nt(gz, router_ref[...])
    drouter_ref[...] = mm_tn(h2_ref[...], gz)
    r2 = lax.rsqrt(jnp.mean(x1 * x1, axis=-1, keepdims=True) + eps)
    scaled = x1 * r2
    dgain = jnp.sum(dh2 * scaled, axis=0, keepdims=True)
    dgain_ref[...] = jnp.broadcast_to(dgain, (8, WIDTH))
    gd = gain_ref[1:2, :] * dh2
    dx1 = dy + r2 * (gd - scaled * jnp.mean(gd * scaled, axis=-1, keepdims=True))
    dx1_ref[...] = dx1
    gw = dx1.astype(bf16)
    for k, g_ref in enumerate((g0_ref, g1_ref, g2_ref, g3_ref)):
        dst = lax.rem(y + k, 4)
        rows = wo_ref[pl.ds(pl.multiple_of(dst * COLS, COLS), COLS), :]
        g_ref[...] = mm_nt(gw, rows).astype(bf16)
    for k, o_ref in enumerate((o0_ref, o1_ref, o2_ref, o3_ref)):
        src = lax.rem(y + 4 - k, 4)
        terms = mm_tn(o_ref[...], gw)
        for j in range(6):
            dwo_ref[j, pl.ds(pl.multiple_of(src * COLS, COLS), COLS), :] = terms[
                :, 128 * j : 128 * j + 128
            ]


def returned(idx, back, x1, h2, prob, hot, cot, router, gains, wo, o_parts):
    outs = (
        [sds(TOK, WIDTH), sds(TOK, WIDTH, dtype=f32)]
        + [sds(TOK, COLS)] * 4
        + [sds(6, WIDTH, 128, dtype=f32), sds(WIDTH, 128, dtype=f32), sds(8, WIDTH, dtype=f32)]
    )
    return call(
        return_kernel,
        outs,
        [smem] + [vmem] * 13,
        [pltpu.VMEM((3, LEN, 128), f32)],
        name="returned",
    )(idx, back, x1, h2, prob, hot, cot, router, gains, wo, *o_parts)


def two_parts(v):
    high = v.astype(bf16)
    return high, (v - high.astype(f32)).astype(bf16)


def backward_kernel(
    idx_ref, g0_ref, g1_ref, g2_ref, g3_ref, x_ref, h_ref, wqkv_ref, qe_ref, ke_ref, v_ref,
    band_ref, lse_ref, dwo_ref, drouter_ref, dgain_ref,
    send_ref, own_ref, other_ref,
    gs_ref, gk_ref, gv_ref, dq_ref, acc_ref, sf_ref, dw_ref, line_ref,
):
    y, c = idx_ref[0], idx_ref[1]
    for k, g_ref in enumerate((g0_ref, g1_ref, g2_ref, g3_ref)):
        gs_ref[k] = g_ref[...]
    gk_ref[...] = jnp.zeros_like(gk_ref)
    gv_ref[...] = jnp.zeros_like(gv_ref)
    dq_ref[...] = jnp.zeros_like(dq_ref)
    acc_ref[...] = jnp.zeros_like(acc_ref)

    def block(k, _):
        yq = lax.rem(y + 4 - k, 4)
        pq = 2 * yq + c
        at = pl.ds(pl.multiple_of(pq * TOK, TOK), TOK)
        shift = pl.ds(pl.multiple_of((7 - pq) * TOK, TOK), LEN)
        lse = lse_ref[yq]
        go = gs_ref[k]
        outs = []
        for h in range(GROUP):
            q = qe_ref[at, 128 * h : 128 * h + 128]
            keys = ke_ref[:, 128 * h : 128 * h + 128]
            g = go[:, HD * h : HD * h + HD]
            s = mm_nt(q, keys) + band_ref[h, :, shift]
            p = jnp.exp(s - lse[:, h : h + 1])
            pd = p * mm_nt(g, v_ref[:, HD * h : HD * h + HD])
            gs = pd - p * jnp.sum(pd, axis=-1, keepdims=True)
            acc_ref[h, :, shift] += gs
            low = gs.astype(bf16)
            outs.append(mm(low, keys)[:, :HD] * 0.125)
            gk_ref[HD * h : HD * h + HD, :] += mm_tn(q, low)[:HD]
            gv_ref[HD * h : HD * h + HD, :] += mm_tn(g, p.astype(bf16))
        dq_ref[at, :COLS] = jnp.concatenate(outs, axis=1).astype(bf16)
        return 0

    lax.fori_loop(0, 4, block, 0)
    dq_ref[:, COLS : 2 * COLS] = gk_ref[...].T.astype(bf16)
    dq_ref[:, 2 * COLS :] = gv_ref[...].T.astype(bf16)

    line_ref[...] = jnp.zeros_like(line_ref)

    def spread(i, _):
        own = (i & 1) == c
        at = pl.ds(pl.multiple_of(i * TOK, TOK), TOK)
        d = mm_nt(dq_ref[at, :], wqkv_ref[...])
        x = x_ref[at, :].astype(f32)
        r1 = lax.rsqrt(jnp.mean(x * x, axis=-1, keepdims=True) + eps)
        line_ref[...] += jnp.broadcast_to(jnp.sum(d * (x * r1), axis=0, keepdims=True), (8, WIDTH))

        @pl.when(own)
        def _():
            own_ref[i >> 1] = d

        @pl.when(jnp.logical_not(own))
        def _():
            other_ref[i >> 1] = d.astype(bf16)

        return 0

    lax.fori_loop(0, 8, spread, 0)

    def weights(j, _):
        at = pl.ds(pl.multiple_of(j * 128, 128), 128)
        terms = mm_tn(h_ref[:, at], dq_ref[...])
        terms = jnp.concatenate([terms, jnp.zeros((128, 64), f32)], axis=1)
        for m in range(5):
            dw_ref[m, at, :] = terms[:, 128 * m : 128 * m + 128]
        return 0

    lax.fori_loop(0, 6, weights, 0)

    tails = []
    for r in range(6):
        mine = load_rows(dwo_ref, r, 6)
        tails.append(mine[:, 3 * COLS :])
        mine = jnp.concatenate([load_rows(dw_ref, r, 6)[:, : 3 * COLS], mine[:, : 3 * COLS]], axis=1)
        store_rows(sf_ref, r, 8, mine)
        sf_ref[r, pl.ds(7, 128, stride=8), :] = drouter_ref[pl.ds(r, 128, stride=6), :]
    store_rows(sf_ref, 6, 8, jnp.concatenate(tails, axis=1))

    rows = iota((128, WIDTH), 0)
    lanes = iota((128, WIDTH), 1)
    own = sixth(lanes) == rows
    lane = iota((WIDTH, 128), 1)
    part = iota((WIDTH, 128), 0)
    part = part - 6 * sixth(part)
    extra = jnp.zeros((128, 128), f32)
    for base, line in ((0, line_ref[:1, :]), (12, dgain_ref[:1, :])):
        for off, v in zip((0, 6), two_parts(jnp.where(own, line, 0.0))):
            extra = extra + mm(v, (lane == part + base + off).astype(bf16))

    ids = bucket_of(iota((512, 128), 0) - 255)
    flat = iota((512, 128), 1)
    turn = (iota((TOK, TOK), 0) + iota((TOK, TOK), 1) == TOK - 1).astype(f32)
    table = jnp.zeros((8, 128), f32)
    flat_lane = iota((8, 128), 1)
    for h in range(GROUP):
        near = exact(turn, acc_ref[h, :, 6 * TOK : 9 * TOK])
        near = jnp.concatenate([near, jnp.zeros((TOK, TOK), f32)], axis=1)
        near = pltpu.roll(near, 0, 1, stride=1, stride_axis=0)
        diag = jnp.broadcast_to(jnp.sum(near, axis=0, keepdims=True), (8, 512))
        table = table + exact(diag, (flat == ids + 32 * h).astype(f32))
        low = jnp.sum(acc_ref[h, :, : 6 * TOK])
        high = jnp.sum(acc_ref[h, :, 9 * TOK :])
        table = table + jnp.where(flat_lane == 32 * h + 15, low, 0.0)
        table = table + jnp.where(flat_lane == 32 * h + 31, high, 0.0)
    lanes = iota((32, 128), 1)
    mine = third(lanes) == iota((32, 128), 0)
    lane = iota((128, 128), 1)
    part = iota((128, 128), 0)
    part = part - 3 * third(part)
    entries = jnp.zeros((32, 128), f32)
    for off, v in zip((24, 27), two_parts(jnp.where(mine, table[:1], 0.0))):
        entries = entries + mm(v, (lane == part + off).astype(bf16))
    zero = jnp.zeros((32, 128), f32)
    entries = jnp.concatenate([jnp.where(y == q, entries, zero) for q in range(4)], axis=0)
    last = pl.ds(7, 128, stride=8)
    sf_ref[6, last, :] = extra + entries
    sf_ref[7, last, :] = jnp.zeros((128, 128), f32)
    sf_ref[8, last, :] = jnp.zeros((128, 128), f32)
    send_ref[...] = whole(sf_ref, 0, 9).astype(bf16)


def attend_back(idx, go_parts, x_all, h, wqkv, qe, ke, v, band, lse, dwo, drouter, dgain):
    outs = [sds(LEN, PACK), sds(4, TOK, WIDTH, dtype=f32), sds(4, TOK, WIDTH)]
    return call(
        backward_kernel,
        outs,
        [smem] + [vmem] * 15,
        [
            pltpu.VMEM((4, TOK, COLS), bf16),
            pltpu.VMEM((COLS, LEN), f32),
            pltpu.VMEM((COLS, LEN), f32),
            pltpu.VMEM((LEN, 3 * COLS), bf16),
            pltpu.VMEM((GROUP, TOK, BAND), f32),
            pltpu.VMEM((9, LEN, 128), f32),
            pltpu.VMEM((5, WIDTH, 128), f32),
            pltpu.VMEM((8, WIDTH), f32),
        ],
        name="attend_back",
    )(idx, *go_parts, x_all, h, wqkv, qe, ke, v, band, lse, dwo, drouter, dgain)


def pair_kernel(idx_ref, own_ref, got_ref, d0_ref, d1_ref, d2_ref, d3_ref):
    y = idx_ref[0]
    for k, d_ref in enumerate((d0_ref, d1_ref, d2_ref, d3_ref)):
        dst = lax.rem(y + k, 4)
        d_ref[...] = (own_ref[dst] + got_ref[dst].astype(f32)).astype(d_ref.dtype)


def pair_sum(idx, own, got):
    outs = [sds(TOK, WIDTH, dtype=f32)] + [sds(TOK, WIDTH)] * 3
    return call(pair_kernel, outs, [smem, vmem, vmem], name="pair_sum")(idx, own, got)


def tokens_kernel(d0_ref, d1_ref, d2_ref, d3_ref, x_ref, gain_ref, dx1_ref, out_ref):
    dh = d0_ref[...] + d1_ref[...].astype(f32) + d2_ref[...].astype(f32) + d3_ref[...].astype(f32)
    x = x_ref[...].astype(f32)
    r1 = lax.rsqrt(jnp.mean(x * x, axis=-1, keepdims=True) + eps)
    gd = gain_ref[:1, :] * dh
    scaled = x * r1
    out_ref[...] = dx1_ref[...] + r1 * (gd - scaled * jnp.mean(gd * scaled, axis=-1, keepdims=True))


def tokens_last(d_parts, x_own, gains, dx1):
    return call(tokens_kernel, [sds(TOK, WIDTH, dtype=f32)], [vmem] * 7, name="tokens_last")(
        *d_parts, x_own, gains, dx1
    )[0]


def sums_kernel(recv_ref, q_ref, k_ref, v_ref, o_ref, router_ref, small_ref, acc_ref):
    acc_ref[...] = recv_ref[:64, :].astype(f32)

    def add(f, _):
        acc_ref[...] += recv_ref[pl.ds(pl.multiple_of(f * 64, 64), 64), :].astype(f32)
        return 0

    lax.fori_loop(1, 16, add, 0)
    quads = [acc_ref[16 * q : 16 * q + 8, :] + acc_ref[16 * q + 8 : 16 * q + 16, :] for q in range(4)]
    for m, ref in enumerate((q_ref, k_ref, v_ref)):
        whole = jnp.concatenate([a[:, COLS * m : COLS * m + COLS] for a in quads], axis=1)
        ref[...] = whole[:6].astype(bf16)
    every = quads[0] + quads[1] + quads[2] + quads[3]
    tail = [every[6:7, 192 * r : 192 * r + 192] for r in range(6)]
    o_ref[:, : 3 * COLS] = every[:6, 3 * COLS :].astype(bf16)
    o_ref[:, 3 * COLS :] = jnp.concatenate(tail, axis=0).astype(bf16)
    router = [every[7:8, 128 * r : 128 * r + 128] for r in range(6)]
    router_ref[...] = jnp.concatenate(router, axis=0).astype(bf16)
    small_ref[...] = every[:, WIDTH : WIDTH + 128]


def sums_last(recv):
    outs = [sds(6, WIDTH)] * 4 + [sds(6, 128), sds(8, 128, dtype=f32)]
    return call(sums_kernel, outs, [vmem], [pltpu.VMEM((64, PACK), f32)], name="sums_last")(recv)


def along_y(v, k):
    return lax.ppermute(v, "seq", [(s, (s + 2 * k) % 8) for s in range(8)])


def every_device(v):
    return lax.all_to_all(v, BOTH, split_axis=0, concat_axis=0, tiled=True)


def on_device(
    tokens, segments, routes, gain_attn, w_query, w_key, w_value, w_output, rel_table, gain_moe,
    w_router, w_inner, w_outer, cotangent,
):
    seq = lax.axis_index("seq")
    idx = jnp.stack([seq // 2, seq % 2]).astype(jnp.int32)
    x_all = lax.all_gather(tokens, "seq", axis=0, tiled=True)

    qkv = jnp.stack([w_query, w_key, w_value]).reshape(3, 6, 4, COLS)
    qkv = qkv.transpose(2, 1, 0, 3).reshape(4, 6, 3 * COLS)
    left = jnp.broadcast_to(w_output[None, :, : 3 * COLS], (4, 6, 3 * COLS))
    six = jnp.concatenate([qkv, left], axis=2)
    row6 = w_output[:, 3 * COLS :].reshape(1, 1, PACK)
    row7 = jnp.concatenate(
        [
            w_router.reshape(-1), gain_attn, gain_moe, rel_table,
            jnp.zeros((PACK - WIDTH - 15,), bf16),
        ]
    ).reshape(1, 1, PACK)
    two = jnp.broadcast_to(jnp.concatenate([row6, row7], axis=1), (4, 2, PACK))
    eight = jnp.concatenate([six, two], axis=1)
    pack = jnp.broadcast_to(eight[None, :, None], (16, 4, 2, 8, PACK)).reshape(LEN, PACK)
    pack = every_device(pack)

    attended = attend(idx, x_all, pack, segments.reshape(LEN, 1))
    o_parts = attended[:4]
    h, wqkv, wo, router, gains, qe, ke, v, band, lse = attended[4:]
    o_parts = [o_parts[0]] + [along_y(o_parts[k], k) for k in (1, 2, 3)]
    x1, h2, prob, hot, send = dispatch(
        idx, tokens, o_parts, wo, router, gains, routes, cotangent
    )
    ret, grad_inner, grad_outer = experts(every_device(send), w_inner, w_outer)
    back = every_device(ret)
    layer_out, dx1, *rest = returned(
        idx, back, x1, h2, prob, hot, cotangent, router, gains, wo, o_parts
    )
    go_parts = [rest[0]] + [along_y(rest[k], k) for k in (1, 2, 3)]
    dwo, drouter, dgain = rest[4:]
    terms, own, other = attend_back(
        idx, go_parts, x_all, h, wqkv, qe, ke, v, band, lse, dwo, drouter, dgain
    )
    got = lax.ppermute(other, "seq", [(s, s ^ 1) for s in range(8)])
    d_parts = pair_sum(idx, own, got)
    d_parts = [d_parts[0]] + [along_y(d_parts[k], k) for k in (1, 2, 3)]
    dq, dk, dv, do, dr, small = sums_last(every_device(terms))
    tokens_grad = tokens_last(d_parts, tokens, gains, dx1)
    line = small[7]
    return (
        layer_out,
        tokens_grad,
        (line[0:6] + line[6:12]).astype(bf16),
        dq,
        dk,
        dv,
        do,
        (line[24:27] + line[27:30]).astype(bf16),
        (line[12:18] + line[18:24]).astype(bf16),
        dr,
        grad_inner,
        grad_outer,
    )


def solution(mesh):
    rows = P(BOTH, None)
    flat = P(BOTH)
    cube = P(BOTH, None, None)
    return jax.shard_map(
        on_device,
        mesh=mesh,
        in_specs=(
            rows, P("fsdp", None), rows, flat, rows, rows, rows, rows, flat, flat, rows, cube, cube,
            rows,
        ),
        out_specs=(rows, rows, flat, rows, rows, rows, rows, flat, flat, rows, cube, cube),
        check_vma=False,
    )
```

time: 1440 us -> 249 us (0.17)
  blocking collectives: 557 us -> 46.5 us
  starting transfers between devices: 334 us -> 29.5 us
  waiting for transfers between devices: 274 us -> 66.2 us
  local copies, waits for them, and re-layouts: 151 us -> 16 us
  matrix products: 79.2 us -> 0 us
  Pallas kernels: 0 us -> 72.1 us
    unnamed x3 -> x0, blocking collectives: 504 us -> none
    unnamed x130 -> x0, starting transfers between devices: 315 us -> none
    all_gather x6 -> x1, waiting for transfers between devices: 204 us -> 0.01 us  [on_device(): x_all = lax.all_gather(tokens, 'seq', axis=0, tiled=True)]
    unnamed x300 -> x31, local copies, waits for them, and re-layouts: 110 us -> 6.42 us
    dot_general x30 -> x0, matrix products: 79.2 us -> none  [the longest x7 21.6 us: inner_rows(): lax.dot_general(left, right, (((0,), (0,)), ((), ())), preferred_element_...]
    pallas_call x0 -> x8, Pallas kernels: none -> 72.1 us  [the longest x1 23.4 us: attend_back(): call(backward_kernel, outs, [smem] + [vmem] * 15, [pltpu.VMEM((4, TOK, CO...]
    unnamed x138 -> x1, waiting for transfers between devices: 45.8 us -> 0.68 us
    all_gather x1 -> x0, blocking collectives: 37 us -> none  [on_device(): lax.all_gather(w_router, ('fsdp', 'seq'), axis=0, tiled=True)]
  transfers between devices with their start and end apart: 139 -> 13, of which waited for: 11 -> 10; matrix products, arithmetic and copies ran while one was open for 11% -> 4% of each run, Pallas kernels for 0% -> 2%
where the time goes in v1:
time: 249 us; the launch traced here: 248 us
  Pallas kernels  72.1 us (29%)
  waiting for transfers between devices  66.2 us (27%)
  blocking collectives  46.5 us (19%)
  starting transfers between devices  29.5 us (12%)
  local copies, waits for them, and re-layouts  16 us (6%)
  between operations  14.2 us (6%)
  other arithmetic  3.53 us (1%)
    all_to_all x2, blocking collectives, every_device(): return lax.all_to_all(v, BOTH, split_axis=0, concat_axis=0, tiled=True)  46.5 us
    ppermute x9, waiting for transfers between devices, along_y(): return lax.ppermute(v, 'seq', [(s, (s + 2 * k) % 8) for s in range(8)])  31.8 us
    all_to_all x2, waiting for transfers between devices, every_device(): return lax.all_to_all(v, BOTH, split_axis=0, concat_axis=0, tiled=True)  31.8 us
    pallas_call x1, Pallas kernels, attend_back(): call(backward_kernel, outs, [smem] + [vmem] * 15, [pltpu.VMEM((4, TOK, CO...  23.4 us
    all_to_all x2, starting transfers between devices, every_device(): return lax.all_to_all(v, BOTH, split_axis=0, concat_axis=0, tiled=True)  18.3 us
    pallas_call x1, Pallas kernels, attend(): call(attend_kernel, outs, [smem, vmem, vmem, vmem], [pltpu.VMEM((9, LEN,...  17.3 us
    pallas_call x1, Pallas kernels, experts(): pl.pallas_call(expert_kernel, grid=(FF // FF_TILE,), out_shape=[sds(LEN,...  14.4 us
    ppermute x9, starting transfers between devices, along_y(): return lax.ppermute(v, 'seq', [(s, (s + 2 * k) % 8) for s in range(8)])  10 us
  transfers between devices with their start and end apart: 13, of which 10 were waited for; matrix products, arithmetic and copies ran while one was open for 4% of the time, Pallas kernels for 2%

profile of v1, /device:TPU:1, one launch (start us, length us, event | category | flops | bytes accessed | tf_op | source)
XLA Modules:
  0.0 248.1 jit_solution(334252073919849085)
XLA Ops:
  7.2 0.7 all-gather.2.cloned.1.call-update
  7.9 0.8 slice.38
  8.7 0.7 slice.37
  9.4 2.8 %concatenate.14 = bf16[1152]{0:T(1024)(128)(2,1)S(1)} concatenate(bf16[768]{0:T(1024)(128)(2,1)} %bitcast.33, bf16[6]{0:T(256)(128)(2,1)} %param.17, bf16[6]{0:T(256)(128)(2,1)} %param.23, bf16[3]{0:T(256)(128)(2,1)} %param.22, bf16[369]{0:T(512)(128)(2,1)S(1)} %broadcast_in_dim.11), dimensions={0} | concatenate | bytes 4608 | tf_op jit(solution)/shard_map/concatenate | solution.py:647
  12.2 0.8 stack.28
  13.0 0.8 stack.29
  13.8 0.8 stack.30
  15.0 1.7 broadcast_in_dim.26
  16.7 11.5 %all-to-all-start = ((bf16[128,8,1152]{2,1,0:T(8,128)(2,1)}), bf16[128,8,1152]{2,1,0:T(8,128)(2,1)S(1)}, u32[]{:S(2)}, u32[]{:S(2)}) async-start(bf16[128,8,1152]{2,1,0:T(8,128)(2,1)} %bitcast.26), calls=%async_computation | async-start | bytes 4718592 | tf_op jit(solution)/shard_map/all_to_all | solution.py:631
  28.3 1.0 copy.31.seg_ref
  29.3 0.6 pad_add_fusion.idx_ref
  29.9 31.8 %all-to-all-done = bf16[128,8,1152]{2,1,0:T(8,128)(2,1)S(1)} async-done(((bf16[128,8,1152]{2,1,0:T(8,128)(2,1)}), bf16[128,8,1152]{2,1,0:T(8,128)(2,1)S(1)}, u32[]{:S(2)}, u32[]{:S(2)}) %all-to-all-start) | async-done | bytes 2359328 | tf_op jit(solution)/shard_map/all_to_all | solution.py:631
  61.6 1.4 copy-done
  63.0 17.3 %attend.1 = (bf16[128,192]{1,0:T(8,128)(2,1)}, bf16[128,192]{1,0:T(8,128)(2,1)}, bf16[128,192]{1,0:T(8,128)(2,1)}, bf16[128,192]{1,0:T(8,128)(2,1)}, bf16[1024,7...) custom-call(s32[2]{0:T(128)} %pad_add_fusion.idx_ref, ...), custom_call_target="tpu_custom_call" | custom-call | tf_op jit(solution)/shard_map/attend/pallas_call | solution.py:221
  81.2 2.0 collective-permute-start.2
  83.2 0.7 copy.32.route_ref
  84.0 0.9 collective-permute-done.o1_ref
  84.9 0.9 collective-permute-done.1.o2_ref
  85.8 0.6 collective-permute-done.2.o3_ref
  86.4 0.6 copy-done.5
  87.1 3.9 %dispatch.1 = (f32[128,768]{1,0:T(8,128)}, bf16[128,768]{1,0:T(8,128)(2,1)}, f32[128,128]{1,0:T(8,128)}, bf16[2,128,128]{2,1,0:T(8,128)(2,1)}, bf16[1024,384]{1,0:T(8,128)(2,1)}) custom-call(s32[2]{0:T(128)} %pad_add_fusion.idx_ref, bf16[128,768]{1,0:T(8,128)(2,1)} %x_ref.3, bf16[128,192]{1,0:T(8,128)(2,1)} %get-tuple-element.56.o0_ref, ...), custom_call_target="tpu_custom_call" | custom-call | tf_op jit(solution)/shard_map/dispatch/pallas_call | solution.py:277
  91.0 24.7 %all_to_all.44 = bf16[128,8,384]{2,1,0:T(8,128)(2,1)} all-to-all(bf16[128,8,384]{2,1,0:T(8,128)(2,1)} %bitcast.30), channel_id=1, replica_groups=mesh['fsdp'=16,'seq'=8] {'fsdp','seq'}, dimensions={0} | all-to-all | bytes 1572864 | tf_op jit(solution)/shard_map/all_to_all | solution.py:631
  115.7 14.4 %experts.1 = (bf16[1024,384]{1,0:T(8,128)(2,1)}, bf16[1,768,3072]{2,1,0:T(8,128)(2,1)}, bf16[1,3072,768]{2,1,0:T(8,128)(2,1)}) custom-call(bf16[1024,384]{1,0:T(8,128)(2,1)} %bitcast.27, bf16[1,768,3072]{2,1,0:T(8,128)(2,1)} %wi_ref.1, bf16[1,3072,768]{2,1,0:T(8,128)(2,1)} %wo_ref.1), custom_call_target="tpu_custom_call" | custom-call | tf_op jit(solution)/shard_map/experts/pallas_call | solution.py:330
  130.1 21.8 %all_to_all.45 = bf16[128,8,384]{2,1,0:T(8,128)(2,1)} all-to-all(bf16[128,8,384]{2,1,0:T(8,128)(2,1)} %bitcast.31), channel_id=1, replica_groups=mesh['fsdp'=16,'seq'=8] {'fsdp','seq'}, dimensions={0} | all-to-all | bytes 1572864 | tf_op jit(solution)/shard_map/all_to_all | solution.py:631
  152.0 5.1 %returned.1 = (bf16[128,768]{1,0:T(8,128)(2,1)}, f32[128,768]{1,0:T(8,128)}, bf16[128,192]{1,0:T(8,128)(2,1)}, bf16[128,192]{1,0:T(8,128)(2,1)}, bf16[128,192]{1...) custom-call(s32[2]{0:T(128)} %pad_add_fusion.idx_ref, ...), custom_call_target="tpu_custom_call" | custom-call | tf_op jit(solution)/shard_map/returned/pallas_call | solution.py:413
  157.1 2.1 collective-permute-start.4
  159.2 0.7 collective-permute-start.5
  159.9 2.0 collective-permute-done.3.g1_ref
  161.9 0.7 collective-permute-done.4.g2_ref
  162.6 0.6 collective-permute-done.5.g3_ref
  163.2 0.6 copy-done.11
  163.8 23.4 %attend_back.1 = (bf16[1024,1152]{1,0:T(8,128)(2,1)}, f32[4,128,768]{2,1,0:T(8,128)}, bf16[4,128,768]{2,1,0:T(8,128)(2,1)}) custom-call(s32[2]{0:T(128)} %pad_add_fusion.idx_ref, bf16[128,192]{1,0:T(8,128)(2,1)} %get-tuple-element.70.g0_ref, bf16[128,192]{1,0:T(8,128)(2,1)} %copy-done.9, bf16[128,192]{1,0:T(8,128)(2,1)} %copy-done.10, ...), custom_call_target="tpu_custom_call" | custom-call | tf_op jit(solution)/shard_map/attend_back/pallas_call | solution.py:555
  187.2 6.8 %all-to-all-start.3 = ((bf16[128,8,1152]{2,1,0:T(8,128)(2,1)}), bf16[128,8,1152]{2,1,0:T(8,128)(2,1)S(1)}, u32[]{:S(2)}, u32[]{:S(2)}) async-start(bf16[128,8,1152]{2,1,0:T(8,128)(2,1)} %bitcast.29), calls=%async_computation.3 | async-start | bytes 4718592 | tf_op jit(solution)/shard_map/all_to_all | solution.py:631
  194.0 1.1 collective-permute-start.6
  195.2 1.9 collective-permute-done.6.got_ref
  197.1 0.9 copy-done.2
  198.0 2.7 %pair_sum.1 = (f32[128,768]{1,0:T(8,128)}, bf16[128,768]{1,0:T(8,128)(2,1)}, bf16[128,768]{1,0:T(8,128)(2,1)}, bf16[128,768]{1,0:T(8,128)(2,1)}) custom-call(s32[2]{0:T(128)} %pad_add_fusion.idx_ref, f32[4,128,768]{2,1,0:T(8,128)} %get-tuple-element.84.own_ref, bf16[4,128,768]{2,1,0:T(8,128)(2,1)} %copy-done.2), custom_call_target="tpu_custom_call" | custom-call | tf_op jit(solution)/shard_map/pair_sum/pallas_call | solution.py:582
  200.6 0.7 collective-permute-start.7
  201.3 2.4 collective-permute-start.8
  203.8 1.1 collective-permute-start.9
  204.9 21.3 %collective-permute-done.7.d1_ref = bf16[128,768]{1,0:T(8,128)(2,1)S(1)} collective-permute-done((bf16[128,768]{1,0:T(8,128)(2,1)}, bf16[128,768]{1,0:T(8,128)(2,1)S(1)}, u32[]{:S(2)}, u32[]{:S(2)}) %collective-permute-start.7) | collective-permute-done | bytes 196640 | tf_op jit(solution)/shard_map/ppermute | solution.py:627
  226.2 4.8 %collective-permute-done.8.d2_ref = bf16[128,768]{1,0:T(8,128)(2,1)S(1)} collective-permute-done((bf16[128,768]{1,0:T(8,128)(2,1)}, bf16[128,768]{1,0:T(8,128)(2,1)S(1)}, u32[]{:S(2)}, u32[]{:S(2)}) %collective-permute-start.8) | collective-permute-done | bytes 196640 | tf_op jit(solution)/shard_map/ppermute | solution.py:627
  231.1 0.7 copy-done.7
  231.8 2.5 tokens_last.1
  234.3 1.4 copy-done.1
  235.7 2.9 %sums_last.1 = (bf16[6,768]{1,0:T(8,128)(2,1)}, bf16[6,768]{1,0:T(8,128)(2,1)}, bf16[6,768]{1,0:T(8,128)(2,1)}, bf16[6,768]{1,0:T(8,128)(2,1)}, bf16[6,128]{1,0:T(8,128)(2,1)}, /*index=5*/f32[8,128]{1,0:T(8,128)}) custom-call(bf16[1024,1152]{1,0:T(8,128)(2,1)} %bitcast.25), custom_call_target="tpu_custom_call" | custom-call | tf_op jit(solution)/shard_map/sums_last/pallas_call | solution.py:623
  238.5 1.3 convert_bitcast_fusion.1
  239.9 1.4 convert_bitcast_fusion
  (41 shorter events, 1.5 us)
Async XLA Ops:
  7.2 54.5 %all-gather.2.cloned.1.call-start = ((), (), s32[]{:S(2)}) async-start(), calls=%async_computation.4 | async-start | bytes 1769472 | tf_op jit(solution)/shard_map/all_gather | solution.py:640
  16.7 11.5 %copy-start.12 = (s32[1,1024]{1,0:T(1,128)S(1)}, s32[1,1024]{1,0:T(1,128)}, u32[]{:S(2)}) copy-start(s32[1,1024]{1,0:T(1,128)} %param.15) | copy-start | bytes 12292
  16.7 44.9 %all-to-all-start = ((bf16[128,8,1152]{2,1,0:T(8,128)(2,1)}), bf16[128,8,1152]{2,1,0:T(8,128)(2,1)S(1)}, u32[]{:S(2)}, u32[]{:S(2)}) async-start(bf16[128,8,1152]{2,1,0:T(8,128)(2,1)} %bitcast.26), calls=%async_computation | async-start | bytes 4718592 | tf_op jit(solution)/shard_map/all_to_all | solution.py:631
  29.3 53.9 %copy-start.13 = (s32[128,1]{0,1:T(1,128)S(1)}, s32[128,1]{0,1:T(1,128)}, u32[]{:S(2)}) copy-start(s32[128,1]{0,1:T(1,128)} %param.16) | copy-start | bytes 1540
  61.6 1.4 copy-start
  80.3 4.5 %collective-permute-start = (bf16[128,192]{1,0:T(8,128)(2,1)}, bf16[128,192]{1,0:T(8,128)(2,1)S(1)}, u32[]{:S(2)}, u32[]{:S(2)}) collective-permute-start(bf16[128,192]{1,0:T(8,128)(2,1)} %get-tuple-element.57), channel_id=1, source_target_pairs={{0,2},{1,3},{2,4},{3,5},{4,6},{5,7},{6,0},{7,1},{8,10},{9,11},{10,... | collective-permute-start | bytes 147464 | tf_op jit(solution)/shard_map/ppermute | solution.py:627
  80.7 5.0 %collective-permute-start.1 = (bf16[128,192]{1,0:T(8,128)(2,1)}, bf16[128,192]{1,0:T(8,128)(2,1)S(1)}, u32[]{:S(2)}, u32[]{:S(2)}) collective-permute-start(bf16[128,192]{1,0:T(8,128)(2,1)} %get-tuple-element.58), channel_id=1, source_target_pairs={{0,4},{1,5},{2,6},{3,7},{4,0},{5,1},{6,2},{7,3},{8,12},{9,13},{10,... | collective-permute-start | bytes 147464 | tf_op jit(solution)/shard_map/ppermute | solution.py:627
  81.2 5.2 %collective-permute-start.2 = (bf16[128,192]{1,0:T(8,128)(2,1)}, bf16[128,192]{1,0:T(8,128)(2,1)S(1)}, u32[]{:S(2)}, u32[]{:S(2)}) collective-permute-start(bf16[128,192]{1,0:T(8,128)(2,1)} %get-tuple-element.59), channel_id=1, source_target_pairs={{0,6},{1,7},{2,0},{3,1},{4,2},{5,3},{6,4},{7,5},{8,14},{9,15},{10,... | collective-permute-start | bytes 147464 | tf_op jit(solution)/shard_map/ppermute | solution.py:627
  84.9 1.6 copy-start.3
  85.8 0.7 copy-start.4
  86.4 0.6 copy-start.5
  157.1 4.8 %collective-permute-start.3 = (bf16[128,192]{1,0:T(8,128)(2,1)}, bf16[128,192]{1,0:T(8,128)(2,1)S(1)}, u32[]{:S(2)}, u32[]{:S(2)}) collective-permute-start(bf16[128,192]{1,0:T(8,128)(2,1)} %get-tuple-element.71), channel_id=1, source_target_pairs={{0,2},{1,3},{2,4},{3,5},{4,6},{5,7},{6,0},{7,1},{8,10},{9,11},{10,... | collective-permute-start | bytes 147464 | tf_op jit(solution)/shard_map/ppermute | solution.py:627
  157.1 5.5 %collective-permute-start.4 = (bf16[128,192]{1,0:T(8,128)(2,1)}, bf16[128,192]{1,0:T(8,128)(2,1)S(1)}, u32[]{:S(2)}, u32[]{:S(2)}) collective-permute-start(bf16[128,192]{1,0:T(8,128)(2,1)} %get-tuple-element.72), channel_id=1, source_target_pairs={{0,4},{1,5},{2,6},{3,7},{4,0},{5,1},{6,2},{7,3},{8,12},{9,13},{10,... | collective-permute-start | bytes 147464 | tf_op jit(solution)/shard_map/ppermute | solution.py:627
  159.2 4.0 %collective-permute-start.5 = (bf16[128,192]{1,0:T(8,128)(2,1)}, bf16[128,192]{1,0:T(8,128)(2,1)S(1)}, u32[]{:S(2)}, u32[]{:S(2)}) collective-permute-start(bf16[128,192]{1,0:T(8,128)(2,1)} %get-tuple-element.73), channel_id=1, source_target_pairs={{0,6},{1,7},{2,0},{3,1},{4,2},{5,3},{6,4},{7,5},{8,14},{9,15},{10,... | collective-permute-start | bytes 147464 | tf_op jit(solution)/shard_map/ppermute | solution.py:627
  161.9 1.3 copy-start.9
  162.6 0.6 copy-start.10
  163.2 0.6 copy-start.11
  187.2 6.8 %copy-start.14 = (bf16[4,128,768]{2,1,0:T(8,128)(2,1)S(1)}, bf16[4,128,768]{2,1,0:T(8,128)(2,1)}, u32[]{:S(2)}) copy-start(bf16[4,128,768]{2,1,0:T(8,128)(2,1)} %get-tuple-element.85) | copy-start | bytes 2359300
  187.2 47.0 %all-to-all-start.3 = ((bf16[128,8,1152]{2,1,0:T(8,128)(2,1)}), bf16[128,8,1152]{2,1,0:T(8,128)(2,1)S(1)}, u32[]{:S(2)}, u32[]{:S(2)}) async-start(bf16[128,8,1152]{2,1,0:T(8,128)(2,1)} %bitcast.29), calls=%async_computation.3 | async-start | bytes 4718592 | tf_op jit(solution)/shard_map/all_to_all | solution.py:631
  194.0 3.1 %collective-permute-start.6 = (bf16[4,128,768]{2,1,0:T(8,128)(2,1)S(1)}, bf16[4,128,768]{2,1,0:T(8,128)(2,1)S(1)}, u32[]{:S(2)}, u32[]{:S(2)}) collective-permute-start(bf16[4,128,768]{2,1,0:T(8,128)(2,1)S(1)} %copy-done.14), channel_id=1, source_target_pairs={{0,1},{1,0},{2,3},{3,2},{4,5},{5,4},{6,7},{7,6},{8,9},{9,8},{10,11... | collective-permute-start | bytes 2359304 | tf_op jit(solution)/shard_map/ppermute | solution.py:675
  197.1 0.9 copy-start.2
  200.6 25.6 %collective-permute-start.7 = (bf16[128,768]{1,0:T(8,128)(2,1)}, bf16[128,768]{1,0:T(8,128)(2,1)S(1)}, u32[]{:S(2)}, u32[]{:S(2)}) collective-permute-start(bf16[128,768]{1,0:T(8,128)(2,1)} %get-tuple-element.87), channel_id=1, source_target_pairs={{0,2},{1,3},{2,4},{3,5},{4,6},{5,7},{6,0},{7,1},{8,10},{9,11},{10,... | collective-permute-start | bytes 589832 | tf_op jit(solution)/shard_map/ppermute | solution.py:627
  201.3 29.7 %collective-permute-start.8 = (bf16[128,768]{1,0:T(8,128)(2,1)}, bf16[128,768]{1,0:T(8,128)(2,1)S(1)}, u32[]{:S(2)}, u32[]{:S(2)}) collective-permute-start(bf16[128,768]{1,0:T(8,128)(2,1)} %get-tuple-element.88), channel_id=1, source_target_pairs={{0,4},{1,5},{2,6},{3,7},{4,0},{5,1},{6,2},{7,3},{8,12},{9,13},{10,... | collective-permute-start | bytes 589832 | tf_op jit(solution)/shard_map/ppermute | solution.py:627
  203.8 27.3 %collective-permute-start.9 = (bf16[128,768]{1,0:T(8,128)(2,1)}, bf16[128,768]{1,0:T(8,128)(2,1)S(1)}, u32[]{:S(2)}, u32[]{:S(2)}) collective-permute-start(bf16[128,768]{1,0:T(8,128)(2,1)} %get-tuple-element.89), channel_id=1, source_target_pairs={{0,6},{1,7},{2,0},{3,1},{4,2},{5,3},{6,4},{7,5},{8,14},{9,15},{10,... | collective-permute-start | bytes 589832 | tf_op jit(solution)/shard_map/ppermute | solution.py:627
  226.2 4.8 %copy-start.6 = (bf16[128,768]{1,0:T(8,128)(2,1)}, bf16[128,768]{1,0:T(8,128)(2,1)S(1)}, u32[]{:S(2)}) copy-start(bf16[128,768]{1,0:T(8,128)(2,1)S(1)} %collective-permute-done.7.d1_ref) | copy-start | bytes 589828
  231.1 0.7 copy-start.7
  231.1 0.7 copy-start.8
  234.3 1.4 copy-start.1
Sparse Core Ops, SparseCore 0:
  9.7 46.3 all-gather.1

commit v2 on v1

v2 whole, which is shorter than its diff:
```python
import functools

import jax
import jax.numpy as jnp
from jax import lax
from jax.experimental import pallas as pl
from jax.experimental.pallas import tpu as pltpu
from jax.sharding import PartitionSpec as P

bf16 = jnp.bfloat16
f32 = jnp.float32

WIDTH = 768
TOK = 128
LEN = 1024
FF = 3072
GROUP = 3
HD = 64
COLS = GROUP * HD
BAND = 5 * TOK
HALF = WIDTH // 2
PACK = 896
SENT = 640
LATE = 512
FF_TILE = 512
eps = 1e-06
bucket_edges = (12, 16, 23, 32, 46, 64, 91)
BOTH = ("fsdp", "seq")


def params(mib):
    return pltpu.CompilerParams(vmem_limit_bytes=mib << 20)


smem = pl.BlockSpec(memory_space=pltpu.SMEM)
vmem = pl.BlockSpec(memory_space=pltpu.VMEM)


def iota(shape, dim):
    return lax.broadcasted_iota(jnp.int32, shape, dim)


def sixth(n):
    return (n * 10923) >> 16


def third(n):
    return (n * 21846) >> 16


def bucket_of(offsets):
    spread = jnp.abs(offsets)
    ids = (offsets > 0).astype(jnp.int32) * 16 + jnp.minimum(spread, 8)
    for border in bucket_edges:
        ids = ids + (spread >= border).astype(jnp.int32)
    return ids


def mm(a, b):
    return jnp.dot(a, b, preferred_element_type=f32)


def mm_nt(a, b):
    return lax.dot_general(a, b, (((1,), (1,)), ((), ())), preferred_element_type=f32)


def mm_tn(a, b):
    return lax.dot_general(a, b, (((0,), (0,)), ((), ())), preferred_element_type=f32)


def exact(a, b):
    return lax.dot_general(
        a,
        b,
        (((1,), (0,)), ((), ())),
        precision=lax.Precision.HIGHEST,
        preferred_element_type=f32,
    )


def cost(us):
    return pl.CostEstimate(flops=int(us * 1.15e9), bytes_accessed=1 << 20, transcendentals=0)


def call(kernel, outs, ins, scratch=(), mib=16, us=2, **kw):
    return pl.pallas_call(
        kernel,
        out_shape=outs,
        in_specs=ins,
        out_specs=jax.tree.map(lambda _: vmem, outs),
        scratch_shapes=list(scratch),
        compiler_params=params(mib),
        cost_estimate=cost(us),
        **kw,
    )


def load_rows(ref, start, stride):
    return jnp.concatenate(
        [ref[j, pl.ds(start, 128, stride=stride), :] for j in range(ref.shape[0])], axis=1
    )


def store_rows(ref, start, stride, value):
    for j in range(value.shape[1] // 128):
        ref[j, pl.ds(start, 128, stride=stride), :] = value[:, 128 * j : 128 * j + 128]


def whole(ref, first, last):
    return jnp.concatenate([ref[j] for j in range(first, last)], axis=1)


def fill(ref, value):
    for j in range(ref.shape[0]):
        ref[j] = value[:, 128 * j : 128 * j + 128].astype(f32)


def sds(*shape, dtype=bf16):
    return jax.ShapeDtypeStruct(shape, dtype)


def pack_kernel(q_ref, k_ref, v_ref, o_ref, r_ref, small_ref, out_ref):
    zero = jnp.zeros((2, 576), f32)
    q, k, v, o, r = (ref[...].astype(f32) for ref in (q_ref, k_ref, v_ref, o_ref, r_ref))
    small = small_ref[...].astype(f32)
    blocks = []
    for y in range(4):
        at = slice(COLS * y, COLS * y + COLS)
        three = jnp.concatenate([q[:, at], k[:, at], v[:, at]], axis=1)
        for c in range(2):
            left = o[:, HALF * c : HALF * c + 320]
            right = [o[i : i + 1, HALF * c + 320 : HALF * c + HALF] for i in range(6)]
            routed = [r[i : i + 1, 64 * c : 64 * c + 64] for i in range(6)]
            row6 = jnp.concatenate(right + routed + [small], axis=1)
            six = jnp.concatenate([three, left], axis=1)
            blocks.append(jnp.concatenate([six, row6, jnp.zeros((1, PACK), f32)], axis=0))
    block = jnp.concatenate(blocks, axis=0).astype(bf16)
    for f in range(16):
        out_ref[64 * f : 64 * f + 64, :] = block


def pack_weights(w_query, w_key, w_value, w_output, w_router, small):
    return call(pack_kernel, [sds(LEN, PACK)], [vmem] * 6, name="pack_weights", mib=56)(
        w_query, w_key, w_value, w_output, w_router, small
    )[0]


def unpack_kernel(
    idx_ref, pack_ref, wqkv_ref, half_ref, gain_ref, band_ref, pf_ref, wf_ref, tail_ref
):
    y = idx_ref[0]
    fill(pf_ref, pack_ref)
    for r in range(6):
        store_rows(wf_ref, r, 6, load_rows(pf_ref, r, 8))
    row6 = load_rows(pf_ref, 6, 8)
    for r in range(6):
        tail = [row6[:, 64 * r : 64 * r + 64], row6[:, HALF + 64 * r : HALF + 64 * r + 64]]
        tail_ref[pl.ds(r, 128, stride=6), :] = jnp.concatenate(tail, axis=1)
    wqkv_ref[...] = whole(wf_ref, 0, 5)[:, : 3 * COLS].astype(bf16)
    left = whole(wf_ref, 4, 7)[:, 64:]
    blank = jnp.zeros((WIDTH, 64), f32)
    half_ref[...] = jnp.concatenate([left, tail_ref[...], blank], axis=1).astype(bf16)
    small = row6[:, WIDTH:].astype(bf16)

    lanes = iota((128, WIDTH), 1)
    rows = iota((128, WIDTH), 0)
    own = sixth(lanes) == rows
    within = lanes - 6 * sixth(lanes)
    gains = []
    for base in (0, 6):
        spread = mm(small, (rows == within + base).astype(bf16))
        gains.append(jnp.sum(jnp.where(own, spread, 0.0), axis=0, keepdims=True))
    gain_ref[...] = jnp.concatenate([gains[0], gains[1], jnp.zeros((6, WIDTH), f32)], axis=0)
    lanes = iota((128, 384), 1)
    rows = iota((128, 384), 0)
    spread = mm(small, (rows == lanes - 3 * third(lanes) + 12).astype(bf16))
    table = jnp.sum(jnp.where(third(lanes) == rows, spread, 0.0), axis=0, keepdims=True)
    table = jnp.broadcast_to(table, (8, 384)).astype(bf16)
    ids = bucket_of(iota((384, 512), 1) - 255)
    entry = iota((384, 512), 0)
    for h in range(GROUP):
        hot = (entry == ids + 32 * (3 * y + h)).astype(bf16)
        line = mm(table, hot)[:1]
        wide = pltpu.roll(
            jnp.broadcast_to(line, (TOK, 512)), 385, 1, stride=1, stride_axis=0
        )
        band_ref[h, :, :TOK] = jnp.broadcast_to(line[:, :1], (TOK, TOK))
        band_ref[h, :, TOK : 4 * TOK] = wide[:, : 3 * TOK]
        band_ref[h, :, 4 * TOK :] = jnp.broadcast_to(line[:, 511:], (TOK, TOK))


def unpack_weights(idx, pack):
    outs = [
        sds(WIDTH, 3 * COLS), sds(WIDTH, 512), sds(8, WIDTH, dtype=f32),
        sds(GROUP, TOK, BAND, dtype=f32),
    ]
    return call(
        unpack_kernel,
        outs,
        [smem, vmem],
        [
            pltpu.VMEM((7, LEN, 128), f32),
            pltpu.VMEM((7, WIDTH, 128), f32),
            pltpu.VMEM((WIDTH, 128), f32),
        ],
        name="unpack_weights",
        mib=56,
        us=4,
    )(idx, pack)


def banded(band_ref, h, pq):
    parts = []
    for j in range(8):
        at = jnp.clip(j - pq + 2, 0, 4) * TOK
        parts.append(band_ref[h, :, pl.ds(pl.multiple_of(at, TOK), TOK)])
    return jnp.concatenate(parts, axis=1)


def attend_kernel(
    idx_ref, x_ref, seg_ref, wqkv_ref, gain_ref, band_ref,
    o0_ref, o1_ref, o2_ref, o3_ref, h_ref, qe_ref, ke_ref, v_ref, lse_ref,
    os_ref,
):
    y, c = idx_ref[0], idx_ref[1]
    gain = gain_ref[:1, :]

    def project(i, _):
        at = pl.ds(pl.multiple_of(i * TOK, TOK), TOK)
        x = x_ref[at, :].astype(f32)
        hb = (x * lax.rsqrt(jnp.mean(x * x, axis=-1, keepdims=True) + eps) * gain).astype(bf16)
        h_ref[at, :] = hb
        qkv = mm(hb, wqkv_ref[...])
        doc = seg_ref[at, :]
        lane = iota((TOK, HD), 1)
        same = lane == doc
        q_mark = jnp.where(same, -1e30, 0.0)
        k_mark = jnp.where((lane < 3) & jnp.logical_not(same), 1.0, 0.0)
        q_parts, k_parts = [], []
        for h in range(GROUP):
            q = qkv[:, HD * h : HD * h + HD]
            k = qkv[:, COLS + HD * h : COLS + HD * h + HD]
            q_parts += [q.astype(bf16).astype(f32) * 0.125, q_mark]
            k_parts += [k, k_mark]
        qe_ref[at, :] = jnp.concatenate(q_parts, axis=1).astype(bf16)
        ke_ref[at, :] = jnp.concatenate(k_parts, axis=1).astype(bf16)
        v_ref[at, :] = qkv[:, 2 * COLS :].astype(bf16)
        return 0

    lax.fori_loop(0, 8, project, 0)

    def attend(k, _):
        yq = lax.rem(y + k, 4)
        pq = 2 * yq + c
        at = pl.ds(pl.multiple_of(pq * TOK, TOK), TOK)
        lane = iota((TOK, 128), 1)
        lse_all = jnp.zeros((TOK, 128), f32)
        outs = []
        for h in range(GROUP):
            s = mm_nt(qe_ref[at, 128 * h : 128 * h + 128], ke_ref[:, 128 * h : 128 * h + 128])
            s = s + banded(band_ref, h, pq)
            top = jnp.max(s, axis=-1, keepdims=True)
            e = jnp.exp(s - top)
            total = jnp.sum(e, axis=-1, keepdims=True)
            p = (e * (1.0 / total)).astype(bf16)
            outs.append(mm(p, v_ref[:, HD * h : HD * h + HD]))
            lse_all = jnp.where(lane == h, top + jnp.log(total), lse_all)
        os_ref[k] = jnp.concatenate(outs, axis=1).astype(bf16)
        lse_ref[yq] = lse_all
        return 0

    lax.fori_loop(0, 4, attend, 0)
    o0_ref[...] = os_ref[0]
    o1_ref[...] = os_ref[1]
    o2_ref[...] = os_ref[2]
    o3_ref[...] = os_ref[3]


def attend(idx, x_all, seg_col, wqkv, gains, band):
    outs = [sds(TOK, COLS)] * 4 + [
        sds(LEN, WIDTH), sds(LEN, 384), sds(LEN, 384), sds(LEN, COLS),
        sds(4, TOK, 128, dtype=f32),
    ]
    return call(
        attend_kernel,
        outs,
        [smem] + [vmem] * 5,
        [pltpu.VMEM((4, TOK, COLS), bf16)],
        name="attend",
        mib=56,
        us=12,
    )(idx, x_all, seg_col, wqkv, gains, band)


def dispatch_kernel(
    idx_ref, x_ref, o0_ref, o1_ref, o2_ref, o3_ref, half_ref, rest_ref, gain_ref,
    route_ref, cot_ref,
    x1_ref, h2_ref, prob_ref, hot_ref, send_ref, wo_ref, router_ref,
    sf_ref,
):
    y, c = idx_ref[0], idx_ref[1]
    wo_ref[:, pl.ds(pl.multiple_of(c * HALF, 128), HALF)] = half_ref[:, :HALF]
    wo_ref[:, pl.ds(pl.multiple_of((1 - c) * HALF, 128), HALF)] = rest_ref[:, :HALF]
    here = half_ref[:, HALF : HALF + 128].astype(f32)[:, :64]
    there = rest_ref[:, HALF : HALF + 128].astype(f32)[:, :64]
    router_ref[...] = jnp.where(
        c == 0,
        jnp.concatenate([here, there], axis=1),
        jnp.concatenate([there, here], axis=1),
    ).astype(bf16)
    x1 = x_ref[...].astype(f32)
    for k, o_ref in enumerate((o0_ref, o1_ref, o2_ref, o3_ref)):
        src = lax.rem(y + 4 - k, 4)
        x1 = x1 + mm(o_ref[...], wo_ref[pl.ds(pl.multiple_of(src * COLS, COLS), COLS), :])
    x1_ref[...] = x1
    r2 = lax.rsqrt(jnp.mean(x1 * x1, axis=-1, keepdims=True) + eps)
    h2 = (x1 * r2 * gain_ref[1:2, :]).astype(bf16)
    h2_ref[...] = h2
    logits = mm(h2, router_ref[...])
    e = jnp.exp(logits - jnp.max(logits, axis=-1, keepdims=True))
    prob = e / jnp.sum(e, axis=-1, keepdims=True)
    prob_ref[...] = prob
    expert = iota((TOK, 128), 1)
    picked = (route_ref[...] == expert).astype(f32)
    gate = jnp.sum(prob * picked, axis=-1, keepdims=True)
    earlier = (iota((TOK, TOK), 0) > iota((TOK, TOK), 1)).astype(bf16)
    slot = jnp.sum(mm(earlier, picked.astype(bf16)) * picked, axis=-1, keepdims=True)
    geo = (gate * cot_ref[...].astype(f32)).astype(bf16)
    for s in range(2):
        hot = jnp.where((slot > 0.5) == (s == 1), picked, 0.0).astype(bf16)
        hot_ref[s] = hot
        for kind, src in enumerate((h2, geo)):
            placed = mm_tn(hot, src)
            for half in range(2):
                part = placed[:, HALF * half : HALF * half + HALF]
                store_rows(sf_ref, kind * 4 + s * 2 + half, 8, part)
    send_ref[...] = whole(sf_ref, 0, 3).astype(bf16)


def dispatch(idx, x_own, o_parts, half, rest, gains, route_col, cot):
    outs = [
        sds(TOK, WIDTH, dtype=f32), sds(TOK, WIDTH), sds(TOK, 128, dtype=f32),
        sds(2, TOK, 128), sds(LEN, HALF), sds(WIDTH, WIDTH), sds(WIDTH, 128),
    ]
    return call(
        dispatch_kernel,
        outs,
        [smem] + [vmem] * 10,
        [pltpu.VMEM((3, LEN, 128), f32)],
        name="dispatch",
        mib=10,
    )(idx, x_own, *o_parts, half, rest, gains, route_col, cot)


def expert_kernel(
    recv_ref, wi_ref, wo_ref, ret_ref, gi_ref, go_ref, rf_ref, x_ref, xt_ref, g_ref, eo_ref, gx_ref
):
    step = pl.program_id(0)

    @pl.when(step == 0)
    def _():
        fill(rf_ref, recv_ref)
        for kind, dst in enumerate((x_ref, g_ref)):
            for s in range(2):
                for half in range(2):
                    dst[TOK * s : TOK * s + TOK, HALF * half : HALF * half + HALF] = load_rows(
                        rf_ref, kind * 4 + s * 2 + half, 8
                    ).astype(bf16)
        xt_ref[...] = x_ref[...].T
        eo_ref[...] = jnp.zeros_like(eo_ref)
        gx_ref[...] = jnp.zeros_like(gx_ref)

    wi = wi_ref[...]
    wo = wo_ref[...]
    g = g_ref[...]
    a = mm(x_ref[...], wi)
    cc = 0.7978845608028654
    sq = a * a
    t = jnp.tanh(cc * (a + 0.044715 * (sq * a)))
    u = (0.5 * a * (1.0 + t)).astype(bf16)
    slope = 0.5 * (1.0 + t) + (0.5 * cc) * a * (1.0 - t * t) * (1.0 + 0.134145 * sq)
    eo_ref[...] += mm(u, wo)
    ga = (mm_nt(g, wo) * slope).astype(bf16)
    go_ref[...] = mm_tn(u, g).astype(bf16)
    gi_ref[...] = mm(xt_ref[...], ga).astype(bf16)
    gx_ref[...] += mm_nt(ga, wi)

    @pl.when(step == FF // FF_TILE - 1)
    def _():
        for kind, src in enumerate((eo_ref, gx_ref)):
            for s in range(2):
                for half in range(2):
                    part = src[TOK * s : TOK * s + TOK, HALF * half : HALF * half + HALF]
                    store_rows(rf_ref, kind * 4 + s * 2 + half, 8, part)
        ret_ref[...] = whole(rf_ref, 0, 3).astype(bf16)


def experts(recv, w_inner, w_outer):
    return pl.pallas_call(
        expert_kernel,
        grid=(FF // FF_TILE,),
        out_shape=[sds(LEN, HALF), sds(1, WIDTH, FF), sds(1, FF, WIDTH)],
        in_specs=[
            pl.BlockSpec((LEN, HALF), lambda i: (0, 0)),
            pl.BlockSpec((None, WIDTH, FF_TILE), lambda i: (0, 0, i)),
            pl.BlockSpec((None, FF_TILE, WIDTH), lambda i: (0, i, 0)),
        ],
        out_specs=[
            pl.BlockSpec((LEN, HALF), lambda i: (0, 0)),
            pl.BlockSpec((None, WIDTH, FF_TILE), lambda i: (0, 0, i)),
            pl.BlockSpec((None, FF_TILE, WIDTH), lambda i: (0, i, 0)),
        ],
        scratch_shapes=[
            pltpu.VMEM((3, LEN, 128), f32),
            pltpu.VMEM((2 * TOK, WIDTH), bf16),
            pltpu.VMEM((WIDTH, 2 * TOK), bf16),
            pltpu.VMEM((2 * TOK, WIDTH), bf16),
            pltpu.VMEM((2 * TOK, WIDTH), f32),
            pltpu.VMEM((2 * TOK, WIDTH), f32),
        ],
        compiler_params=params(56),
        cost_estimate=cost(14),
        name="experts",
    )(recv, w_inner, w_outer)


def return_kernel(
    idx_ref, back_ref, x1_ref, h2_ref, prob_ref, hot_ref, cot_ref, router_ref, gain_ref, wo_ref,
    o0_ref, o1_ref, o2_ref, o3_ref,
    out_ref, dx1_ref, g0_ref, g1_ref, g2_ref, g3_ref, keep_ref, give_ref, dgain_ref,
    bf_ref,
):
    y, c = idx_ref[0], idx_ref[1]
    fill(bf_ref, back_ref)
    parts = []
    for kind in range(2):
        halves = []
        for half in range(2):
            got = jnp.zeros((TOK, HALF), f32)
            for s in range(2):
                rows = load_rows(bf_ref, kind * 4 + s * 2 + half, 8).astype(bf16)
                got = got + mm(hot_ref[s], rows)
            halves.append(got)
        parts.append(jnp.concatenate(halves, axis=1))
    eo, gx = parts
    x1 = x1_ref[...]
    prob = prob_ref[...]
    picked = hot_ref[0].astype(f32) + hot_ref[1].astype(f32)
    gate = jnp.sum(prob * picked, axis=-1, keepdims=True)
    out_ref[...] = (x1 + gate * eo).astype(bf16)
    dy = cot_ref[...].astype(f32)
    dgate = jnp.sum(dy * eo, axis=-1, keepdims=True)
    gz = (dgate * gate * (picked - prob)).astype(bf16)
    dh2 = gx + mm_nt(gz, router_ref[...])
    routed = mm_tn(h2_ref[...], gz)
    blank = jnp.zeros((WIDTH, 64), f32)
    near = jnp.concatenate([routed[:, :64], blank], axis=1)
    far = jnp.concatenate([routed[:, 64:], blank], axis=1)
    keep_ref[:, HALF:] = jnp.where(c == 0, near, far).astype(bf16)
    give_ref[:, HALF:] = jnp.where(c == 0, far, near).astype(bf16)
    r2 = lax.rsqrt(jnp.mean(x1 * x1, axis=-1, keepdims=True) + eps)
    scaled = x1 * r2
    dgain = jnp.sum(dh2 * scaled, axis=0, keepdims=True)
    dgain_ref[...] = jnp.broadcast_to(dgain, (8, WIDTH))
    gd = gain_ref[1:2, :] * dh2
    dx1 = dy + r2 * (gd - scaled * jnp.mean(gd * scaled, axis=-1, keepdims=True))
    dx1_ref[...] = dx1
    gw = dx1.astype(bf16)
    for k, g_ref in enumerate((g0_ref, g1_ref, g2_ref, g3_ref)):
        dst = lax.rem(y + k, 4)
        rows = wo_ref[pl.ds(pl.multiple_of(dst * COLS, COLS), COLS), :]
        g_ref[...] = mm_nt(gw, rows).astype(bf16)
    for k, o_ref in enumerate((o0_ref, o1_ref, o2_ref, o3_ref)):
        src = lax.rem(y + 4 - k, 4)
        rows = pl.ds(pl.multiple_of(src * COLS, COLS), COLS)
        terms = mm_tn(o_ref[...], gw)
        near, far = terms[:, :HALF], terms[:, HALF:]
        keep_ref[rows, :HALF] = jnp.where(c == 0, near, far).astype(bf16)
        give_ref[rows, :HALF] = jnp.where(c == 0, far, near).astype(bf16)


def returned(idx, back, x1, h2, prob, hot, cot, router, gains, wo, o_parts):
    outs = (
        [sds(TOK, WIDTH), sds(TOK, WIDTH, dtype=f32)]
        + [sds(TOK, COLS)] * 4
        + [sds(WIDTH, LATE), sds(WIDTH, LATE), sds(8, WIDTH, dtype=f32)]
    )
    return call(
        return_kernel,
        outs,
        [smem] + [vmem] * 13,
        [pltpu.VMEM((3, LEN, 128), f32)],
        name="returned",
        mib=14,
    )(idx, back, x1, h2, prob, hot, cot, router, gains, wo, *o_parts)


def backward_kernel(
    idx_ref, g0_ref, g1_ref, g2_ref, g3_ref, x_ref, wqkv_ref, qe_ref, ke_ref, v_ref,
    band_ref, lse_ref,
    own_ref, other_ref, dq_ref, line_ref, acc_ref,
    gs_ref, gk_ref, gv_ref,
):
    y, c = idx_ref[0], idx_ref[1]
    for k, g_ref in enumerate((g0_ref, g1_ref, g2_ref, g3_ref)):
        gs_ref[k] = g_ref[...]
    gk_ref[...] = jnp.zeros_like(gk_ref)
    gv_ref[...] = jnp.zeros_like(gv_ref)
    acc_ref[...] = jnp.zeros_like(acc_ref)

    def block(k, _):
        yq = lax.rem(y + 4 - k, 4)
        pq = 2 * yq + c
        at = pl.ds(pl.multiple_of(pq * TOK, TOK), TOK)
        not_at = pl.ds(pl.multiple_of((pq + 1 - 2 * c) * TOK, TOK), TOK)
        lse = lse_ref[yq]
        go = gs_ref[k]
        outs = []
        for h in range(GROUP):
            q = qe_ref[at, 128 * h : 128 * h + 128]
            keys = ke_ref[:, 128 * h : 128 * h + 128]
            g = go[:, HD * h : HD * h + HD]
            s = mm_nt(q, keys) + banded(band_ref, h, pq)
            p = jnp.exp(s - lse[:, h : h + 1])
            pd = p * mm_nt(g, v_ref[:, HD * h : HD * h + HD])
            gs = pd - p * jnp.sum(pd, axis=-1, keepdims=True)
            for j in range(8):
                to = pl.multiple_of(jnp.clip(j - pq + 2, 0, 4) * TOK, TOK)
                acc_ref[h, :, pl.ds(to, TOK)] += gs[:, TOK * j : TOK * j + TOK]
            low = gs.astype(bf16)
            outs.append(mm(low, keys)[:, :HD] * 0.125)
            gk_ref[HD * h : HD * h + HD, :] += mm_tn(q, low)[:HD]
            gv_ref[HD * h : HD * h + HD, :] += mm_tn(g, p.astype(bf16))
        dq_ref[at, :COLS] = jnp.concatenate(outs, axis=1).astype(bf16)
        dq_ref[not_at, :COLS] = jnp.zeros((TOK, COLS), bf16)
        return 0

    lax.fori_loop(0, 4, block, 0)
    dq_ref[:, COLS : 2 * COLS] = gk_ref[...].T.astype(bf16)
    dq_ref[:, 2 * COLS :] = gv_ref[...].T.astype(bf16)
    line_ref[...] = jnp.zeros_like(line_ref)

    def spread(yq, _):
        lines = jnp.zeros((1, WIDTH), f32)
        for side in range(2):
            pq = 2 * yq + (c if side == 0 else 1 - c)
            at = pl.ds(pl.multiple_of(pq * TOK, TOK), TOK)
            d = mm_nt(dq_ref[at, :], wqkv_ref[...])
            x = x_ref[at, :].astype(f32)
            r1 = lax.rsqrt(jnp.mean(x * x, axis=-1, keepdims=True) + eps)
            lines = lines + jnp.sum(d * (x * r1), axis=0, keepdims=True)
            if side == 0:
                own_ref[yq] = d
            else:
                other_ref[yq] = d.astype(bf16)
        line_ref[...] += jnp.broadcast_to(lines, (8, WIDTH))
        return 0

    lax.fori_loop(0, 4, spread, 0)


def attend_back(idx, go_parts, x_all, wqkv, qe, ke, v, band, lse):
    outs = [
        sds(4, TOK, WIDTH, dtype=f32), sds(4, TOK, WIDTH), sds(LEN, 3 * COLS),
        sds(8, WIDTH, dtype=f32), sds(GROUP, TOK, BAND, dtype=f32),
    ]
    return call(
        backward_kernel,
        outs,
        [smem] + [vmem] * 11,
        [
            pltpu.VMEM((4, TOK, COLS), bf16),
            pltpu.VMEM((COLS, LEN), f32),
            pltpu.VMEM((COLS, LEN), f32),
        ],
        name="attend_back",
        mib=24,
        us=12,
    )(idx, *go_parts, x_all, wqkv, qe, ke, v, band, lse)


def terms_kernel(
    idx_ref, h_ref, dq_ref, line_ref, dgain_ref, acc_ref, keep_ref, got_ref, send_ref
):
    y = idx_ref[0]
    ids = bucket_of(iota((512, 128), 0) - 255)
    flat = iota((512, 128), 1)
    turn = (iota((TOK, TOK), 0) + iota((TOK, TOK), 1) == TOK - 1).astype(f32)
    table = jnp.zeros((8, 128), f32)
    flat_lane = iota((8, 128), 1)
    for h in range(GROUP):
        near = exact(turn, acc_ref[h, :, TOK : 4 * TOK])
        near = jnp.concatenate([near, jnp.zeros((TOK, TOK), f32)], axis=1)
        near = pltpu.roll(near, 0, 1, stride=1, stride_axis=0)
        diag = jnp.broadcast_to(jnp.sum(near, axis=0, keepdims=True), (8, 512))
        table = table + exact(diag, (flat == ids + 32 * h).astype(f32))
        low = jnp.sum(acc_ref[h, :, :TOK])
        high = jnp.sum(acc_ref[h, :, 4 * TOK :])
        table = table + jnp.where(flat_lane == 32 * h + 15, low, 0.0)
        table = table + jnp.where(flat_lane == 32 * h + 31, high, 0.0)
    lanes = iota((128, WIDTH), 1)
    entry = iota((128, WIDTH), 0)
    group = sixth(lanes)
    within = lanes - 6 * group
    place = (within < 3) & (entry + 96 * y == 3 * group + within) & (entry < 96)
    table = exact(table, place.astype(f32))
    lines = []
    for v in (line_ref[:1, :], dgain_ref[:1, :], table[:1, :]):
        high = v.astype(bf16).astype(f32)
        lines += [high, v - high]
    block = jnp.concatenate(lines + [jnp.zeros((122, WIDTH), f32)], axis=0).T
    block = jnp.concatenate([jnp.zeros((WIDTH, 64), f32), block[:, :64]], axis=1)
    send_ref[:, 512:SENT] = block.astype(bf16)
    send_ref[:, SENT:] = (keep_ref[...].astype(f32) + got_ref[...].astype(f32)).astype(bf16)

    def weights(j, _):
        at = pl.ds(pl.multiple_of(j * 128, 128), 128)
        terms = mm_tn(h_ref[:, at], dq_ref[...])
        send_ref[at, :512] = terms[:, :512].astype(bf16)
        extra = send_ref[at, 512:SENT].astype(f32)
        last = jnp.concatenate([terms[:, 512:], extra[:, 64:]], axis=1)
        send_ref[at, 512:SENT] = last.astype(bf16)
        return 0

    lax.fori_loop(0, 6, weights, 0)


def weight_terms(idx, h, dq, line, dgain, acc, keep, got):
    return call(
        terms_kernel,
        [sds(WIDTH, SENT + LATE)],
        [smem] + [vmem] * 7,
        name="weight_terms",
        mib=14,
        us=5,
    )(idx, h, dq, line, dgain, acc, keep, got)[0]


def pair_kernel(idx_ref, own_ref, got_ref, d0_ref, d1_ref, d2_ref, d3_ref):
    y = idx_ref[0]
    for k, d_ref in enumerate((d0_ref, d1_ref, d2_ref, d3_ref)):
        dst = lax.rem(y + k, 4)
        d_ref[...] = (own_ref[dst] + got_ref[dst].astype(f32)).astype(d_ref.dtype)


def pair_sum(idx, own, got):
    outs = [sds(TOK, WIDTH, dtype=f32)] + [sds(TOK, WIDTH)] * 3
    return call(pair_kernel, outs, [smem, vmem, vmem], name="pair_sum")(idx, own, got)


def tokens_kernel(d0_ref, d1_ref, d2_ref, d3_ref, x_ref, gain_ref, dx1_ref, out_ref):
    dh = d0_ref[...] + d1_ref[...].astype(f32) + d2_ref[...].astype(f32) + d3_ref[...].astype(f32)
    x = x_ref[...].astype(f32)
    r1 = lax.rsqrt(jnp.mean(x * x, axis=-1, keepdims=True) + eps)
    gd = gain_ref[:1, :] * dh
    scaled = x * r1
    out_ref[...] = dx1_ref[...] + r1 * (gd - scaled * jnp.mean(gd * scaled, axis=-1, keepdims=True))


def tokens_last(d_parts, x_own, gains, dx1):
    return call(tokens_kernel, [sds(TOK, WIDTH, dtype=f32)], [vmem] * 7, name="tokens_last")(
        *d_parts, x_own, gains, dx1
    )[0]


def middle_kernel(got_ref, out_ref):
    def total(a, b):
        sums = got_ref[:48, a:b].astype(f32)
        for f in range(1, 16):
            sums = sums + got_ref[48 * f : 48 * f + 48, a:b].astype(f32)
        return sums

    pieces = [total(0, 512)]
    last = total(512, SENT)
    lane = iota((48, 128), 1)
    both = last + pltpu.roll(last, 127, 1)
    high = both.astype(bf16).astype(f32)
    rest = pltpu.roll(both - high, 1, 1)
    last = jnp.where(lane < 64, last, jnp.where(lane % 2 == 0, high, rest))
    pieces += [last, total(SENT, SENT + LATE)]
    sums = jnp.concatenate(pieces, axis=1)
    blank = jnp.zeros((2, SENT + LATE), f32)
    rows = []
    for s in range(8):
        rows += [sums[6 * s : 6 * s + 6], blank]
    out_ref[...] = jnp.concatenate(rows, axis=0).astype(bf16)


def middle_sums(got):
    return call(middle_kernel, [sds(64, SENT + LATE)], [vmem], name="middle_sums", mib=8)(got)[0]


def sums_kernel(recv_ref, q_ref, k_ref, v_ref, o_ref, router_ref, small_ref):
    got = recv_ref[...].astype(f32)
    parts = [got[8 * s : 8 * s + 8] for s in range(8)]
    quads = [parts[2 * y] + parts[2 * y + 1] for y in range(4)]
    for m, ref in enumerate((q_ref, k_ref, v_ref)):
        cols = jnp.concatenate([a[:, COLS * m : COLS * m + COLS] for a in quads], axis=1)
        ref[...] = cols[:6].astype(bf16)
    halves = [parts[c] + parts[2 + c] + parts[4 + c] + parts[6 + c] for c in range(2)]
    o_ref[...] = jnp.concatenate([a[:6, SENT : SENT + HALF] for a in halves], axis=1).astype(bf16)
    routed = [a[:6, SENT + HALF : SENT + HALF + 64] for a in halves]
    router_ref[...] = jnp.concatenate(routed, axis=1).astype(bf16)
    small_ref[...] = halves[0][:, 512:SENT] + halves[1][:, 512:SENT]


def sums_last(recv):
    outs = [sds(6, WIDTH)] * 4 + [sds(6, 128), sds(8, 128, dtype=f32)]
    return call(sums_kernel, outs, [vmem], name="sums_last", mib=4)(recv)


def along_y(v, k):
    return lax.ppermute(v, "seq", [(s, (s + 2 * k) % 8) for s in range(8)])


def exchange(v, axes):
    return lax.all_to_all(v, axes, split_axis=0, concat_axis=0, tiled=True)


def other_core(v):
    return lax.ppermute(v, "seq", [(s, s ^ 1) for s in range(8)])


def on_device(
    tokens, segments, routes, gain_attn, w_query, w_key, w_value, w_output, rel_table, gain_moe,
    w_router, w_inner, w_outer, cotangent,
):
    seq = lax.axis_index("seq")
    idx = jnp.stack([seq // 2, seq % 2]).astype(jnp.int32)
    x_all = lax.all_gather(tokens, "seq", axis=0, tiled=True)
    small = jnp.concatenate([gain_attn, gain_moe, rel_table, jnp.zeros((113,), bf16)])
    pack = pack_weights(w_query, w_key, w_value, w_output, w_router, small.reshape(1, 128))
    wqkv, half, gains, band = unpack_weights(idx, exchange(pack, BOTH))
    rest = other_core(half)
    attended = attend(idx, x_all, segments.reshape(LEN, 1), wqkv, gains, band)
    o_parts = attended[:4]
    h, qe, ke, v, lse = attended[4:]
    o_parts = [o_parts[0]] + [along_y(o_parts[k], k) for k in (1, 2, 3)]
    x1, h2, prob, hot, send, wo, router = dispatch(
        idx, tokens, o_parts, half, rest, gains, routes, cotangent
    )
    ret, grad_inner, grad_outer = experts(exchange(send, BOTH), w_inner, w_outer)
    back = exchange(ret, BOTH)
    layer_out, dx1, *more = returned(
        idx, back, x1, h2, prob, hot, cotangent, router, gains, wo, o_parts
    )
    go_parts = [more[0]] + [along_y(more[k], k) for k in (1, 2, 3)]
    keep, give, dgain = more[4:]
    late = other_core(give)
    own, other, dq_all, line, acc = attend_back(idx, go_parts, x_all, wqkv, qe, ke, v, band, lse)
    got = other_core(other)
    terms = weight_terms(idx, h, dq_all, line, dgain, acc, keep, late)
    d_parts = pair_sum(idx, own, got)
    d_parts = [d_parts[0]] + [along_y(d_parts[k], k) for k in (1, 2, 3)]
    sums = exchange(middle_sums(exchange(terms, "fsdp")), "seq")
    dq, dk, dv, do, dr, small = sums_last(sums)
    tokens_grad = tokens_last(d_parts, tokens, gains, dx1)
    lines = small[:6, 64:70]
    lines = lines[:, 0::2] + lines[:, 1::2]
    return (
        layer_out,
        tokens_grad,
        lines[:, 0].astype(bf16),
        dq,
        dk,
        dv,
        do,
        lines[:3, 2].astype(bf16),
        lines[:, 1].astype(bf16),
        dr,
        grad_inner,
        grad_outer,
    )


def solution(mesh):
    rows = P(BOTH, None)
    flat = P(BOTH)
    cube = P(BOTH, None, None)
    return jax.shard_map(
        on_device,
        mesh=mesh,
        in_specs=(
            rows, P("fsdp", None), rows, flat, rows, rows, rows, rows, flat, flat, rows, cube, cube,
            rows,
        ),
        out_specs=(rows, rows, flat, rows, rows, rows, rows, flat, flat, rows, cube, cube),
        check_vma=False,
    )
```

time: 249 us -> 219 us (0.88)
  waiting for transfers between devices: 66.2 us -> 48.7 us
  Pallas kernels: 72.1 us -> 61.3 us
  starting transfers between devices: 29.5 us -> 38.2 us
  local copies, waits for them, and re-layouts: 16 us -> 8.78 us
    ppermute x9, waiting for transfers between devices: 31.8 us -> 3.58 us  [along_y(): return lax.ppermute(v, 'seq', [(s, (s + 2 * k) % 8) for s in range(8)])]
    all_to_all x2 -> x3, waiting for transfers between devices: 31.8 us -> 42.5 us  [exchange(): return lax.all_to_all(v, axes, split_axis=0, concat_axis=0, tiled=True)]
    all_to_all x2 -> x3, starting transfers between devices: 18.3 us -> 23.4 us  [exchange(): return lax.all_to_all(v, axes, split_axis=0, concat_axis=0, tiled=True)]
    pallas_call x3 -> x7, Pallas kernels: 43.6 us -> 40.5 us  [the longest x1 13.5 us: attend(): call(attend_kernel, outs, [smem] + [vmem] * 5, [pltpu.VMEM((4, TOK, COLS)...]
    ppermute x1 -> x3, starting transfers between devices: 1.15 us -> 4.04 us  [other_core(): return lax.ppermute(v, 'seq', [(s, s ^ 1) for s in range(8)])]
    concatenate x2 -> x0, local copies, waits for them, and re-layouts: 2.78 us -> none  [the longest x1 2.77 us: on_device(): jnp.concatenate([w_router.reshape(-1), gain_attn, gain_moe, rel_table, jn...]
    convert_element_type x2 -> x0, other arithmetic: 2.74 us -> none  [the longest x1 1.41 us: on_device(): (line[12:18] + line[18:24]).astype(bf16)]
    pallas_call x1, Pallas kernels: 5.08 us -> 2.42 us  [returned(): call(return_kernel, outs, [smem] + [vmem] * 13, [pltpu.VMEM((3, LEN, 128)...]
  transfers between devices with their start and end apart: 13 -> 16, of which waited for: 10 -> 9; matrix products, arithmetic and copies ran while one was open for 4% -> 1% of each run, Pallas kernels for 2% -> 16%
where the time goes in v2:
time: 219 us
  Pallas kernels  61.3 us (28%)
  waiting for transfers between devices  48.7 us (22%)
  blocking collectives  45.5 us (21%)
  starting transfers between devices  38.2 us (17%)
  between operations  14.3 us (7%)
  local copies, waits for them, and re-layouts  8.78 us (4%)
    all_to_all x2, blocking collectives, exchange(): return lax.all_to_all(v, axes, split_axis=0, concat_axis=0, tiled=True)  45.5 us
    all_to_all x3, waiting for transfers between devices, exchange(): return lax.all_to_all(v, axes, split_axis=0, concat_axis=0, tiled=True)  42.5 us
    all_to_all x3, starting transfers between devices, exchange(): return lax.all_to_all(v, axes, split_axis=0, concat_axis=0, tiled=True)  23.4 us
    pallas_call x1, Pallas kernels, experts(): pl.pallas_call(expert_kernel, grid=(FF // FF_TILE,), out_shape=[sds(LEN,...  14.4 us
    pallas_call x1, Pallas kernels, attend(): call(attend_kernel, outs, [smem] + [vmem] * 5, [pltpu.VMEM((4, TOK, COLS)...  13.5 us
    pallas_call x1, Pallas kernels, attend_back(): call(backward_kernel, outs, [smem] + [vmem] * 11, [pltpu.VMEM((4, TOK, CO...  12 us
    ppermute x9, starting transfers between devices, along_y(): return lax.ppermute(v, 'seq', [(s, (s + 2 * k) % 8) for s in range(8)])  10.8 us
    pallas_call x1, Pallas kernels, weight_terms(): call(terms_kernel, [sds(WIDTH, SENT + LATE)], [smem] + [vmem] * 7, name='...  6.62 us
  transfers between devices with their start and end apart: 16, of which 9 were waited for; matrix products, arithmetic and copies ran while one was open for 1% of the time, Pallas kernels for 16%

profile of v2, /device:TPU:1, one launch (start us, length us, event | category | flops | bytes accessed | tf_op | source)
XLA Modules:
  0.0 218.6 jit_solution(14433723211046751843)
XLA Ops:
  7.2 0.7 all-gather.2.cloned.1.call-update
  7.9 1.3 maximum_bitcast_fusion.small_ref
  9.2 2.3 %pack_weights.1 = bf16[1024,896]{1,0:T(8,128)(2,1)} custom-call(bf16[6,768]{1,0:T(8,128)(2,1)} %q_ref.1, bf16[6,768]{1,0:T(8,128)(2,1)} %k_ref.1, bf16[6,768]{1,0:T(8,128)(2,1)} %v_ref.1, bf16[6,768]{1,0:T(8,128)(2,1)} %o_ref.1, bf16[6,128]{1,0:T(8,128)(2,1)} %r_ref.1, bf16[1,128]{1,0:T(2,128)(2,1)} %maximum_bitcast_fusion.small_ref), custom_call_target="tpu_custom_call" | custom-call | flops 2300000000 | bytes 1048576 | tf_op jit(solution)/shard_map/pack_weights/pallas_call | solution.py:143
  11.5 11.5 %all-to-all-start = ((bf16[128,8,896]{2,1,0:T(8,128)(2,1)}), bf16[128,8,896]{2,1,0:T(8,128)(2,1)S(1)}, u32[]{:S(2)}, u32[]{:S(2)}) async-start(bf16[128,8,896]{2,1,0:T(8,128)(2,1)} %bitcast.20), calls=%async_computation | async-start | bytes 3670016 | tf_op jit(solution)/shard_map/all_to_all | solution.py:717
  23.0 1.0 copy.27.seg_ref
  24.0 0.6 pad_add_fusion.idx_ref
  24.6 28.2 %all-to-all-done = bf16[128,8,896]{2,1,0:T(8,128)(2,1)S(1)} async-done(((bf16[128,8,896]{2,1,0:T(8,128)(2,1)}), bf16[128,8,896]{2,1,0:T(8,128)(2,1)S(1)}, u32[]{:S(2)}, u32[]{:S(2)}) %all-to-all-start) | async-done | bytes 1835040 | tf_op jit(solution)/shard_map/all_to_all | solution.py:717
  52.8 1.2 copy-done.19
  54.0 4.5 %unpack_weights.1 = (bf16[768,576]{1,0:T(8,128)(2,1)}, bf16[768,512]{1,0:T(8,128)(2,1)}, f32[8,768]{1,0:T(8,128)}, f32[3,128,640]{2,1,0:T(8,128)}) custom-call(s32[2]{0:T(128)} %pad_add_fusion.idx_ref, bf16[1024,896]{1,0:T(8,128)(2,1)} %bitcast.19), custom_call_target="tpu_custom_call" | custom-call | flops 4600000000 | bytes 1048576 | tf_op jit(solution)/shard_map/unpack_weights/pallas_call | solution.py:197
  58.6 13.5 %attend.1 = (bf16[128,192]{1,0:T(8,128)(2,1)}, bf16[128,192]{1,0:T(8,128)(2,1)}, bf16[128,192]{1,0:T(8,128)(2,1)}, bf16[128,192]{1,0:T(8,128)(2,1)}, bf16[1024,7...) custom-call(s32[2]{0:T(128)} %pad_add_fusion.idx_ref, ...), custom_call_target="tpu_custom_call" | custom-call | flops 13799999488 | bytes 1048576 | tf_op jit(solution)/shard_map/attend/pallas_call | solution.py:284
  72.1 1.2 collective-permute-start
  73.3 1.3 collective-permute-start.1
  74.6 2.0 collective-permute-start.2
  76.7 1.5 collective-permute-done.1.o2_ref
  78.2 0.6 collective-permute-done.2.o3_ref
  78.8 0.8 copy-done.12
  79.7 2.2 dispatch.1
  81.9 24.3 %all_to_all.55 = bf16[128,8,384]{2,1,0:T(8,128)(2,1)} all-to-all(bf16[128,8,384]{2,1,0:T(8,128)(2,1)S(1)} %bitcast.17), channel_id=1, replica_groups=mesh['fsdp'=16,'seq'=8] {'fsdp','seq'}, dimensions={0} | all-to-all | bytes 1572864 | tf_op jit(solution)/shard_map/all_to_all | solution.py:717
  106.2 14.4 %experts.1 = (bf16[1024,384]{1,0:T(8,128)(2,1)}, bf16[1,768,3072]{2,1,0:T(8,128)(2,1)}, bf16[1,3072,768]{2,1,0:T(8,128)(2,1)}) custom-call(bf16[1024,384]{1,0:T(8,128)(2,1)} %bitcast.21, bf16[1,768,3072]{2,1,0:T(8,128)(2,1)} %wi_ref.1, bf16[1,3072,768]{2,1,0:T(8,128)(2,1)} %wo_ref.1), custom_call_target="tpu_custom_call" | custom-call | flops 16099999744 | bytes 1048576 | tf_op jit(solution)/shard_map/experts/pallas_call | solution.py:399
  120.6 21.2 %all_to_all.56 = bf16[128,8,384]{2,1,0:T(8,128)(2,1)S(1)} all-to-all(bf16[128,8,384]{2,1,0:T(8,128)(2,1)} %bitcast.22), channel_id=1, replica_groups=mesh['fsdp'=16,'seq'=8] {'fsdp','seq'}, dimensions={0} | all-to-all | bytes 1572864 | tf_op jit(solution)/shard_map/all_to_all | solution.py:717
  141.8 2.4 %returned.1 = (bf16[128,768]{1,0:T(8,128)(2,1)}, f32[128,768]{1,0:T(8,128)S(1)}, bf16[128,192]{1,0:T(8,128)(2,1)S(1)}, bf16[128,192]{1,0:T(8,128)(2,1)S(1)}, bf1...) custom-call(s32[2]{0:T(128)S(1)} %copy-done.4, ...), custom_call_target="tpu_custom_call" | custom-call | flops 2300000000 | bytes 1048576 | tf_op jit(solution)/shard_map/returned/pallas_call | solution.py:488
  144.2 2.1 collective-permute-start.5
  146.4 0.7 collective-permute-start.6
  147.1 1.6 collective-permute-start.11
  148.7 0.3 collective-permute-done.4.g1_ref
  149.0 0.6 collective-permute-done.5.g2_ref
  149.5 0.6 collective-permute-done.6.g3_ref
  150.2 12.0 %attend_back.1 = (f32[4,128,768]{2,1,0:T(8,128)S(1)}, bf16[4,128,768]{2,1,0:T(8,128)(2,1)S(1)}, bf16[1024,576]{1,0:T(8,128)(2,1)S(1)}, f32[8,768]{1,0:T(8,128)S(1)}, f32[3,128,640]{2,1,0:T(8,128)S(1)}) custom-call(s32[2]{0:T(128)S(1)} %copy-done.4, bf16[128,192]{1,0:T(8,128)(2,1)S(1)} %get-tuple-element.76.g0_ref, ...), custom_call_target="tpu_custom_call" | custom-call | flops 13799999488 | bytes 1048576 | tf_op jit(solution)/shard_map/attend_back/pallas_call | solution.py:567
  162.2 6.6 %weight_terms.1 = bf16[768,1152]{1,0:T(8,128)(2,1)} custom-call(s32[2]{0:T(128)S(1)} %copy-done.4, bf16[1024,768]{1,0:T(8,128)(2,1)S(1)} %copy-done.9, bf16[1024,576]{1,0:T(8,128)(2,1)S(1)} %get-tuple-element.92.dq_ref, f32[8,768]{1,0:T(8,128)S(1)} %get-tuple-element.93.line_ref, f32[8,768]{1,0:T(8,128)S(1)} %get-tuple-element.94.dgain_ref, ...), custom_call_target="tpu_custom_call" | custom-call | flops 5750000128 | bytes 1048576 | tf_op jit(solution)/shard_map/weight_terms/pallas_call | solution.py:629
  168.9 3.7 %all-to-all-start.3 = ((bf16[16,48,1152]{2,1,0:T(8,128)(2,1)}), bf16[16,48,1152]{2,1,0:T(8,128)(2,1)S(1)}, u32[]{:S(2)}, u32[]{:S(2)}) async-start(bf16[16,48,1152]{2,1,0:T(8,128)(2,1)} %bitcast.10), calls=%async_computation.3 | async-start | bytes 3538944 | tf_op jit(solution)/shard_map/all_to_all | solution.py:717
  172.6 2.4 %collective-permute-start.7 = (bf16[4,128,768]{2,1,0:T(8,128)(2,1)S(1)}, bf16[4,128,768]{2,1,0:T(8,128)(2,1)S(1)}, u32[]{:S(2)}, u32[]{:S(2)}) collective-permute-start(bf16[4,128,768]{2,1,0:T(8,128)(2,1)S(1)} %get-tuple-element.85), channel_id=1, source_target_pairs={{0,1},{1,0},{2,3},{3,2},{4,5},{5,4},{6,7},{7,6},{8,9},{9,8},{10,11... | collective-permute-start | bytes 2359304 | tf_op jit(solution)/shard_map/ppermute | solution.py:721
  175.0 1.9 collective-permute-done.7.got_ref
  176.9 1.4 copy-done.6
  178.3 0.7 pair_sum.1
  179.0 0.7 copy-done.7
  179.8 1.1 collective-permute-start.8
  180.8 2.2 %collective-permute-start.9 = (bf16[128,768]{1,0:T(8,128)(2,1)S(1)}, bf16[128,768]{1,0:T(8,128)(2,1)S(1)}, u32[]{:S(2)}, u32[]{:S(2)}) collective-permute-start(bf16[128,768]{1,0:T(8,128)(2,1)S(1)} %get-tuple-element.88), channel_id=1, source_target_pairs={{0,4},{1,5},{2,6},{3,7},{4,0},{5,1},{6,2},{7,3},{8,12},{9,13},{10,... | collective-permute-start | bytes 589832 | tf_op jit(solution)/shard_map/ppermute | solution.py:713
  183.1 0.2 collective-permute-start.10
  183.2 11.6 %all-to-all-done.3 = bf16[16,48,1152]{2,1,0:T(8,128)(2,1)S(1)} async-done(((bf16[16,48,1152]{2,1,0:T(8,128)(2,1)}), bf16[16,48,1152]{2,1,0:T(8,128)(2,1)S(1)}, u32[]{:S(2)}, u32[]{:S(2)}) %all-to-all-start.3) | async-done | bytes 1769504 | tf_op jit(solution)/shard_map/all_to_all | solution.py:717
  194.8 1.0 middle_sums.1
  195.8 8.2 %all-to-all-start.4 = ((bf16[8,8,1152]{2,1,0:T(8,128)(2,1)}), bf16[8,8,1152]{2,1,0:T(8,128)(2,1)S(1)}, u32[]{:S(2)}, u32[]{:S(2)}) async-start(bf16[8,8,1152]{2,1,0:T(8,128)(2,1)} %bitcast.12), calls=%async_computation.4 | async-start | bytes 294912 | tf_op jit(solution)/shard_map/all_to_all | solution.py:717
  204.0 1.0 copy-done.8
  205.0 0.7 copy-done.14
  205.7 1.0 tokens_last.1
  206.8 2.7 %all-to-all-done.4 = bf16[8,8,1152]{2,1,0:T(8,128)(2,1)S(1)} async-done(((bf16[8,8,1152]{2,1,0:T(8,128)(2,1)}), bf16[8,8,1152]{2,1,0:T(8,128)(2,1)S(1)}, u32[]{:S(2)}, u32[]{:S(2)}) %all-to-all-start.4) | async-done | bytes 147488 | tf_op jit(solution)/shard_map/all_to_all | solution.py:717
  209.4 0.7 sums_last.1
  210.4 0.7 slice_reduce_fusion.2
  211.1 0.7 slice_reduce_fusion
  (54 shorter events, 0.5 us)
Async XLA Ops:
  7.2 51.4 %all-gather.2.cloned.1.call-start = ((), (), s32[]{:S(2)}) async-start(), calls=%async_computation.5 | async-start | bytes 1769472 | tf_op jit(solution)/shard_map/all_gather | solution.py:730
  11.5 11.5 %copy-start.20 = (s32[1,1024]{1,0:T(1,128)S(1)}, s32[1,1024]{1,0:T(1,128)}, u32[]{:S(2)}) copy-start(s32[1,1024]{1,0:T(1,128)} %param.15) | copy-start | bytes 12292
  11.5 41.4 %all-to-all-start = ((bf16[128,8,896]{2,1,0:T(8,128)(2,1)}), bf16[128,8,896]{2,1,0:T(8,128)(2,1)S(1)}, u32[]{:S(2)}, u32[]{:S(2)}) async-start(bf16[128,8,896]{2,1,0:T(8,128)(2,1)} %bitcast.20), calls=%async_computation | async-start | bytes 3670016 | tf_op jit(solution)/shard_map/all_to_all | solution.py:717
  52.8 1.2 copy-start.19
  58.6 18.1 %collective-permute-start.3 = (bf16[768,512]{1,0:T(8,128)(2,1)}, bf16[768,512]{1,0:T(8,128)(2,1)S(1)}, u32[]{:S(2)}, u32[]{:S(2)}) collective-permute-start(bf16[768,512]{1,0:T(8,128)(2,1)} %get-tuple-element.66.half_ref), channel_id=1, source_target_pairs={{0,1},{1,0},{2,3},{3,2},{4,5},{5,4},{6,7},{7,6},{8,9},{9,8},{10,11... | collective-permute-start | bytes 2359304 | tf_op jit(solution)/shard_map/ppermute | solution.py:721
  58.6 18.0 %copy-start.21 = (s32[128,1]{0,1:T(1,128)S(1)}, s32[128,1]{0,1:T(1,128)}, u32[]{:S(2)}) copy-start(s32[128,1]{0,1:T(1,128)} %param.16) | copy-start | bytes 1540
  58.6 20.2 %copy-start = (bf16[128,768]{1,0:T(8,128)(2,1)S(1)}, bf16[128,768]{1,0:T(8,128)(2,1)}, u32[]{:S(2)}) copy-start(bf16[128,768]{1,0:T(8,128)(2,1)} %x_ref.3) | copy-start | bytes 589828
  58.6 20.2 %copy-start.2 = (bf16[768,512]{1,0:T(8,128)(2,1)S(1)}, bf16[768,512]{1,0:T(8,128)(2,1)}, u32[]{:S(2)}) copy-start(bf16[768,512]{1,0:T(8,128)(2,1)} %get-tuple-element.66.half_ref) | copy-start | bytes 2359300
  58.6 20.2 %copy-start.3 = (bf16[128,768]{1,0:T(8,128)(2,1)S(1)}, bf16[128,768]{1,0:T(8,128)(2,1)}, u32[]{:S(2)}) copy-start(bf16[128,768]{1,0:T(8,128)(2,1)} %cot_ref.3) | copy-start | bytes 589828
  58.6 20.2 %copy-start.4 = (s32[2]{0:T(128)S(1)}, s32[2]{0:T(128)}, u32[]{:S(2)}) copy-start(s32[2]{0:T(128)} %pad_add_fusion.idx_ref) | copy-start | bytes 28
  58.6 20.2 %copy-start.13 = (f32[8,768]{1,0:T(8,128)S(1)}, f32[8,768]{1,0:T(8,128)}, u32[]{:S(2)}) copy-start(f32[8,768]{1,0:T(8,128)} %get-tuple-element.60.gain_ref) | copy-start | bytes 73732
  72.1 4.6 %collective-permute-start = (bf16[128,192]{1,0:T(8,128)(2,1)}, bf16[128,192]{1,0:T(8,128)(2,1)S(1)}, u32[]{:S(2)}, u32[]{:S(2)}) collective-permute-start(bf16[128,192]{1,0:T(8,128)(2,1)} %get-tuple-element.63), channel_id=1, source_target_pairs={{0,2},{1,3},{2,4},{3,5},{4,6},{5,7},{6,0},{7,1},{8,10},{9,11},{10,... | collective-permute-start | bytes 147464 | tf_op jit(solution)/shard_map/ppermute | solution.py:713
  73.3 4.9 %collective-permute-start.1 = (bf16[128,192]{1,0:T(8,128)(2,1)}, bf16[128,192]{1,0:T(8,128)(2,1)S(1)}, u32[]{:S(2)}, u32[]{:S(2)}) collective-permute-start(bf16[128,192]{1,0:T(8,128)(2,1)} %get-tuple-element.64), channel_id=1, source_target_pairs={{0,4},{1,5},{2,6},{3,7},{4,0},{5,1},{6,2},{7,3},{8,12},{9,13},{10,... | collective-permute-start | bytes 147464 | tf_op jit(solution)/shard_map/ppermute | solution.py:713
  74.6 4.2 %collective-permute-start.2 = (bf16[128,192]{1,0:T(8,128)(2,1)}, bf16[128,192]{1,0:T(8,128)(2,1)S(1)}, u32[]{:S(2)}, u32[]{:S(2)}) collective-permute-start(bf16[128,192]{1,0:T(8,128)(2,1)} %get-tuple-element.65), channel_id=1, source_target_pairs={{0,6},{1,7},{2,0},{3,1},{4,2},{5,3},{6,4},{7,5},{8,14},{9,15},{10,... | collective-permute-start | bytes 147464 | tf_op jit(solution)/shard_map/ppermute | solution.py:713
  78.8 0.8 copy-start.12
  141.8 8.4 %copy-start.1 = (bf16[1024,768]{1,0:T(8,128)(2,1)S(1)}, bf16[1024,768]{1,0:T(8,128)(2,1)}, u32[]{:S(2)}) copy-start(bf16[1024,768]{1,0:T(8,128)(2,1)} %all-gather.2.cloned.1.call-done.x_ref) | copy-start | bytes 4718596
  141.8 8.4 %copy-start.10 = (bf16[768,576]{1,0:T(8,128)(2,1)S(1)}, bf16[768,576]{1,0:T(8,128)(2,1)}, u32[]{:S(2)}) copy-start(bf16[768,576]{1,0:T(8,128)(2,1)} %get-tuple-element.59.wqkv_ref) | copy-start | bytes 2654212
  141.8 8.4 %copy-start.11 = (f32[3,128,640]{2,1,0:T(8,128)S(1)}, f32[3,128,640]{2,1,0:T(8,128)}, u32[]{:S(2)}) copy-start(f32[3,128,640]{2,1,0:T(8,128)} %get-tuple-element.61.band_ref) | copy-start | bytes 2949124
  141.8 8.4 %copy-start.15 = (bf16[1024,384]{1,0:T(8,128)(2,1)S(1)}, bf16[1024,384]{1,0:T(8,128)(2,1)}, u32[]{:S(2)}) copy-start(bf16[1024,384]{1,0:T(8,128)(2,1)} %get-tuple-element.80.qe_ref) | copy-start | bytes 2359300
  141.8 8.4 %copy-start.16 = (bf16[1024,384]{1,0:T(8,128)(2,1)S(1)}, bf16[1024,384]{1,0:T(8,128)(2,1)}, u32[]{:S(2)}) copy-start(bf16[1024,384]{1,0:T(8,128)(2,1)} %get-tuple-element.81.ke_ref) | copy-start | bytes 2359300
  141.8 8.4 %copy-start.17 = (bf16[1024,192]{1,0:T(8,128)(2,1)S(1)}, bf16[1024,192]{1,0:T(8,128)(2,1)}, u32[]{:S(2)}) copy-start(bf16[1024,192]{1,0:T(8,128)(2,1)} %get-tuple-element.82.v_ref) | copy-start | bytes 1179652
  141.8 8.4 %copy-start.18 = (f32[4,128,128]{2,1,0:T(8,128)S(1)}, f32[4,128,128]{2,1,0:T(8,128)}, u32[]{:S(2)}) copy-start(f32[4,128,128]{2,1,0:T(8,128)} %get-tuple-element.83.lse_ref) | copy-start | bytes 786436
  144.2 4.7 %collective-permute-start.4 = (bf16[128,192]{1,0:T(8,128)(2,1)S(1)}, bf16[128,192]{1,0:T(8,128)(2,1)S(1)}, u32[]{:S(2)}, u32[]{:S(2)}) collective-permute-start(bf16[128,192]{1,0:T(8,128)(2,1)S(1)} %get-tuple-element.77), channel_id=1, source_target_pairs={{0,2},{1,3},{2,4},{3,5},{4,6},{5,7},{6,0},{7,1},{8,10},{9,11},{10,... | collective-permute-start | bytes 147464 | tf_op jit(solution)/shard_map/ppermute | solution.py:713
  144.2 5.3 %collective-permute-start.5 = (bf16[128,192]{1,0:T(8,128)(2,1)S(1)}, bf16[128,192]{1,0:T(8,128)(2,1)S(1)}, u32[]{:S(2)}, u32[]{:S(2)}) collective-permute-start(bf16[128,192]{1,0:T(8,128)(2,1)S(1)} %get-tuple-element.78), channel_id=1, source_target_pairs={{0,4},{1,5},{2,6},{3,7},{4,0},{5,1},{6,2},{7,3},{8,12},{9,13},{10,... | collective-permute-start | bytes 147464 | tf_op jit(solution)/shard_map/ppermute | solution.py:713
  146.4 3.8 %collective-permute-start.6 = (bf16[128,192]{1,0:T(8,128)(2,1)S(1)}, bf16[128,192]{1,0:T(8,128)(2,1)S(1)}, u32[]{:S(2)}, u32[]{:S(2)}) collective-permute-start(bf16[128,192]{1,0:T(8,128)(2,1)S(1)} %get-tuple-element.79), channel_id=1, source_target_pairs={{0,6},{1,7},{2,0},{3,1},{4,2},{5,3},{6,4},{7,5},{8,14},{9,15},{10,... | collective-permute-start | bytes 147464 | tf_op jit(solution)/shard_map/ppermute | solution.py:713
  147.1 15.1 %collective-permute-start.11 = (bf16[768,512]{1,0:T(8,128)(2,1)S(1)}, bf16[768,512]{1,0:T(8,128)(2,1)S(1)}, u32[]{:S(2)}, u32[]{:S(2)}) collective-permute-start(bf16[768,512]{1,0:T(8,128)(2,1)S(1)} %get-tuple-element.97), channel_id=1, source_target_pairs={{0,1},{1,0},{2,3},{3,2},{4,5},{5,4},{6,7},{7,6},{8,9},{9,8},{10,11... | collective-permute-start | bytes 2359304 | tf_op jit(solution)/shard_map/ppermute | solution.py:721
  150.2 12.0 %copy-start.9 = (bf16[1024,768]{1,0:T(8,128)(2,1)S(1)}, bf16[1024,768]{1,0:T(8,128)(2,1)}, u32[]{:S(2)}) copy-start(bf16[1024,768]{1,0:T(8,128)(2,1)} %get-tuple-element.91.h_ref) | copy-start | bytes 4718596
  162.2 6.7 %copy-start.5 = (f32[4,128,768]{2,1,0:T(8,128)}, f32[4,128,768]{2,1,0:T(8,128)S(1)}, u32[]{:S(2)}) copy-start(f32[4,128,768]{2,1,0:T(8,128)S(1)} %get-tuple-element.84.own_ref) | copy-start | bytes 4718596
  168.9 26.0 %all-to-all-start.3 = ((bf16[16,48,1152]{2,1,0:T(8,128)(2,1)}), bf16[16,48,1152]{2,1,0:T(8,128)(2,1)S(1)}, u32[]{:S(2)}, u32[]{:S(2)}) async-start(bf16[16,48,1152]{2,1,0:T(8,128)(2,1)} %bitcast.10), calls=%async_computation.3 | async-start | bytes 3538944 | tf_op jit(solution)/shard_map/all_to_all | solution.py:717
  172.6 4.3 %collective-permute-start.7 = (bf16[4,128,768]{2,1,0:T(8,128)(2,1)S(1)}, bf16[4,128,768]{2,1,0:T(8,128)(2,1)S(1)}, u32[]{:S(2)}, u32[]{:S(2)}) collective-permute-start(bf16[4,128,768]{2,1,0:T(8,128)(2,1)S(1)} %get-tuple-element.85), channel_id=1, source_target_pairs={{0,1},{1,0},{2,3},{3,2},{4,5},{5,4},{6,7},{7,6},{8,9},{9,8},{10,11... | collective-permute-start | bytes 2359304 | tf_op jit(solution)/shard_map/ppermute | solution.py:721
  176.9 1.4 copy-start.6
  179.0 0.7 copy-start.7
  179.8 24.2 %collective-permute-start.8 = (bf16[128,768]{1,0:T(8,128)(2,1)S(1)}, bf16[128,768]{1,0:T(8,128)(2,1)S(1)}, u32[]{:S(2)}, u32[]{:S(2)}) collective-permute-start(bf16[128,768]{1,0:T(8,128)(2,1)S(1)} %get-tuple-element.87), channel_id=1, source_target_pairs={{0,2},{1,3},{2,4},{3,5},{4,6},{5,7},{6,0},{7,1},{8,10},{9,11},{10,... | collective-permute-start | bytes 589832 | tf_op jit(solution)/shard_map/ppermute | solution.py:713
  180.8 23.2 %collective-permute-start.9 = (bf16[128,768]{1,0:T(8,128)(2,1)S(1)}, bf16[128,768]{1,0:T(8,128)(2,1)S(1)}, u32[]{:S(2)}, u32[]{:S(2)}) collective-permute-start(bf16[128,768]{1,0:T(8,128)(2,1)S(1)} %get-tuple-element.88), channel_id=1, source_target_pairs={{0,4},{1,5},{2,6},{3,7},{4,0},{5,1},{6,2},{7,3},{8,12},{9,13},{10,... | collective-permute-start | bytes 589832 | tf_op jit(solution)/shard_map/ppermute | solution.py:713
  183.1 20.9 %collective-permute-start.10 = (bf16[128,768]{1,0:T(8,128)(2,1)S(1)}, bf16[128,768]{1,0:T(8,128)(2,1)S(1)}, u32[]{:S(2)}, u32[]{:S(2)}) collective-permute-start(bf16[128,768]{1,0:T(8,128)(2,1)S(1)} %get-tuple-element.89), channel_id=1, source_target_pairs={{0,6},{1,7},{2,0},{3,1},{4,2},{5,3},{6,4},{7,5},{8,14},{9,15},{10,... | collective-permute-start | bytes 589832 | tf_op jit(solution)/shard_map/ppermute | solution.py:713
  195.8 13.6 %all-to-all-start.4 = ((bf16[8,8,1152]{2,1,0:T(8,128)(2,1)}), bf16[8,8,1152]{2,1,0:T(8,128)(2,1)S(1)}, u32[]{:S(2)}, u32[]{:S(2)}) async-start(bf16[8,8,1152]{2,1,0:T(8,128)(2,1)} %bitcast.12), calls=%async_computation.4 | async-start | bytes 294912 | tf_op jit(solution)/shard_map/all_to_all | solution.py:717
  204.0 1.0 copy-start.8
  205.0 0.7 copy-start.14
Sparse Core Ops, SparseCore 0:
  9.7 45.0 all-gather.1

commit v3 on v2

--- a/solution.py
+++ b/solution.py
@@ -19,10 +19,12 @@
 COLS = GROUP * HD
 BAND = 5 * TOK
 HALF = WIDTH // 2
-PACK = 896
+PACK = 2432
+MORE = 896
 SENT = 640
 LATE = 512
-FF_TILE = 512
+FF_TILE = 768
+PROJ = 512
 eps = 1e-06
 bucket_edges = (12, 16, 23, 32, 46, 64, 91)
 BOTH = ("fsdp", "seq")
@@ -95,15 +97,17 @@
     )
 
 
-def load_rows(ref, start, stride):
+def load_rows(ref, start, stride, count=128):
     return jnp.concatenate(
-        [ref[j, pl.ds(start, 128, stride=stride), :] for j in range(ref.shape[0])], axis=1
+        [ref[j, pl.ds(start, count, stride=stride), :] for j in range(ref.shape[0])], axis=1
     )
 
 
-def store_rows(ref, start, stride, value):
+def store_rows(ref, start, stride, value, first=0):
     for j in range(value.shape[1] // 128):
-        ref[j, pl.ds(start, 128, stride=stride), :] = value[:, 128 * j : 128 * j + 128]
+        ref[first + j, pl.ds(start, value.shape[0], stride=stride), :] = value[
+            :, 128 * j : 128 * j + 128
+        ]
 
 
 def whole(ref, first, last):
@@ -120,67 +124,112 @@
 
 
 def pack_kernel(q_ref, k_ref, v_ref, o_ref, r_ref, small_ref, out_ref):
-    zero = jnp.zeros((2, 576), f32)
     q, k, v, o, r = (ref[...].astype(f32) for ref in (q_ref, k_ref, v_ref, o_ref, r_ref))
-    small = small_ref[...].astype(f32)
-    blocks = []
+    six = jnp.concatenate([q, k, v, r], axis=1)
+    row6 = jnp.concatenate([o[0:1], o[1:2], o[2:3], small_ref[...].astype(f32)], axis=1)
+    row7 = jnp.concatenate([o[3:4], o[4:5], o[5:6], jnp.zeros((1, 128), f32)], axis=1)
+    block = jnp.concatenate([six, row6, row7] * 2, axis=0).astype(bf16)
+    for f in range(8):
+        out_ref[16 * f : 16 * f + 16, :] = block
+
+
+def pack_weights(w_query, w_key, w_value, w_output, w_router, small):
+    return call(pack_kernel, [sds(128, PACK)], [vmem] * 6, name="pack_weights", mib=56)(
+        w_query, w_key, w_value, w_output, w_router, small
+    )[0]
+
+
+def split_kernel(got_ref, heads_ref, more_ref, gf_ref, qf_ref, mf_ref):
+    fill(gf_ref, got_ref)
+    small = gf_ref[18, pl.ds(6, 16, stride=8), :]
+    for r in range(6):
+        for j in range(18):
+            qf_ref[j, pl.ds(r, 16, stride=6), :] = gf_ref[j, pl.ds(r, 16, stride=8), :]
+        mf_ref[6, pl.ds(r, 16, stride=6), :] = gf_ref[18, pl.ds(r, 16, stride=8), :]
+        for j in range(6):
+            mf_ref[j, pl.ds(r, 16, stride=6), :] = gf_ref[
+                6 * (r % 3) + j, pl.ds(6 + r // 3, 16, stride=8), :
+            ]
+        third_lane = small[:, 12 + r : 13 + r] if r < 3 else jnp.zeros((16, 1), f32)
+        cols = [small[:, r : r + 1], small[:, 6 + r : 7 + r], third_lane, jnp.zeros((16, 125), f32)]
+        qf_ref[18, pl.ds(r, 16, stride=6), :] = jnp.concatenate(cols, axis=1)
+    q, k, v = (whole(qf_ref, 6 * m, 6 * m + 6) for m in range(3))
+    small = qf_ref[18][:, :64]
     for y in range(4):
         at = slice(COLS * y, COLS * y + COLS)
-        three = jnp.concatenate([q[:, at], k[:, at], v[:, at]], axis=1)
-        for c in range(2):
-            left = o[:, HALF * c : HALF * c + 320]
-            right = [o[i : i + 1, HALF * c + 320 : HALF * c + HALF] for i in range(6)]
-            routed = [r[i : i + 1, 64 * c : 64 * c + 64] for i in range(6)]
-            row6 = jnp.concatenate(right + routed + [small], axis=1)
-            six = jnp.concatenate([three, left], axis=1)
-            blocks.append(jnp.concatenate([six, row6, jnp.zeros((1, PACK), f32)], axis=0))
-    block = jnp.concatenate(blocks, axis=0).astype(bf16)
-    for f in range(16):
-        out_ref[64 * f : 64 * f + 64, :] = block
-
-
-def pack_weights(w_query, w_key, w_value, w_output, w_router, small):
-    return call(pack_kernel, [sds(LEN, PACK)], [vmem] * 6, name="pack_weights", mib=56)(
-        w_query, w_key, w_value, w_output, w_router, small
-    )[0]
-
-
-def unpack_kernel(
-    idx_ref, pack_ref, wqkv_ref, half_ref, gain_ref, band_ref, pf_ref, wf_ref, tail_ref
-):
-    y = idx_ref[0]
+        rows = jnp.concatenate([q[:, at], k[:, at], v[:, at], small], axis=1).astype(bf16)
+        heads_ref[192 * y : 192 * y + 96, :] = rows
+        heads_ref[192 * y + 96 : 192 * y + 192, :] = rows
+    more_ref[...] = whole(mf_ref, 0, 7).astype(bf16)
+
+
+def split_weights(got):
+    return call(
+        split_kernel,
+        [sds(WIDTH, SENT), sds(96, MORE)],
+        [vmem],
+        [
+            pltpu.VMEM((19, 128, 128), f32),
+            pltpu.VMEM((19, 96, 128), f32),
+            pltpu.VMEM((7, 96, 128), f32),
+        ],
+        name="split_weights",
+        mib=56,
+    )(got)
+
+
+def output_kernel(idx_ref, *refs):
+    blocks, refs = refs[:8], refs[8:]
+    wo_ref, router_ref, src_ref, dst_ref = refs
+    y, c = idx_ref[0], idx_ref[1]
+    for side in range(2):
+        for k in range(4):
+            place = 2 * lax.rem(y + 4 - k, 4) + (c if side == 0 else 1 - c)
+            n = 4 * side + k
+            for j in range(7):
+                src_ref[n, j] = blocks[n][:, 128 * j : 128 * j + 128].astype(f32)
+                for r in range(6):
+                    dst_ref[j, pl.ds(place * 6 + r, 16, stride=48), :] = src_ref[
+                        n, j, pl.ds(r, 16, stride=6), :
+                    ]
+    wo_ref[...] = whole(dst_ref, 0, 6).astype(bf16)
+    router_ref[...] = dst_ref[6].astype(bf16)
+
+
+def output_weights(idx, blocks):
+    return call(
+        output_kernel,
+        [sds(WIDTH, WIDTH), sds(WIDTH, 128)],
+        [smem] + [vmem] * 8,
+        [pltpu.VMEM((8, 7, 96, 128), f32), pltpu.VMEM((7, WIDTH, 128), f32)],
+        name="output_weights",
+        mib=24,
+        us=3,
+    )(idx, *blocks)
+
+
+def unpack(y, pack_ref, wqkv_ref, gain_ref, band_ref, pf_ref, wf_ref):
     fill(pf_ref, pack_ref)
-    for r in range(6):
-        store_rows(wf_ref, r, 6, load_rows(pf_ref, r, 8))
-    row6 = load_rows(pf_ref, 6, 8)
-    for r in range(6):
-        tail = [row6[:, 64 * r : 64 * r + 64], row6[:, HALF + 64 * r : HALF + 64 * r + 64]]
-        tail_ref[pl.ds(r, 128, stride=6), :] = jnp.concatenate(tail, axis=1)
+    for s in range(8):
+        for r in range(6):
+            rows = load_rows(pf_ref, 96 * s + r, 6, 16)
+            store_rows(wf_ref, 6 * s + r, 48, rows)
     wqkv_ref[...] = whole(wf_ref, 0, 5)[:, : 3 * COLS].astype(bf16)
-    left = whole(wf_ref, 4, 7)[:, 64:]
-    blank = jnp.zeros((WIDTH, 64), f32)
-    half_ref[...] = jnp.concatenate([left, tail_ref[...], blank], axis=1).astype(bf16)
-    small = row6[:, WIDTH:].astype(bf16)
-
-    lanes = iota((128, WIDTH), 1)
-    rows = iota((128, WIDTH), 0)
-    own = sixth(lanes) == rows
-    within = lanes - 6 * sixth(lanes)
-    gains = []
-    for base in (0, 6):
-        spread = mm(small, (rows == within + base).astype(bf16))
-        gains.append(jnp.sum(jnp.where(own, spread, 0.0), axis=0, keepdims=True))
-    gain_ref[...] = jnp.concatenate([gains[0], gains[1], jnp.zeros((6, WIDTH), f32)], axis=0)
-    lanes = iota((128, 384), 1)
-    rows = iota((128, 384), 0)
-    spread = mm(small, (rows == lanes - 3 * third(lanes) + 12).astype(bf16))
-    table = jnp.sum(jnp.where(third(lanes) == rows, spread, 0.0), axis=0, keepdims=True)
-    table = jnp.broadcast_to(table, (8, 384)).astype(bf16)
-    ids = bucket_of(iota((384, 512), 1) - 255)
-    entry = iota((384, 512), 0)
+    small = wf_ref[4].T
+    gain_ref[...] = jnp.concatenate([small[64:66], jnp.zeros((6, WIDTH), f32)], axis=0)
+    lanes = iota((8, WIDTH), 1)
+    group = sixth(lanes)
+    entry = 3 * group + lanes - 6 * group
+    mine = (lanes - 6 * group < 3) & ((entry >> 5) == 3 * y + iota((8, WIDTH), 0))
+    table = jnp.where(mine, small[66:67], 0.0).astype(bf16)
+    rows = iota((WIDTH, 128), 0)
+    group = sixth(rows)
+    entry = 3 * group + rows - 6 * group
+    table = mm(table, ((entry & 31) == iota((WIDTH, 128), 1)).astype(bf16)).astype(bf16)
+    hot = bucket_of(iota((128, 512), 1) - 255) == iota((128, 512), 0)
+    lines = mm(table, hot.astype(bf16))
     for h in range(GROUP):
-        hot = (entry == ids + 32 * (3 * y + h)).astype(bf16)
-        line = mm(table, hot)[:1]
+        line = lines[h : h + 1]
         wide = pltpu.roll(
             jnp.broadcast_to(line, (TOK, 512)), 385, 1, stride=1, stride_axis=0
         )
@@ -189,26 +238,6 @@
         band_ref[h, :, 4 * TOK :] = jnp.broadcast_to(line[:, 511:], (TOK, TOK))
 
 
-def unpack_weights(idx, pack):
-    outs = [
-        sds(WIDTH, 3 * COLS), sds(WIDTH, 512), sds(8, WIDTH, dtype=f32),
-        sds(GROUP, TOK, BAND, dtype=f32),
-    ]
-    return call(
-        unpack_kernel,
-        outs,
-        [smem, vmem],
-        [
-            pltpu.VMEM((7, LEN, 128), f32),
-            pltpu.VMEM((7, WIDTH, 128), f32),
-            pltpu.VMEM((WIDTH, 128), f32),
-        ],
-        name="unpack_weights",
-        mib=56,
-        us=4,
-    )(idx, pack)
-
-
 def banded(band_ref, h, pq):
     parts = []
     for j in range(8):
@@ -218,36 +247,58 @@
 
 
 def attend_kernel(
-    idx_ref, x_ref, seg_ref, wqkv_ref, gain_ref, band_ref,
-    o0_ref, o1_ref, o2_ref, o3_ref, h_ref, qe_ref, ke_ref, v_ref, lse_ref,
-    os_ref,
+    idx_ref, pack_ref, seg_ref, *refs
 ):
+    blocks, refs = refs[:8], refs[8:]
+    o0_ref, o1_ref, o2_ref, o3_ref, gain_ref, lse_ref = refs[:6]
+    saved, refs = refs[6:12], refs[12:]
+    wqkv_ref, band_ref, x_ref, qe_ref, ke_ref, v_ref = refs[:6]
+    pf_ref, wf_ref, os_ref, in_sem, out_sem = refs[6:]
     y, c = idx_ref[0], idx_ref[1]
+    loads = []
+    for side in range(2):
+        for k in range(4):
+            place = 2 * lax.rem(y + 4 - k, 4) + (c if side == 0 else 1 - c)
+            at = pl.ds(pl.multiple_of(place * TOK, TOK), TOK)
+            n = 4 * side + k
+            loads.append(pltpu.make_async_copy(blocks[n], x_ref.at[at, :], in_sem.at[n]))
+    for load in loads:
+        load.start()
+    stores = [
+        pltpu.make_async_copy(src, dst, out_sem.at[n])
+        for n, (src, dst) in enumerate(zip(refs[:6], saved))
+    ]
+    unpack(y, pack_ref, wqkv_ref, gain_ref, band_ref, pf_ref, wf_ref)
+    for store in stores[:2]:
+        store.start()
+    for load in loads:
+        load.wait()
+    stores[2].start()
     gain = gain_ref[:1, :]
 
     def project(i, _):
-        at = pl.ds(pl.multiple_of(i * TOK, TOK), TOK)
+        at = pl.ds(pl.multiple_of(i * PROJ, PROJ), PROJ)
         x = x_ref[at, :].astype(f32)
         hb = (x * lax.rsqrt(jnp.mean(x * x, axis=-1, keepdims=True) + eps) * gain).astype(bf16)
-        h_ref[at, :] = hb
-        qkv = mm(hb, wqkv_ref[...])
         doc = seg_ref[at, :]
-        lane = iota((TOK, HD), 1)
+        lane = iota((PROJ, HD), 1)
         same = lane == doc
-        q_mark = jnp.where(same, -1e30, 0.0)
-        k_mark = jnp.where((lane < 3) & jnp.logical_not(same), 1.0, 0.0)
+        q_mark = jnp.where(same, -1e30, 0.0).astype(bf16)
+        k_mark = jnp.where((lane < 3) & jnp.logical_not(same), 1.0, 0.0).astype(bf16)
+        q = (mm(hb, wqkv_ref[:, :COLS]).astype(bf16).astype(f32) * 0.125).astype(bf16)
+        k = mm(hb, wqkv_ref[:, COLS : 2 * COLS]).astype(bf16)
+        v_ref[at, :] = mm(hb, wqkv_ref[:, 2 * COLS :]).astype(bf16)
         q_parts, k_parts = [], []
         for h in range(GROUP):
-            q = qkv[:, HD * h : HD * h + HD]
-            k = qkv[:, COLS + HD * h : COLS + HD * h + HD]
-            q_parts += [q.astype(bf16).astype(f32) * 0.125, q_mark]
-            k_parts += [k, k_mark]
-        qe_ref[at, :] = jnp.concatenate(q_parts, axis=1).astype(bf16)
-        ke_ref[at, :] = jnp.concatenate(k_parts, axis=1).astype(bf16)
-        v_ref[at, :] = qkv[:, 2 * COLS :].astype(bf16)
+            q_parts += [q[:, HD * h : HD * h + HD], q_mark]
+            k_parts += [k[:, HD * h : HD * h + HD], k_mark]
+        qe_ref[at, :] = jnp.concatenate(q_parts, axis=1)
+        ke_ref[at, :] = jnp.concatenate(k_parts, axis=1)
         return 0
 
-    lax.fori_loop(0, 8, project, 0)
+    lax.fori_loop(0, LEN // PROJ, project, 0)
+    for store in stores[3:]:
+        store.start()
 
     def attend(k, _):
         yq = lax.rem(y + k, 4)
@@ -269,45 +320,48 @@
         lse_ref[yq] = lse_all
         return 0
 
-    lax.fori_loop(0, 4, attend, 0)
+    lax.fori_loop(0, 4, attend, 0, unroll=2)
     o0_ref[...] = os_ref[0]
     o1_ref[...] = os_ref[1]
     o2_ref[...] = os_ref[2]
     o3_ref[...] = os_ref[3]
-
-
-def attend(idx, x_all, seg_col, wqkv, gains, band):
-    outs = [sds(TOK, COLS)] * 4 + [
+    for store in stores:
+        store.wait()
+
+
+def attend(idx, pack, seg_col, blocks):
+    saved = [
+        sds(WIDTH, 3 * COLS), sds(GROUP, TOK, BAND, dtype=f32),
         sds(LEN, WIDTH), sds(LEN, 384), sds(LEN, 384), sds(LEN, COLS),
-        sds(4, TOK, 128, dtype=f32),
     ]
-    return call(
+    outs = [sds(TOK, COLS)] * 4 + [sds(8, WIDTH, dtype=f32), sds(4, TOK, 128, dtype=f32)]
+    place = pl.BlockSpec(memory_space=pl.ANY)
+    return pl.pallas_call(
         attend_kernel,
-        outs,
-        [smem] + [vmem] * 5,
-        [pltpu.VMEM((4, TOK, COLS), bf16)],
+        out_shape=outs + saved,
+        in_specs=[smem, vmem, vmem] + [place] * 8,
+        out_specs=[vmem] * 6 + [place] * 6,
+        scratch_shapes=[pltpu.VMEM(v.shape, v.dtype) for v in saved]
+        + [
+            pltpu.VMEM((5, WIDTH, 128), f32),
+            pltpu.VMEM((5, WIDTH, 128), f32),
+            pltpu.VMEM((4, TOK, COLS), bf16),
+            pltpu.SemaphoreType.DMA((8,)),
+            pltpu.SemaphoreType.DMA((6,)),
+        ],
+        compiler_params=params(56),
+        cost_estimate=cost(14),
         name="attend",
-        mib=56,
-        us=12,
-    )(idx, x_all, seg_col, wqkv, gains, band)
+    )(idx, pack, seg_col, *blocks)
 
 
 def dispatch_kernel(
-    idx_ref, x_ref, o0_ref, o1_ref, o2_ref, o3_ref, half_ref, rest_ref, gain_ref,
+    idx_ref, x_ref, o0_ref, o1_ref, o2_ref, o3_ref, wo_ref, router_ref, gain_ref,
     route_ref, cot_ref,
-    x1_ref, h2_ref, prob_ref, hot_ref, send_ref, wo_ref, router_ref,
+    x1_ref, h2_ref, prob_ref, hot_ref, send_ref,
     sf_ref,
 ):
-    y, c = idx_ref[0], idx_ref[1]
-    wo_ref[:, pl.ds(pl.multiple_of(c * HALF, 128), HALF)] = half_ref[:, :HALF]
-    wo_ref[:, pl.ds(pl.multiple_of((1 - c) * HALF, 128), HALF)] = rest_ref[:, :HALF]
-    here = half_ref[:, HALF : HALF + 128].astype(f32)[:, :64]
-    there = rest_ref[:, HALF : HALF + 128].astype(f32)[:, :64]
-    router_ref[...] = jnp.where(
-        c == 0,
-        jnp.concatenate([here, there], axis=1),
-        jnp.concatenate([there, here], axis=1),
-    ).astype(bf16)
+    y = idx_ref[0]
     x1 = x_ref[...].astype(f32)
     for k, o_ref in enumerate((o0_ref, o1_ref, o2_ref, o3_ref)):
         src = lax.rem(y + 4 - k, 4)
@@ -337,10 +391,10 @@
     send_ref[...] = whole(sf_ref, 0, 3).astype(bf16)
 
 
-def dispatch(idx, x_own, o_parts, half, rest, gains, route_col, cot):
+def dispatch(idx, x_own, o_parts, wo, router, gains, route_col, cot):
     outs = [
         sds(TOK, WIDTH, dtype=f32), sds(TOK, WIDTH), sds(TOK, 128, dtype=f32),
-        sds(2, TOK, 128), sds(LEN, HALF), sds(WIDTH, WIDTH), sds(WIDTH, 128),
+        sds(2, TOK, 128), sds(LEN, HALF),
     ]
     return call(
         dispatch_kernel,
@@ -349,67 +403,83 @@
         [pltpu.VMEM((3, LEN, 128), f32)],
         name="dispatch",
         mib=10,
-    )(idx, x_own, *o_parts, half, rest, gains, route_col, cot)
+    )(idx, x_own, *o_parts, wo, router, gains, route_col, cot)
 
 
 def expert_kernel(
-    recv_ref, wi_ref, wo_ref, ret_ref, gi_ref, go_ref, rf_ref, x_ref, xt_ref, g_ref, eo_ref, gx_ref
+    recv_ref, wi_hbm, wo_hbm, ret_ref, gi_hbm, go_hbm,
+    rf_ref, x_ref, xt_ref, g_ref, eo_ref, gx_ref, wi_ref, wo_ref, gi_ref, go_ref, in_sem, out_sem,
 ):
-    step = pl.program_id(0)
-
-    @pl.when(step == 0)
-    def _():
-        fill(rf_ref, recv_ref)
-        for kind, dst in enumerate((x_ref, g_ref)):
-            for s in range(2):
-                for half in range(2):
-                    dst[TOK * s : TOK * s + TOK, HALF * half : HALF * half + HALF] = load_rows(
-                        rf_ref, kind * 4 + s * 2 + half, 8
-                    ).astype(bf16)
-        xt_ref[...] = x_ref[...].T
-        eo_ref[...] = jnp.zeros_like(eo_ref)
-        gx_ref[...] = jnp.zeros_like(gx_ref)
-
-    wi = wi_ref[...]
-    wo = wo_ref[...]
-    g = g_ref[...]
-    a = mm(x_ref[...], wi)
-    cc = 0.7978845608028654
-    sq = a * a
-    t = jnp.tanh(cc * (a + 0.044715 * (sq * a)))
-    u = (0.5 * a * (1.0 + t)).astype(bf16)
-    slope = 0.5 * (1.0 + t) + (0.5 * cc) * a * (1.0 - t * t) * (1.0 + 0.134145 * sq)
-    eo_ref[...] += mm(u, wo)
-    ga = (mm_nt(g, wo) * slope).astype(bf16)
-    go_ref[...] = mm_tn(u, g).astype(bf16)
-    gi_ref[...] = mm(xt_ref[...], ga).astype(bf16)
-    gx_ref[...] += mm_nt(ga, wi)
-
-    @pl.when(step == FF // FF_TILE - 1)
-    def _():
-        for kind, src in enumerate((eo_ref, gx_ref)):
-            for s in range(2):
-                for half in range(2):
-                    part = src[TOK * s : TOK * s + TOK, HALF * half : HALF * half + HALF]
-                    store_rows(rf_ref, kind * 4 + s * 2 + half, 8, part)
-        ret_ref[...] = whole(rf_ref, 0, 3).astype(bf16)
+    tiles = FF // FF_TILE
+    loads, stores = [], []
+    for i in range(tiles):
+        at = pl.ds(i * FF_TILE, FF_TILE)
+        loads.append(
+            (
+                pltpu.make_async_copy(wi_hbm.at[0, :, at], wi_ref.at[i], in_sem.at[0, i]),
+                pltpu.make_async_copy(wo_hbm.at[0, at, :], wo_ref.at[i], in_sem.at[1, i]),
+            )
+        )
+        stores.append(
+            (
+                pltpu.make_async_copy(gi_ref.at[i], gi_hbm.at[0, :, at], out_sem.at[0, i]),
+                pltpu.make_async_copy(go_ref.at[i], go_hbm.at[0, at, :], out_sem.at[1, i]),
+            )
+        )
+    for pair in loads:
+        for load in pair:
+            load.start()
+    fill(rf_ref, recv_ref)
+    for kind, dst in enumerate((x_ref, g_ref)):
+        for s in range(2):
+            for half in range(2):
+                dst[TOK * s : TOK * s + TOK, HALF * half : HALF * half + HALF] = load_rows(
+                    rf_ref, kind * 4 + s * 2 + half, 8
+                ).astype(bf16)
+    xt_ref[...] = x_ref[...].T
+    for i in range(tiles):
+        for load in loads[i]:
+            load.wait()
+        wi = wi_ref[i]
+        wo = wo_ref[i]
+        g = g_ref[...]
+        a = mm(x_ref[...], wi)
+        gu = mm_nt(g, wo)
+        cc = 0.7978845608028654
+        sq = a * a
+        t = jnp.tanh(cc * (a + 0.044715 * (sq * a)))
+        u = (0.5 * a * (1.0 + t)).astype(bf16)
+        slope = 0.5 * (1.0 + t) + (0.5 * cc) * a * (1.0 - t * t) * (1.0 + 0.134145 * sq)
+        ga = (gu * slope).astype(bf16)
+        go_ref[i] = mm_tn(u, g).astype(bf16)
+        gi_ref[i] = mm(xt_ref[...], ga).astype(bf16)
+        for store in stores[i]:
+            store.start()
+        if i == 0:
+            eo_ref[...] = mm(u, wo)
+            gx_ref[...] = mm_nt(ga, wi)
+        else:
+            eo_ref[...] += mm(u, wo)
+            gx_ref[...] += mm_nt(ga, wi)
+    for kind, src in enumerate((eo_ref, gx_ref)):
+        for s in range(2):
+            for half in range(2):
+                part = src[TOK * s : TOK * s + TOK, HALF * half : HALF * half + HALF]
+                store_rows(rf_ref, kind * 4 + s * 2 + half, 8, part)
+    ret_ref[...] = whole(rf_ref, 0, 3).astype(bf16)
+    for pair in stores:
+        for store in pair:
+            store.wait()
 
 
 def experts(recv, w_inner, w_outer):
+    place = pl.BlockSpec(memory_space=pl.ANY)
+    tiles = FF // FF_TILE
     return pl.pallas_call(
         expert_kernel,
-        grid=(FF // FF_TILE,),
         out_shape=[sds(LEN, HALF), sds(1, WIDTH, FF), sds(1, FF, WIDTH)],
-        in_specs=[
-            pl.BlockSpec((LEN, HALF), lambda i: (0, 0)),
-            pl.BlockSpec((None, WIDTH, FF_TILE), lambda i: (0, 0, i)),
-            pl.BlockSpec((None, FF_TILE, WIDTH), lambda i: (0, i, 0)),
-        ],
-        out_specs=[
-            pl.BlockSpec((LEN, HALF), lambda i: (0, 0)),
-            pl.BlockSpec((None, WIDTH, FF_TILE), lambda i: (0, 0, i)),
-            pl.BlockSpec((None, FF_TILE, WIDTH), lambda i: (0, i, 0)),
-        ],
+        in_specs=[vmem, place, place],
+        out_specs=[vmem, place, place],
         scratch_shapes=[
             pltpu.VMEM((3, LEN, 128), f32),
             pltpu.VMEM((2 * TOK, WIDTH), bf16),
@@ -417,9 +487,15 @@
             pltpu.VMEM((2 * TOK, WIDTH), bf16),
             pltpu.VMEM((2 * TOK, WIDTH), f32),
             pltpu.VMEM((2 * TOK, WIDTH), f32),
+            pltpu.VMEM((tiles, WIDTH, FF_TILE), bf16),
+            pltpu.VMEM((tiles, FF_TILE, WIDTH), bf16),
+            pltpu.VMEM((tiles, WIDTH, FF_TILE), bf16),
+            pltpu.VMEM((tiles, FF_TILE, WIDTH), bf16),
+            pltpu.SemaphoreType.DMA((2, tiles)),
+            pltpu.SemaphoreType.DMA((2, tiles)),
         ],
         compiler_params=params(56),
-        cost_estimate=cost(14),
+        cost_estimate=cost(12),
         name="experts",
     )(recv, w_inner, w_outer)
 
@@ -497,8 +573,8 @@
 
 def backward_kernel(
     idx_ref, g0_ref, g1_ref, g2_ref, g3_ref, x_ref, wqkv_ref, qe_ref, ke_ref, v_ref,
-    band_ref, lse_ref,
-    own_ref, other_ref, dq_ref, line_ref, acc_ref,
+    band_ref, lse_ref, gain_ref,
+    own_ref, other_ref, dq_ref, line_ref, acc_ref, h_ref,
     gs_ref, gk_ref, gv_ref,
 ):
     y, c = idx_ref[0], idx_ref[1]
@@ -538,36 +614,36 @@
     lax.fori_loop(0, 4, block, 0)
     dq_ref[:, COLS : 2 * COLS] = gk_ref[...].T.astype(bf16)
     dq_ref[:, 2 * COLS :] = gv_ref[...].T.astype(bf16)
-    line_ref[...] = jnp.zeros_like(line_ref)
-
-    def spread(yq, _):
-        lines = jnp.zeros((1, WIDTH), f32)
-        for side in range(2):
+    lines = jnp.zeros((1, WIDTH), f32)
+    for side in range(2):
+        rows = []
+        for yq in range(4):
             pq = 2 * yq + (c if side == 0 else 1 - c)
-            at = pl.ds(pl.multiple_of(pq * TOK, TOK), TOK)
-            d = mm_nt(dq_ref[at, :], wqkv_ref[...])
-            x = x_ref[at, :].astype(f32)
-            r1 = lax.rsqrt(jnp.mean(x * x, axis=-1, keepdims=True) + eps)
-            lines = lines + jnp.sum(d * (x * r1), axis=0, keepdims=True)
+            rows.append(pl.ds(pl.multiple_of(pq * TOK, TOK), TOK))
+        d = mm_nt(jnp.concatenate([dq_ref[at, :] for at in rows], axis=0), wqkv_ref[...])
+        x = jnp.concatenate([x_ref[at, :] for at in rows], axis=0).astype(f32)
+        scaled = x * lax.rsqrt(jnp.mean(x * x, axis=-1, keepdims=True) + eps)
+        lines = lines + jnp.sum(d * scaled, axis=0, keepdims=True)
+        hb = (scaled * gain_ref[:1, :]).astype(bf16)
+        for yq in range(4):
+            part = slice(TOK * yq, TOK * yq + TOK)
+            h_ref[rows[yq], :] = hb[part]
             if side == 0:
-                own_ref[yq] = d
+                own_ref[yq] = d[part]
             else:
-                other_ref[yq] = d.astype(bf16)
-        line_ref[...] += jnp.broadcast_to(lines, (8, WIDTH))
-        return 0
-
-    lax.fori_loop(0, 4, spread, 0)
-
-
-def attend_back(idx, go_parts, x_all, wqkv, qe, ke, v, band, lse):
+                other_ref[yq] = d[part].astype(bf16)
+    line_ref[...] = jnp.broadcast_to(lines, (8, WIDTH))
+
+
+def attend_back(idx, go_parts, x_all, wqkv, qe, ke, v, band, lse, gains):
     outs = [
         sds(4, TOK, WIDTH, dtype=f32), sds(4, TOK, WIDTH), sds(LEN, 3 * COLS),
-        sds(8, WIDTH, dtype=f32), sds(GROUP, TOK, BAND, dtype=f32),
+        sds(8, WIDTH, dtype=f32), sds(GROUP, TOK, BAND, dtype=f32), sds(LEN, WIDTH),
     ]
     return call(
         backward_kernel,
         outs,
-        [smem] + [vmem] * 11,
+        [smem] + [vmem] * 12,
         [
             pltpu.VMEM((4, TOK, COLS), bf16),
             pltpu.VMEM((COLS, LEN), f32),
@@ -576,7 +652,7 @@
         name="attend_back",
         mib=24,
         us=12,
-    )(idx, *go_parts, x_all, wqkv, qe, ke, v, band, lse)
+    )(idx, *go_parts, x_all, wqkv, qe, ke, v, band, lse, gains)
 
 
 def terms_kernel(
@@ -586,26 +662,34 @@
     ids = bucket_of(iota((512, 128), 0) - 255)
     flat = iota((512, 128), 1)
     turn = (iota((TOK, TOK), 0) + iota((TOK, TOK), 1) == TOK - 1).astype(f32)
-    table = jnp.zeros((8, 128), f32)
-    flat_lane = iota((8, 128), 1)
+    near = jnp.concatenate([acc_ref[h, :, TOK : 4 * TOK] for h in range(GROUP)], axis=1)
+    near = exact(turn, near)
+    blank = jnp.zeros((TOK, TOK), f32)
+    lane = iota((1, 128), 1)
+    diags, sides = [], []
     for h in range(GROUP):
-        near = exact(turn, acc_ref[h, :, TOK : 4 * TOK])
-        near = jnp.concatenate([near, jnp.zeros((TOK, TOK), f32)], axis=1)
-        near = pltpu.roll(near, 0, 1, stride=1, stride_axis=0)
-        diag = jnp.broadcast_to(jnp.sum(near, axis=0, keepdims=True), (8, 512))
-        table = table + exact(diag, (flat == ids + 32 * h).astype(f32))
+        part = jnp.concatenate([near[:, 3 * TOK * h : 3 * TOK * h + 3 * TOK], blank], axis=1)
+        part = pltpu.roll(part, 0, 1, stride=1, stride_axis=0)
+        diags.append(jnp.sum(part, axis=0, keepdims=True))
         low = jnp.sum(acc_ref[h, :, :TOK])
         high = jnp.sum(acc_ref[h, :, 4 * TOK :])
-        table = table + jnp.where(flat_lane == 32 * h + 15, low, 0.0)
-        table = table + jnp.where(flat_lane == 32 * h + 31, high, 0.0)
+        sides.append(jnp.where(lane == 15, low, 0.0) + jnp.where(lane == 31, high, 0.0))
+    diags = jnp.concatenate(diags + [jnp.zeros((5, 512), f32)], axis=0)
+    sides = jnp.concatenate(sides + [jnp.zeros((5, 128), f32)], axis=0)
+    table = exact(diags, (flat == ids).astype(f32)) + sides
     lanes = iota((128, WIDTH), 1)
-    entry = iota((128, WIDTH), 0)
     group = sixth(lanes)
-    within = lanes - 6 * group
-    place = (within < 3) & (entry + 96 * y == 3 * group + within) & (entry < 96)
-    table = exact(table, place.astype(f32))
+    entry = 3 * group + lanes - 6 * group
+    place = ((entry & 31) == iota((128, WIDTH), 0)).astype(f32)
+    lanes = iota((8, WIDTH), 1)
+    group = sixth(lanes)
+    entry = 3 * group + lanes - 6 * group
+    mine = (lanes - 6 * group < 3) & ((entry >> 5) == 3 * y + iota((8, WIDTH), 0))
+    mine = mine & (iota((8, WIDTH), 0) < GROUP)
+    table = jnp.where(mine, exact(table, place), 0.0)
+    table = jnp.sum(table, axis=0, keepdims=True)
     lines = []
-    for v in (line_ref[:1, :], dgain_ref[:1, :], table[:1, :]):
+    for v in (line_ref[:1, :], dgain_ref[:1, :], table):
         high = v.astype(bf16).astype(f32)
         lines += [high, v - high]
     block = jnp.concatenate(lines + [jnp.zeros((122, WIDTH), f32)], axis=0).T
@@ -622,7 +706,7 @@
         send_ref[at, 512:SENT] = last.astype(bf16)
         return 0
 
-    lax.fori_loop(0, 6, weights, 0)
+    lax.fori_loop(0, 6, weights, 0, unroll=6)
 
 
 def weight_terms(idx, h, dq, line, dgain, acc, keep, got):
@@ -727,17 +811,23 @@
 ):
     seq = lax.axis_index("seq")
     idx = jnp.stack([seq // 2, seq % 2]).astype(jnp.int32)
-    x_all = lax.all_gather(tokens, "seq", axis=0, tiled=True)
+    blocks = [tokens] + [along_y(tokens, k) for k in (1, 2, 3)]
+    first = other_core(tokens)
     small = jnp.concatenate([gain_attn, gain_moe, rel_table, jnp.zeros((113,), bf16)])
     pack = pack_weights(w_query, w_key, w_value, w_output, w_router, small.reshape(1, 128))
-    wqkv, half, gains, band = unpack_weights(idx, exchange(pack, BOTH))
-    rest = other_core(half)
-    attended = attend(idx, x_all, segments.reshape(LEN, 1), wqkv, gains, band)
+    heads, more = split_weights(exchange(pack, "fsdp"))
+    heads, blocks, first = lax.optimization_barrier((heads, blocks, first))
+    heads, more = lax.optimization_barrier((exchange(heads, "seq"), more))
+    blocks = blocks + [first] + [other_core(b) for b in blocks[1:]]
+    attended = attend(idx, heads, segments.reshape(LEN, 1), blocks)
+    more = [more] + [along_y(more, k) for k in (1, 2, 3)]
+    more, attended = lax.optimization_barrier((more, attended))
+    wo, router = output_weights(idx, more + [other_core(b) for b in more])
     o_parts = attended[:4]
-    h, qe, ke, v, lse = attended[4:]
+    gains, lse, wqkv, band, x_all, qe, ke, v = attended[4:]
     o_parts = [o_parts[0]] + [along_y(o_parts[k], k) for k in (1, 2, 3)]
-    x1, h2, prob, hot, send, wo, router = dispatch(
-        idx, tokens, o_parts, half, rest, gains, routes, cotangent
+    x1, h2, prob, hot, send = dispatch(
+        idx, tokens, o_parts, wo, router, gains, routes, cotangent
     )
     ret, grad_inner, grad_outer = experts(exchange(send, BOTH), w_inner, w_outer)
     back = exchange(ret, BOTH)
@@ -747,7 +837,9 @@
     go_parts = [more[0]] + [along_y(more[k], k) for k in (1, 2, 3)]
     keep, give, dgain = more[4:]
     late = other_core(give)
-    own, other, dq_all, line, acc = attend_back(idx, go_parts, x_all, wqkv, qe, ke, v, band, lse)
+    own, other, dq_all, line, acc, h = attend_back(
+        idx, go_parts, x_all, wqkv, qe, ke, v, band, lse, gains
+    )
     got = other_core(other)
     terms = weight_terms(idx, h, dq_all, line, dgain, acc, keep, late)
     d_parts = pair_sum(idx, own, got)

time: 219 us -> 203 us (0.927)
  between operations: 14.3 us -> 1.06 us
  starting transfers between devices: 38.2 us -> 50.8 us
  waiting for transfers between devices: 48.7 us -> 38.8 us
  Pallas kernels: 61.3 us -> 53.7 us
    all_to_all x3 -> x4, waiting for transfers between devices: 42.5 us -> 33.2 us  [exchange(): return lax.all_to_all(v, axes, split_axis=0, concat_axis=0, tiled=True)]
    ppermute x9 -> x15, starting transfers between devices: 10.8 us -> 17.6 us  [along_y(): return lax.ppermute(v, 'seq', [(s, (s + 2 * k) % 8) for s in range(8)])]
    pallas_call x5 -> x6, Pallas kernels: 46.7 us -> 41.3 us  [the longest x1 13 us: experts(): pl.pallas_call(expert_kernel, out_shape=[sds(LEN, HALF), sds(1, WIDTH, FF...]
    ppermute x3 -> x10, starting transfers between devices: 4.04 us -> 7.7 us  [other_core(): return lax.ppermute(v, 'seq', [(s, s ^ 1) for s in range(8)])]
    all_to_all x3 -> x4, starting transfers between devices: 23.4 us -> 25.5 us  [exchange(): return lax.all_to_all(v, axes, split_axis=0, concat_axis=0, tiled=True)]
    unnamed x45 -> x61, local copies, waits for them, and re-layouts: 6.12 us -> 6.25 us
  transfers between devices with their start and end apart: 16 -> 29, of which waited for: 9 -> 11; matrix products, arithmetic and copies ran while one was open for 1% -> 1% of each run, Pallas kernels for 16% -> 15%
where the time goes in v3:
time: 203 us; the launch traced here: 202 us
  Pallas kernels  53.7 us (26%)
  starting transfers between devices  50.8 us (25%)
  blocking collectives  46.6 us (23%)
  waiting for transfers between devices  38.8 us (19%)
  local copies, waits for them, and re-layouts  8.92 us (4%)
    all_to_all x2, blocking collectives, exchange(): return lax.all_to_all(v, axes, split_axis=0, concat_axis=0, tiled=True)  46.6 us
    all_to_all x4, waiting for transfers between devices, exchange(): return lax.all_to_all(v, axes, split_axis=0, concat_axis=0, tiled=True)  33.2 us
    all_to_all x4, starting transfers between devices, exchange(): return lax.all_to_all(v, axes, split_axis=0, concat_axis=0, tiled=True)  25.5 us
    ppermute x15, starting transfers between devices, along_y(): return lax.ppermute(v, 'seq', [(s, (s + 2 * k) % 8) for s in range(8)])  17.6 us
    pallas_call x1, Pallas kernels, experts(): pl.pallas_call(expert_kernel, out_shape=[sds(LEN, HALF), sds(1, WIDTH, FF...  13 us
    pallas_call x1, Pallas kernels, attend(): pl.pallas_call(attend_kernel, out_shape=outs + saved, in_specs=[smem, vme...  12.2 us
    pallas_call x1, Pallas kernels, attend_back(): call(backward_kernel, outs, [smem] + [vmem] * 12, [pltpu.VMEM((4, TOK, CO...  10.3 us
    ppermute x10, starting transfers between devices, other_core(): return lax.ppermute(v, 'seq', [(s, s ^ 1) for s in range(8)])  7.7 us
  transfers between devices with their start and end apart: 29, of which 11 were waited for; matrix products, arithmetic and copies ran while one was open for 1% of the time, Pallas kernels for 15%

profile of v3, /device:TPU:1, one launch (start us, length us, event | category | flops | bytes accessed | tf_op | source)
XLA Modules:
  0.0 201.8 jit_solution(4354263902496384632)
XLA Ops:
  0.7 1.3 maximum_bitcast_fusion.small_ref
  1.9 1.7 pack_weights.1
  3.6 8.4 %all-to-all-start = ((bf16[16,8,2432]{2,1,0:T(8,128)(2,1)}), bf16[16,8,2432]{2,1,0:T(8,128)(2,1)S(1)}, u32[]{:S(2)}, u32[]{:S(2)}) async-start(bf16[16,8,2432]{2,1,0:T(8,128)(2,1)} %bitcast.26), calls=%async_computation | async-start | bytes 1245184 | tf_op jit(solution)/shard_map/all_to_all | solution.py:801
  12.1 1.0 collective-permute-start.3
  13.1 2.7 %collective-permute-start.2 = (bf16[128,768]{1,0:T(8,128)(2,1)S(1)}, bf16[128,768]{1,0:T(8,128)(2,1)S(1)}, u32[]{:S(2)}, u32[]{:S(2)}) collective-permute-start(bf16[128,768]{1,0:T(8,128)(2,1)S(1)} %copy-done.1), channel_id=1, source_target_pairs={{0,6},{1,7},{2,0},{3,1},{4,2},{5,3},{6,4},{7,5},{8,14},{9,15},{10,... | collective-permute-start | bytes 589832 | tf_op jit(solution)/shard_map/ppermute | solution.py:797
  16.2 0.7 collective-permute-start
  16.9 6.6 %all-to-all-done = bf16[16,8,2432]{2,1,0:T(8,128)(2,1)S(1)} async-done(((bf16[16,8,2432]{2,1,0:T(8,128)(2,1)}), bf16[16,8,2432]{2,1,0:T(8,128)(2,1)S(1)}, u32[]{:S(2)}, u32[]{:S(2)}) %all-to-all-start) | async-done | bytes 622624 | tf_op jit(solution)/shard_map/all_to_all | solution.py:801
  23.5 0.8 copy-done.20
  24.3 2.5 %split_weights.1 = (bf16[768,640]{1,0:T(8,128)(2,1)}, bf16[96,896]{1,0:T(8,128)(2,1)}) custom-call(bf16[128,2432]{1,0:T(8,128)(2,1)} %bitcast.25), custom_call_target="tpu_custom_call" | custom-call | flops 2300000000 | bytes 1048576 | tf_op jit(solution)/shard_map/split_weights/pallas_call | solution.py:167
  26.8 1.5 collective-permute-done.refs_1_
  28.4 5.2 %all-to-all-start.1 = ((bf16[8,96,640]{2,1,0:T(8,128)(2,1)}), bf16[8,96,640]{2,1,0:T(8,128)(2,1)S(1)}, u32[]{:S(2)}, u32[]{:S(2)}) async-start(bf16[8,96,640]{2,1,0:T(8,128)(2,1)} %bitcast.22), calls=%async_computation.1 | async-start | bytes 1966080 | tf_op jit(solution)/shard_map/all_to_all | solution.py:801
  34.1 1.0 copy.27.seg_ref
  35.7 12.3 %all-to-all-done.1 = bf16[8,96,640]{2,1,0:T(8,128)(2,1)S(1)} async-done(((bf16[8,96,640]{2,1,0:T(8,128)(2,1)}), bf16[8,96,640]{2,1,0:T(8,128)(2,1)S(1)}, u32[]{:S(2)}, u32[]{:S(2)}) %all-to-all-start.1) | async-done | bytes 983072 | tf_op jit(solution)/shard_map/all_to_all | solution.py:801
  48.0 1.0 collective-permute-start.6
  49.0 1.2 collective-permute-start.5
  51.6 12.2 %attend.1 = (bf16[128,192]{1,0:T(8,128)(2,1)}, bf16[128,192]{1,0:T(8,128)(2,1)}, bf16[128,192]{1,0:T(8,128)(2,1)}, bf16[128,192]{1,0:T(8,128)(2,1)}, f32[8,768]{...) custom-call(s32[2]{0:T(128)} %pad_add_fusion.idx_ref, ...), custom_call_target="tpu_custom_call" | custom-call | flops 16099999744 | bytes 1048576 | tf_op jit(solution)/shard_map/attend/pallas_call | solution.py:339
  63.9 1.5 collective-permute-start.13
  66.2 1.7 collective-permute-start.10
  67.9 2.4 %collective-permute-start.11 = (bf16[128,192]{1,0:T(8,128)(2,1)}, bf16[128,192]{1,0:T(8,128)(2,1)S(1)}, u32[]{:S(2)}, u32[]{:S(2)}) collective-permute-start(bf16[128,192]{1,0:T(8,128)(2,1)} %get-tuple-element.109), channel_id=1, source_target_pairs={{0,4},{1,5},{2,6},{3,7},{4,0},{5,1},{6,2},{7,3},{8,12},{9,13},{10,... | collective-permute-start | bytes 147464 | tf_op jit(solution)/shard_map/ppermute | solution.py:797
  70.3 1.2 collective-permute-start.12
  71.5 1.7 output_weights.1
  73.9 2.0 %dispatch.1 = (f32[128,768]{1,0:T(8,128)S(1)}, bf16[128,768]{1,0:T(8,128)(2,1)S(1)}, f32[128,128]{1,0:T(8,128)S(1)}, bf16[2,128,128]{2,1,0:T(8,128)(2,1)S(1)}, bf16[1024,384]{1,0:T(8,128)(2,1)S(1)}) custom-call(s32[2]{0:T(128)S(1)} %copy-done.4, bf16[128,768]{1,0:T(8,128)(2,1)S(1)} %copy-done.2, bf16[128,192]{1,0:T(8,128)(2,1)S(1)} %copy-done.9, ...), custom_call_target="tpu_custom_call" | custom-call | flops 2300000000 | bytes 1048576 | tf_op jit(solution)/shard_map/dispatch/pallas_call | solution.py:399
  76.0 25.4 %all_to_all.67 = bf16[128,8,384]{2,1,0:T(8,128)(2,1)} all-to-all(bf16[128,8,384]{2,1,0:T(8,128)(2,1)S(1)} %bitcast.19), channel_id=1, replica_groups=mesh['fsdp'=16,'seq'=8] {'fsdp','seq'}, dimensions={0} | all-to-all | bytes 1572864 | tf_op jit(solution)/shard_map/all_to_all | solution.py:801
  101.4 13.0 %experts.1 = (bf16[1024,384]{1,0:T(8,128)(2,1)}, bf16[1,768,3072]{2,1,0:T(8,128)(2,1)}, bf16[1,3072,768]{2,1,0:T(8,128)(2,1)}) custom-call(bf16[1024,384]{1,0:T(8,128)(2,1)} %bitcast.23, bf16[1,768,3072]{2,1,0:T(8,128)(2,1)} %wi_hbm.1, bf16[1,3072,768]{2,1,0:T(8,128)(2,1)} %wo_hbm.1), custom_call_target="tpu_custom_call" | custom-call | flops 13799999488 | bytes 1048576 | tf_op jit(solution)/shard_map/experts/pallas_call | solution.py:478
  114.4 21.2 %all_to_all.68 = bf16[128,8,384]{2,1,0:T(8,128)(2,1)S(1)} all-to-all(bf16[128,8,384]{2,1,0:T(8,128)(2,1)} %bitcast.24), channel_id=1, replica_groups=mesh['fsdp'=16,'seq'=8] {'fsdp','seq'}, dimensions={0} | all-to-all | bytes 1572864 | tf_op jit(solution)/shard_map/all_to_all | solution.py:801
  135.6 2.4 %returned.1 = (bf16[128,768]{1,0:T(8,128)(2,1)}, f32[128,768]{1,0:T(8,128)S(1)}, bf16[128,192]{1,0:T(8,128)(2,1)S(1)}, bf16[128,192]{1,0:T(8,128)(2,1)S(1)}, bf1...) custom-call(s32[2]{0:T(128)S(1)} %copy-done.4, ...), custom_call_target="tpu_custom_call" | custom-call | flops 2300000000 | bytes 1048576 | tf_op jit(solution)/shard_map/returned/pallas_call | solution.py:564
  138.0 2.1 %collective-permute-start.18 = (bf16[128,192]{1,0:T(8,128)(2,1)S(1)}, bf16[128,192]{1,0:T(8,128)(2,1)S(1)}, u32[]{:S(2)}, u32[]{:S(2)}) collective-permute-start(bf16[128,192]{1,0:T(8,128)(2,1)S(1)} %get-tuple-element.127), channel_id=1, source_target_pairs={{0,4},{1,5},{2,6},{3,7},{4,0},{5,1},{6,2},{7,3},{8,12},{9,13},{10,... | collective-permute-start | bytes 147464 | tf_op jit(solution)/shard_map/ppermute | solution.py:797
  140.1 0.7 collective-permute-start.19
  140.9 1.6 collective-permute-start.24
  144.0 10.3 %attend_back.1 = (f32[4,128,768]{2,1,0:T(8,128)S(1)}, bf16[4,128,768]{2,1,0:T(8,128)(2,1)S(1)}, bf16[1024,576]{1,0:T(8,128)(2,1)S(1)}, f32[8,768]{1,0:T(8,128)S(...) custom-call(s32[2]{0:T(128)S(1)} %copy-done.4, bf16[128,192]{1,0:T(8,128)(2,1)S(1)} %get-tuple-element.125.g0_ref, ...), custom_call_target="tpu_custom_call" | custom-call | flops 13799999488 | bytes 1048576 | tf_op jit(solution)/shard_map/attend_back/pallas_call | solution.py:643
  154.3 4.6 %weight_terms.1 = bf16[768,1152]{1,0:T(8,128)(2,1)} custom-call(s32[2]{0:T(128)S(1)} %copy-done.4, bf16[1024,768]{1,0:T(8,128)(2,1)S(1)} %get-tuple-element.143.h_ref, bf16[1024,576]{1,0:T(8,128)(2,1)S(1)} %get-tuple-element.144.dq_ref, f32[8,768]{1,0:T(8,128)S(1)} %get-tuple-element.145.line_ref, f32[8,768]{1,0:T(8,128)S(1)} %get-tuple-element.146.dgain_ref, ...), custom_call_target="tpu_custom_call" | custom-call | flops 5750000128 | bytes 1048576 | tf_op jit(solution)/shard_map/weight_terms/pallas_call | solution.py:713
  158.9 3.7 %all-to-all-start.4 = ((bf16[16,48,1152]{2,1,0:T(8,128)(2,1)}), bf16[16,48,1152]{2,1,0:T(8,128)(2,1)S(1)}, u32[]{:S(2)}, u32[]{:S(2)}) async-start(bf16[16,48,1152]{2,1,0:T(8,128)(2,1)} %bitcast.12), calls=%async_computation.4 | async-start | bytes 3538944 | tf_op jit(solution)/shard_map/all_to_all | solution.py:801
  162.6 2.4 %collective-permute-start.20 = (bf16[4,128,768]{2,1,0:T(8,128)(2,1)S(1)}, bf16[4,128,768]{2,1,0:T(8,128)(2,1)S(1)}, u32[]{:S(2)}, u32[]{:S(2)}) collective-permute-start(bf16[4,128,768]{2,1,0:T(8,128)(2,1)S(1)} %get-tuple-element.137), channel_id=1, source_target_pairs={{0,1},{1,0},{2,3},{3,2},{4,5},{5,4},{6,7},{7,6},{8,9},{9,8},{10,11... | collective-permute-start | bytes 2359304 | tf_op jit(solution)/shard_map/ppermute | solution.py:805
  165.0 1.9 collective-permute-done.20.got_ref
  167.0 1.4 copy-done.6
  169.1 0.7 copy-done.7
  169.8 1.0 collective-permute-start.21
  170.8 2.2 %collective-permute-start.22 = (bf16[128,768]{1,0:T(8,128)(2,1)S(1)}, bf16[128,768]{1,0:T(8,128)(2,1)S(1)}, u32[]{:S(2)}, u32[]{:S(2)}) collective-permute-start(bf16[128,768]{1,0:T(8,128)(2,1)S(1)} %get-tuple-element.140), channel_id=1, source_target_pairs={{0,4},{1,5},{2,6},{3,7},{4,0},{5,1},{6,2},{7,3},{8,12},{9,13},{10,... | collective-permute-start | bytes 589832 | tf_op jit(solution)/shard_map/ppermute | solution.py:797
  173.2 11.7 %all-to-all-done.4 = bf16[16,48,1152]{2,1,0:T(8,128)(2,1)S(1)} async-done(((bf16[16,48,1152]{2,1,0:T(8,128)(2,1)}), bf16[16,48,1152]{2,1,0:T(8,128)(2,1)S(1)}, u32[]{:S(2)}, u32[]{:S(2)}) %all-to-all-start.4) | async-done | bytes 1769504 | tf_op jit(solution)/shard_map/all_to_all | solution.py:801
  184.9 1.0 middle_sums.1
  185.9 8.2 %all-to-all-start.5 = ((bf16[8,8,1152]{2,1,0:T(8,128)(2,1)}), bf16[8,8,1152]{2,1,0:T(8,128)(2,1)S(1)}, u32[]{:S(2)}, u32[]{:S(2)}) async-start(bf16[8,8,1152]{2,1,0:T(8,128)(2,1)} %bitcast.14), calls=%async_computation.5 | async-start | bytes 294912 | tf_op jit(solution)/shard_map/all_to_all | solution.py:801
  194.1 1.0 copy-done.8
  195.1 0.7 copy-done.11
  195.8 1.0 tokens_last.1
  196.8 2.7 %all-to-all-done.5 = bf16[8,8,1152]{2,1,0:T(8,128)(2,1)S(1)} async-done(((bf16[8,8,1152]{2,1,0:T(8,128)(2,1)}), bf16[8,8,1152]{2,1,0:T(8,128)(2,1)S(1)}, u32[]{:S(2)}, u32[]{:S(2)}) %all-to-all-start.5) | async-done | bytes 147488 | tf_op jit(solution)/shard_map/all_to_all | solution.py:801
  199.5 0.7 sums_last.1
  200.4 0.7 slice_reduce_fusion.2
  201.1 0.7 slice_reduce_fusion
  (96 shorter events, 6.9 us)
Async XLA Ops:
  1.9 10.1 %copy-start.1 = (bf16[128,768]{1,0:T(8,128)(2,1)S(1)}, bf16[128,768]{1,0:T(8,128)(2,1)}, u32[]{:S(2)}) copy-start(bf16[128,768]{1,0:T(8,128)(2,1)} %x_ref.3) | copy-start | bytes 589828
  3.6 19.9 %all-to-all-start = ((bf16[16,8,2432]{2,1,0:T(8,128)(2,1)}), bf16[16,8,2432]{2,1,0:T(8,128)(2,1)S(1)}, u32[]{:S(2)}, u32[]{:S(2)}) async-start(bf16[16,8,2432]{2,1,0:T(8,128)(2,1)} %bitcast.26), calls=%async_computation | async-start | bytes 1245184 | tf_op jit(solution)/shard_map/all_to_all | solution.py:801
  12.1 14.7 %collective-permute-start.3 = (bf16[128,768]{1,0:T(8,128)(2,1)S(1)}, bf16[128,768]{1,0:T(8,128)(2,1)S(1)}, u32[]{:S(2)}, u32[]{:S(2)}) collective-permute-start(bf16[128,768]{1,0:T(8,128)(2,1)S(1)} %copy-done.1), channel_id=1, source_target_pairs={{0,1},{1,0},{2,3},{3,2},{4,5},{5,4},{6,7},{7,6},{8,9},{9,8},{10,11... | collective-permute-start | bytes 589832 | tf_op jit(solution)/shard_map/ppermute | solution.py:805
  13.1 13.7 %collective-permute-start.2 = (bf16[128,768]{1,0:T(8,128)(2,1)S(1)}, bf16[128,768]{1,0:T(8,128)(2,1)S(1)}, u32[]{:S(2)}, u32[]{:S(2)}) collective-permute-start(bf16[128,768]{1,0:T(8,128)(2,1)S(1)} %copy-done.1), channel_id=1, source_target_pairs={{0,6},{1,7},{2,0},{3,1},{4,2},{5,3},{6,4},{7,5},{8,14},{9,15},{10,... | collective-permute-start | bytes 589832 | tf_op jit(solution)/shard_map/ppermute | solution.py:797
  15.8 11.0 %collective-permute-start.1 = (bf16[128,768]{1,0:T(8,128)(2,1)S(1)}, bf16[128,768]{1,0:T(8,128)(2,1)S(1)}, u32[]{:S(2)}, u32[]{:S(2)}) collective-permute-start(bf16[128,768]{1,0:T(8,128)(2,1)S(1)} %copy-done.1), channel_id=1, source_target_pairs={{0,4},{1,5},{2,6},{3,7},{4,0},{5,1},{6,2},{7,3},{8,12},{9,13},{10,... | collective-permute-start | bytes 589832 | tf_op jit(solution)/shard_map/ppermute | solution.py:797
  16.2 12.2 %collective-permute-start = (bf16[128,768]{1,0:T(8,128)(2,1)S(1)}, bf16[128,768]{1,0:T(8,128)(2,1)S(1)}, u32[]{:S(2)}, u32[]{:S(2)}) collective-permute-start(bf16[128,768]{1,0:T(8,128)(2,1)S(1)} %copy-done.1), channel_id=1, source_target_pairs={{0,2},{1,3},{2,4},{3,5},{4,6},{5,7},{6,0},{7,1},{8,10},{9,11},{10,... | collective-permute-start | bytes 589832 | tf_op jit(solution)/shard_map/ppermute | solution.py:797
  26.8 21.2 %copy-start.3 = (bf16[96,896]{1,0:T(8,128)(2,1)S(1)}, bf16[96,896]{1,0:T(8,128)(2,1)}, u32[]{:S(2)}) copy-start(bf16[96,896]{1,0:T(8,128)(2,1)} %get-tuple-element.111.refs_0_) | copy-start | bytes 516100
  26.8 23.4 %copy-start.23 = (bf16[128,768]{1,0:T(8,128)(2,1)}, bf16[128,768]{1,0:T(8,128)(2,1)S(1)}, u32[]{:S(2)}) copy-start(bf16[128,768]{1,0:T(8,128)(2,1)S(1)} %collective-permute-done.3.refs_4_) | copy-start | bytes 589828
  26.8 23.4 %copy-start.24 = (bf16[128,768]{1,0:T(8,128)(2,1)}, bf16[128,768]{1,0:T(8,128)(2,1)S(1)}, u32[]{:S(2)}) copy-start(bf16[128,768]{1,0:T(8,128)(2,1)S(1)} %collective-permute-done.2.refs_3_) | copy-start | bytes 589828
  26.8 23.4 %copy-start.25 = (bf16[128,768]{1,0:T(8,128)(2,1)}, bf16[128,768]{1,0:T(8,128)(2,1)S(1)}, u32[]{:S(2)}) copy-start(bf16[128,768]{1,0:T(8,128)(2,1)S(1)} %collective-permute-done.1.refs_2_) | copy-start | bytes 589828
  28.4 21.9 %copy-start.26 = (bf16[128,768]{1,0:T(8,128)(2,1)}, bf16[128,768]{1,0:T(8,128)(2,1)S(1)}, u32[]{:S(2)}) copy-start(bf16[128,768]{1,0:T(8,128)(2,1)S(1)} %collective-permute-done.refs_1_) | copy-start | bytes 589828
  28.4 19.6 %all-to-all-start.1 = ((bf16[8,96,640]{2,1,0:T(8,128)(2,1)}), bf16[8,96,640]{2,1,0:T(8,128)(2,1)S(1)}, u32[]{:S(2)}, u32[]{:S(2)}) async-start(bf16[8,96,640]{2,1,0:T(8,128)(2,1)} %bitcast.22), calls=%async_computation.1 | async-start | bytes 1966080 | tf_op jit(solution)/shard_map/all_to_all | solution.py:801
  33.6 16.6 %collective-permute-start.7 = (bf16[128,768]{1,0:T(8,128)(2,1)S(1)}, bf16[128,768]{1,0:T(8,128)(2,1)S(1)}, u32[]{:S(2)}, u32[]{:S(2)}) collective-permute-start(bf16[128,768]{1,0:T(8,128)(2,1)S(1)} %collective-permute-done.refs_1_), channel_id=1, source_target_pairs={{0,1},{1,0},{2,3},{3,2},{4,5},{5,4},{6,7},{7,6},{8,9},{9,8},{10,11... | collective-permute-start | bytes 589832 | tf_op jit(solution)/shard_map/ppermute | solution.py:805
  33.6 16.6 %collective-permute-start.8 = (bf16[128,768]{1,0:T(8,128)(2,1)S(1)}, bf16[128,768]{1,0:T(8,128)(2,1)S(1)}, u32[]{:S(2)}, u32[]{:S(2)}) collective-permute-start(bf16[128,768]{1,0:T(8,128)(2,1)S(1)} %collective-permute-done.1.refs_2_), channel_id=1, source_target_pairs={{0,1},{1,0},{2,3},{3,2},{4,5},{5,4},{6,7},{7,6},{8,9},{9,8},{10,11... | collective-permute-start | bytes 589832 | tf_op jit(solution)/shard_map/ppermute | solution.py:805
  34.1 16.1 %collective-permute-start.9 = (bf16[128,768]{1,0:T(8,128)(2,1)S(1)}, bf16[128,768]{1,0:T(8,128)(2,1)S(1)}, u32[]{:S(2)}, u32[]{:S(2)}) collective-permute-start(bf16[128,768]{1,0:T(8,128)(2,1)S(1)} %collective-permute-done.2.refs_3_), channel_id=1, source_target_pairs={{0,1},{1,0},{2,3},{3,2},{4,5},{5,4},{6,7},{7,6},{8,9},{9,8},{10,11... | collective-permute-start | bytes 589832 | tf_op jit(solution)/shard_map/ppermute | solution.py:805
  48.0 18.0 %copy-start.22 = (s32[128,1]{0,1:T(1,128)S(1)}, s32[128,1]{0,1:T(1,128)}, u32[]{:S(2)}) copy-start(s32[128,1]{0,1:T(1,128)} %param.16) | copy-start | bytes 1540
  48.0 23.5 %copy-start.4 = (s32[2]{0:T(128)S(1)}, s32[2]{0:T(128)}, u32[]{:S(2)}) copy-start(s32[2]{0:T(128)} %pad_add_fusion.idx_ref) | copy-start | bytes 28
  48.0 15.8 %collective-permute-start.6 = (bf16[96,896]{1,0:T(8,128)(2,1)S(1)}, bf16[96,896]{1,0:T(8,128)(2,1)S(1)}, u32[]{:S(2)}, u32[]{:S(2)}) collective-permute-start(bf16[96,896]{1,0:T(8,128)(2,1)S(1)} %copy-done.3), channel_id=1, source_target_pairs={{0,6},{1,7},{2,0},{3,1},{4,2},{5,3},{6,4},{7,5},{8,14},{9,15},{10,... | collective-permute-start | bytes 516104 | tf_op jit(solution)/shard_map/ppermute | solution.py:797
  49.0 14.9 %collective-permute-start.5 = (bf16[96,896]{1,0:T(8,128)(2,1)S(1)}, bf16[96,896]{1,0:T(8,128)(2,1)S(1)}, u32[]{:S(2)}, u32[]{:S(2)}) collective-permute-start(bf16[96,896]{1,0:T(8,128)(2,1)S(1)} %copy-done.3), channel_id=1, source_target_pairs={{0,4},{1,5},{2,6},{3,7},{4,0},{5,1},{6,2},{7,3},{8,12},{9,13},{10,... | collective-permute-start | bytes 516104 | tf_op jit(solution)/shard_map/ppermute | solution.py:797
  50.2 13.7 %collective-permute-start.4 = (bf16[96,896]{1,0:T(8,128)(2,1)S(1)}, bf16[96,896]{1,0:T(8,128)(2,1)S(1)}, u32[]{:S(2)}, u32[]{:S(2)}) collective-permute-start(bf16[96,896]{1,0:T(8,128)(2,1)S(1)} %copy-done.3), channel_id=1, source_target_pairs={{0,2},{1,3},{2,4},{3,5},{4,6},{5,7},{6,0},{7,1},{8,10},{9,11},{10,... | collective-permute-start | bytes 516104 | tf_op jit(solution)/shard_map/ppermute | solution.py:797
  63.9 4.0 %collective-permute-start.13 = (bf16[96,896]{1,0:T(8,128)(2,1)S(1)}, bf16[96,896]{1,0:T(8,128)(2,1)S(1)}, u32[]{:S(2)}, u32[]{:S(2)}) collective-permute-start(bf16[96,896]{1,0:T(8,128)(2,1)S(1)} %copy-done.3), channel_id=1, source_target_pairs={{0,1},{1,0},{2,3},{3,2},{4,5},{5,4},{6,7},{7,6},{8,9},{9,8},{10,11... | collective-permute-start | bytes 516104 | tf_op jit(solution)/shard_map/ppermute | solution.py:805
  65.4 4.9 %collective-permute-start.14 = (bf16[96,896]{1,0:T(8,128)(2,1)S(1)}, bf16[96,896]{1,0:T(8,128)(2,1)S(1)}, u32[]{:S(2)}, u32[]{:S(2)}) collective-permute-start(bf16[96,896]{1,0:T(8,128)(2,1)S(1)} %collective-permute-done.4.refs_1_), channel_id=1, source_target_pairs={{0,1},{1,0},{2,3},{3,2},{4,5},{5,4},{6,7},{7,6},{8,9},{9,8},{10,11... | collective-permute-start | bytes 516104 | tf_op jit(solution)/shard_map/ppermute | solution.py:805
  65.5 6.0 %collective-permute-start.15 = (bf16[96,896]{1,0:T(8,128)(2,1)S(1)}, bf16[96,896]{1,0:T(8,128)(2,1)S(1)}, u32[]{:S(2)}, u32[]{:S(2)}) collective-permute-start(bf16[96,896]{1,0:T(8,128)(2,1)S(1)} %collective-permute-done.5.refs_2_), channel_id=1, source_target_pairs={{0,1},{1,0},{2,3},{3,2},{4,5},{5,4},{6,7},{7,6},{8,9},{9,8},{10,11... | collective-permute-start | bytes 516104 | tf_op jit(solution)/shard_map/ppermute | solution.py:805
  65.9 5.6 %collective-permute-start.16 = (bf16[96,896]{1,0:T(8,128)(2,1)S(1)}, bf16[96,896]{1,0:T(8,128)(2,1)S(1)}, u32[]{:S(2)}, u32[]{:S(2)}) collective-permute-start(bf16[96,896]{1,0:T(8,128)(2,1)S(1)} %collective-permute-done.6.refs_3_), channel_id=1, source_target_pairs={{0,1},{1,0},{2,3},{3,2},{4,5},{5,4},{6,7},{7,6},{8,9},{9,8},{10,11... | collective-permute-start | bytes 516104 | tf_op jit(solution)/shard_map/ppermute | solution.py:805
  66.1 7.8 %copy-start = (bf16[128,768]{1,0:T(8,128)(2,1)S(1)}, bf16[128,768]{1,0:T(8,128)(2,1)}, u32[]{:S(2)}) copy-start(bf16[128,768]{1,0:T(8,128)(2,1)} %cot_ref.3) | copy-start | bytes 589828
  66.1 7.8 %copy-start.2 = (bf16[128,768]{1,0:T(8,128)(2,1)S(1)}, bf16[128,768]{1,0:T(8,128)(2,1)}, u32[]{:S(2)}) copy-start(bf16[128,768]{1,0:T(8,128)(2,1)} %x_ref.3) | copy-start | bytes 589828
  66.1 7.8 %copy-start.9 = (bf16[128,192]{1,0:T(8,128)(2,1)S(1)}, bf16[128,192]{1,0:T(8,128)(2,1)}, u32[]{:S(2)}) copy-start(bf16[128,192]{1,0:T(8,128)(2,1)} %get-tuple-element.107.o0_ref) | copy-start | bytes 147460
  66.1 7.8 %copy-start.10 = (f32[8,768]{1,0:T(8,128)S(1)}, f32[8,768]{1,0:T(8,128)}, u32[]{:S(2)}) copy-start(f32[8,768]{1,0:T(8,128)} %get-tuple-element.117.gain_ref) | copy-start | bytes 73732
  66.2 7.0 %collective-permute-start.10 = (bf16[128,192]{1,0:T(8,128)(2,1)}, bf16[128,192]{1,0:T(8,128)(2,1)S(1)}, u32[]{:S(2)}, u32[]{:S(2)}) collective-permute-start(bf16[128,192]{1,0:T(8,128)(2,1)} %get-tuple-element.108), channel_id=1, source_target_pairs={{0,2},{1,3},{2,4},{3,5},{4,6},{5,7},{6,0},{7,1},{8,10},{9,11},{10,... | collective-permute-start | bytes 147464 | tf_op jit(solution)/shard_map/ppermute | solution.py:797
  67.9 5.5 %collective-permute-start.11 = (bf16[128,192]{1,0:T(8,128)(2,1)}, bf16[128,192]{1,0:T(8,128)(2,1)S(1)}, u32[]{:S(2)}, u32[]{:S(2)}) collective-permute-start(bf16[128,192]{1,0:T(8,128)(2,1)} %get-tuple-element.109), channel_id=1, source_target_pairs={{0,4},{1,5},{2,6},{3,7},{4,0},{5,1},{6,2},{7,3},{8,12},{9,13},{10,... | collective-permute-start | bytes 147464 | tf_op jit(solution)/shard_map/ppermute | solution.py:797
  70.3 3.6 %collective-permute-start.12 = (bf16[128,192]{1,0:T(8,128)(2,1)}, bf16[128,192]{1,0:T(8,128)(2,1)S(1)}, u32[]{:S(2)}, u32[]{:S(2)}) collective-permute-start(bf16[128,192]{1,0:T(8,128)(2,1)} %get-tuple-element.110), channel_id=1, source_target_pairs={{0,6},{1,7},{2,0},{3,1},{4,2},{5,3},{6,4},{7,5},{8,14},{9,15},{10,... | collective-permute-start | bytes 147464 | tf_op jit(solution)/shard_map/ppermute | solution.py:797
  135.5 8.4 %copy-start.12 = (bf16[1024,768]{1,0:T(8,128)(2,1)S(1)}, bf16[1024,768]{1,0:T(8,128)(2,1)}, u32[]{:S(2)}) copy-start(bf16[1024,768]{1,0:T(8,128)(2,1)} %get-tuple-element.129.x_ref) | copy-start | bytes 4718596
  135.5 8.4 %copy-start.13 = (bf16[768,576]{1,0:T(8,128)(2,1)S(1)}, bf16[768,576]{1,0:T(8,128)(2,1)}, u32[]{:S(2)}) copy-start(bf16[768,576]{1,0:T(8,128)(2,1)} %get-tuple-element.130.wqkv_ref) | copy-start | bytes 2654212
  135.5 8.4 %copy-start.14 = (f32[3,128,640]{2,1,0:T(8,128)S(1)}, f32[3,128,640]{2,1,0:T(8,128)}, u32[]{:S(2)}) copy-start(f32[3,128,640]{2,1,0:T(8,128)} %get-tuple-element.134.band_ref) | copy-start | bytes 2949124
  135.6 8.4 %copy-start.15 = (bf16[1024,384]{1,0:T(8,128)(2,1)S(1)}, bf16[1024,384]{1,0:T(8,128)(2,1)}, u32[]{:S(2)}) copy-start(bf16[1024,384]{1,0:T(8,128)(2,1)} %get-tuple-element.131.qe_ref) | copy-start | bytes 2359300
  135.6 8.4 %copy-start.16 = (bf16[1024,384]{1,0:T(8,128)(2,1)S(1)}, bf16[1024,384]{1,0:T(8,128)(2,1)}, u32[]{:S(2)}) copy-start(bf16[1024,384]{1,0:T(8,128)(2,1)} %get-tuple-element.132.ke_ref) | copy-start | bytes 2359300
  135.6 8.4 %copy-start.17 = (bf16[1024,192]{1,0:T(8,128)(2,1)S(1)}, bf16[1024,192]{1,0:T(8,128)(2,1)}, u32[]{:S(2)}) copy-start(bf16[1024,192]{1,0:T(8,128)(2,1)} %get-tuple-element.133.v_ref) | copy-start | bytes 1179652
  135.6 8.4 %copy-start.18 = (f32[4,128,128]{2,1,0:T(8,128)S(1)}, f32[4,128,128]{2,1,0:T(8,128)}, u32[]{:S(2)}) copy-start(f32[4,128,128]{2,1,0:T(8,128)} %get-tuple-element.135.lse_ref) | copy-start | bytes 786436
  138.0 4.7 %collective-permute-start.17 = (bf16[128,192]{1,0:T(8,128)(2,1)S(1)}, bf16[128,192]{1,0:T(8,128)(2,1)S(1)}, u32[]{:S(2)}, u32[]{:S(2)}) collective-permute-start(bf16[128,192]{1,0:T(8,128)(2,1)S(1)} %get-tuple-element.126), channel_id=1, source_target_pairs={{0,2},{1,3},{2,4},{3,5},{4,6},{5,7},{6,0},{7,1},{8,10},{9,11},{10,... | collective-permute-start | bytes 147464 | tf_op jit(solution)/shard_map/ppermute | solution.py:797
  138.0 5.3 %collective-permute-start.18 = (bf16[128,192]{1,0:T(8,128)(2,1)S(1)}, bf16[128,192]{1,0:T(8,128)(2,1)S(1)}, u32[]{:S(2)}, u32[]{:S(2)}) collective-permute-start(bf16[128,192]{1,0:T(8,128)(2,1)S(1)} %get-tuple-element.127), channel_id=1, source_target_pairs={{0,4},{1,5},{2,6},{3,7},{4,0},{5,1},{6,2},{7,3},{8,12},{9,13},{10,... | collective-permute-start | bytes 147464 | tf_op jit(solution)/shard_map/ppermute | solution.py:797
  140.1 3.8 %collective-permute-start.19 = (bf16[128,192]{1,0:T(8,128)(2,1)S(1)}, bf16[128,192]{1,0:T(8,128)(2,1)S(1)}, u32[]{:S(2)}, u32[]{:S(2)}) collective-permute-start(bf16[128,192]{1,0:T(8,128)(2,1)S(1)} %get-tuple-element.128), channel_id=1, source_target_pairs={{0,6},{1,7},{2,0},{3,1},{4,2},{5,3},{6,4},{7,5},{8,14},{9,15},{10,... | collective-permute-start | bytes 147464 | tf_op jit(solution)/shard_map/ppermute | solution.py:797
  140.9 13.4 %collective-permute-start.24 = (bf16[768,512]{1,0:T(8,128)(2,1)S(1)}, bf16[768,512]{1,0:T(8,128)(2,1)S(1)}, u32[]{:S(2)}, u32[]{:S(2)}) collective-permute-start(bf16[768,512]{1,0:T(8,128)(2,1)S(1)} %get-tuple-element.149), channel_id=1, source_target_pairs={{0,1},{1,0},{2,3},{3,2},{4,5},{5,4},{6,7},{7,6},{8,9},{9,8},{10,11... | collective-permute-start | bytes 2359304 | tf_op jit(solution)/shard_map/ppermute | solution.py:805
  158.9 26.0 %all-to-all-start.4 = ((bf16[16,48,1152]{2,1,0:T(8,128)(2,1)}), bf16[16,48,1152]{2,1,0:T(8,128)(2,1)S(1)}, u32[]{:S(2)}, u32[]{:S(2)}) async-start(bf16[16,48,1152]{2,1,0:T(8,128)(2,1)} %bitcast.12), calls=%async_computation.4 | async-start | bytes 3538944 | tf_op jit(solution)/shard_map/all_to_all | solution.py:801
  162.6 4.3 %collective-permute-start.20 = (bf16[4,128,768]{2,1,0:T(8,128)(2,1)S(1)}, bf16[4,128,768]{2,1,0:T(8,128)(2,1)S(1)}, u32[]{:S(2)}, u32[]{:S(2)}) collective-permute-start(bf16[4,128,768]{2,1,0:T(8,128)(2,1)S(1)} %get-tuple-element.137), channel_id=1, source_target_pairs={{0,1},{1,0},{2,3},{3,2},{4,5},{5,4},{6,7},{7,6},{8,9},{9,8},{10,11... | collective-permute-start | bytes 2359304 | tf_op jit(solution)/shard_map/ppermute | solution.py:805
  169.8 24.2 %collective-permute-start.21 = (bf16[128,768]{1,0:T(8,128)(2,1)S(1)}, bf16[128,768]{1,0:T(8,128)(2,1)S(1)}, u32[]{:S(2)}, u32[]{:S(2)}) collective-permute-start(bf16[128,768]{1,0:T(8,128)(2,1)S(1)} %get-tuple-element.139), channel_id=1, source_target_pairs={{0,2},{1,3},{2,4},{3,5},{4,6},{5,7},{6,0},{7,1},{8,10},{9,11},{10,... | collective-permute-start | bytes 589832 | tf_op jit(solution)/shard_map/ppermute | solution.py:797
  170.8 23.2 %collective-permute-start.22 = (bf16[128,768]{1,0:T(8,128)(2,1)S(1)}, bf16[128,768]{1,0:T(8,128)(2,1)S(1)}, u32[]{:S(2)}, u32[]{:S(2)}) collective-permute-start(bf16[128,768]{1,0:T(8,128)(2,1)S(1)} %get-tuple-element.140), channel_id=1, source_target_pairs={{0,4},{1,5},{2,6},{3,7},{4,0},{5,1},{6,2},{7,3},{8,12},{9,13},{10,... | collective-permute-start | bytes 589832 | tf_op jit(solution)/shard_map/ppermute | solution.py:797
  173.1 21.0 %collective-permute-start.23 = (bf16[128,768]{1,0:T(8,128)(2,1)S(1)}, bf16[128,768]{1,0:T(8,128)(2,1)S(1)}, u32[]{:S(2)}, u32[]{:S(2)}) collective-permute-start(bf16[128,768]{1,0:T(8,128)(2,1)S(1)} %get-tuple-element.141), channel_id=1, source_target_pairs={{0,6},{1,7},{2,0},{3,1},{4,2},{5,3},{6,4},{7,5},{8,14},{9,15},{10,... | collective-permute-start | bytes 589832 | tf_op jit(solution)/shard_map/ppermute | solution.py:797
  185.9 13.6 %all-to-all-start.5 = ((bf16[8,8,1152]{2,1,0:T(8,128)(2,1)}), bf16[8,8,1152]{2,1,0:T(8,128)(2,1)S(1)}, u32[]{:S(2)}, u32[]{:S(2)}) async-start(bf16[8,8,1152]{2,1,0:T(8,128)(2,1)} %bitcast.14), calls=%async_computation.5 | async-start | bytes 294912 | tf_op jit(solution)/shard_map/all_to_all | solution.py:801
  (11 other events, 21.0 us)

commit v4 on v3

--- a/solution.py
+++ b/solution.py
@@ -22,6 +22,8 @@
 PACK = 2432
 MORE = 896
 SENT = 640
+SIDE = 320
+PART = 384
 LATE = 512
 FF_TILE = 768
 PROJ = 512
@@ -179,7 +181,7 @@
 
 
 def output_kernel(idx_ref, *refs):
-    blocks, refs = refs[:8], refs[8:]
+    near, far_ref, refs = refs[:4], refs[4], refs[5:]
     wo_ref, router_ref, src_ref, dst_ref = refs
     y, c = idx_ref[0], idx_ref[1]
     for side in range(2):
@@ -187,7 +189,9 @@
             place = 2 * lax.rem(y + 4 - k, 4) + (c if side == 0 else 1 - c)
             n = 4 * side + k
             for j in range(7):
-                src_ref[n, j] = blocks[n][:, 128 * j : 128 * j + 128].astype(f32)
+                at = slice(128 * j, 128 * j + 128)
+                block = near[k][:, at] if side == 0 else far_ref[96 * k : 96 * k + 96, at]
+                src_ref[n, j] = block.astype(f32)
                 for r in range(6):
                     dst_ref[j, pl.ds(place * 6 + r, 16, stride=48), :] = src_ref[
                         n, j, pl.ds(r, 16, stride=6), :
@@ -200,10 +204,10 @@
     return call(
         output_kernel,
         [sds(WIDTH, WIDTH), sds(WIDTH, 128)],
-        [smem] + [vmem] * 8,
+        [smem] + [vmem] * 5,
         [pltpu.VMEM((8, 7, 96, 128), f32), pltpu.VMEM((7, WIDTH, 128), f32)],
         name="output_weights",
-        mib=24,
+        mib=12,
         us=3,
     )(idx, *blocks)
 
@@ -407,28 +411,19 @@
 
 
 def expert_kernel(
-    recv_ref, wi_hbm, wo_hbm, ret_ref, gi_hbm, go_hbm,
-    rf_ref, x_ref, xt_ref, g_ref, eo_ref, gx_ref, wi_ref, wo_ref, gi_ref, go_ref, in_sem, out_sem,
+    recv_ref, wi_ref, wo_ref, ret_ref, gi_hbm, go_hbm,
+    rf_ref, x_ref, xt_ref, g_ref, eo_ref, gx_ref, gi_ref, go_ref, out_sem,
 ):
     tiles = FF // FF_TILE
-    loads, stores = [], []
+    stores = []
     for i in range(tiles):
         at = pl.ds(i * FF_TILE, FF_TILE)
-        loads.append(
-            (
-                pltpu.make_async_copy(wi_hbm.at[0, :, at], wi_ref.at[i], in_sem.at[0, i]),
-                pltpu.make_async_copy(wo_hbm.at[0, at, :], wo_ref.at[i], in_sem.at[1, i]),
-            )
-        )
         stores.append(
             (
                 pltpu.make_async_copy(gi_ref.at[i], gi_hbm.at[0, :, at], out_sem.at[0, i]),
                 pltpu.make_async_copy(go_ref.at[i], go_hbm.at[0, at, :], out_sem.at[1, i]),
             )
         )
-    for pair in loads:
-        for load in pair:
-            load.start()
     fill(rf_ref, recv_ref)
     for kind, dst in enumerate((x_ref, g_ref)):
         for s in range(2):
@@ -438,10 +433,8 @@
                 ).astype(bf16)
     xt_ref[...] = x_ref[...].T
     for i in range(tiles):
-        for load in loads[i]:
-            load.wait()
-        wi = wi_ref[i]
-        wo = wo_ref[i]
+        wi = wi_ref[0, :, FF_TILE * i : FF_TILE * i + FF_TILE]
+        wo = wo_ref[0, FF_TILE * i : FF_TILE * i + FF_TILE, :]
         g = g_ref[...]
         a = mm(x_ref[...], wi)
         gu = mm_nt(g, wo)
@@ -478,7 +471,7 @@
     return pl.pallas_call(
         expert_kernel,
         out_shape=[sds(LEN, HALF), sds(1, WIDTH, FF), sds(1, FF, WIDTH)],
-        in_specs=[vmem, place, place],
+        in_specs=[vmem, vmem, vmem],
         out_specs=[vmem, place, place],
         scratch_shapes=[
             pltpu.VMEM((3, LEN, 128), f32),
@@ -489,12 +482,9 @@
             pltpu.VMEM((2 * TOK, WIDTH), f32),
             pltpu.VMEM((tiles, WIDTH, FF_TILE), bf16),
             pltpu.VMEM((tiles, FF_TILE, WIDTH), bf16),
-            pltpu.VMEM((tiles, WIDTH, FF_TILE), bf16),
-            pltpu.VMEM((tiles, FF_TILE, WIDTH), bf16),
-            pltpu.SemaphoreType.DMA((2, tiles)),
             pltpu.SemaphoreType.DMA((2, tiles)),
         ],
-        compiler_params=params(56),
+        compiler_params=params(20),
         cost_estimate=cost(12),
         name="experts",
     )(recv, w_inner, w_outer)
@@ -574,8 +564,8 @@
 def backward_kernel(
     idx_ref, g0_ref, g1_ref, g2_ref, g3_ref, x_ref, wqkv_ref, qe_ref, ke_ref, v_ref,
     band_ref, lse_ref, gain_ref,
-    own_ref, other_ref, dq_ref, line_ref, acc_ref, h_ref,
-    gs_ref, gk_ref, gv_ref,
+    own_ref, other_ref, keep_ref, give_ref, line_ref, acc_ref, h_ref,
+    gs_ref, gk_ref, gv_ref, dq_ref,
 ):
     y, c = idx_ref[0], idx_ref[1]
     for k, g_ref in enumerate((g0_ref, g1_ref, g2_ref, g3_ref)):
@@ -614,6 +604,10 @@
     lax.fori_loop(0, 4, block, 0)
     dq_ref[:, COLS : 2 * COLS] = gk_ref[...].T.astype(bf16)
     dq_ref[:, 2 * COLS :] = gv_ref[...].T.astype(bf16)
+    first = jnp.concatenate([dq_ref[:, :256], jnp.zeros((LEN, 64), bf16)], axis=1)
+    second = dq_ref[:, 256:]
+    keep_ref[...] = jnp.where(c == 0, first, second)
+    give = jnp.where(c == 0, second, first)
     lines = jnp.zeros((1, WIDTH), f32)
     for side in range(2):
         rows = []
@@ -633,11 +627,15 @@
             else:
                 other_ref[yq] = d[part].astype(bf16)
     line_ref[...] = jnp.broadcast_to(lines, (8, WIDTH))
+    for j in range(6):
+        at = slice(128 * j, 128 * j + 128)
+        give_ref[at, :SIDE] = mm_tn(h_ref[:, at], give).astype(bf16)
+    give_ref[:, SIDE:] = jnp.zeros((WIDTH, PART - SIDE), bf16)
 
 
 def attend_back(idx, go_parts, x_all, wqkv, qe, ke, v, band, lse, gains):
     outs = [
-        sds(4, TOK, WIDTH, dtype=f32), sds(4, TOK, WIDTH), sds(LEN, 3 * COLS),
+        sds(4, TOK, WIDTH, dtype=f32), sds(4, TOK, WIDTH), sds(LEN, SIDE), sds(WIDTH, PART),
         sds(8, WIDTH, dtype=f32), sds(GROUP, TOK, BAND, dtype=f32), sds(LEN, WIDTH),
     ]
     return call(
@@ -648,16 +646,15 @@
             pltpu.VMEM((4, TOK, COLS), bf16),
             pltpu.VMEM((COLS, LEN), f32),
             pltpu.VMEM((COLS, LEN), f32),
+            pltpu.VMEM((LEN, 3 * COLS), bf16),
         ],
         name="attend_back",
-        mib=24,
+        mib=26,
         us=12,
     )(idx, *go_parts, x_all, wqkv, qe, ke, v, band, lse, gains)
 
 
-def terms_kernel(
-    idx_ref, h_ref, dq_ref, line_ref, dgain_ref, acc_ref, keep_ref, got_ref, send_ref
-):
+def kept_kernel(idx_ref, h_ref, dq_ref, line_ref, dgain_ref, acc_ref, kept_ref):
     y = idx_ref[0]
     ids = bucket_of(iota((512, 128), 0) - 255)
     flat = iota((512, 128), 1)
@@ -693,31 +690,32 @@
         high = v.astype(bf16).astype(f32)
         lines += [high, v - high]
     block = jnp.concatenate(lines + [jnp.zeros((122, WIDTH), f32)], axis=0).T
-    block = jnp.concatenate([jnp.zeros((WIDTH, 64), f32), block[:, :64]], axis=1)
-    send_ref[:, 512:SENT] = block.astype(bf16)
-    send_ref[:, SENT:] = (keep_ref[...].astype(f32) + got_ref[...].astype(f32)).astype(bf16)
-
-    def weights(j, _):
-        at = pl.ds(pl.multiple_of(j * 128, 128), 128)
-        terms = mm_tn(h_ref[:, at], dq_ref[...])
-        send_ref[at, :512] = terms[:, :512].astype(bf16)
-        extra = send_ref[at, 512:SENT].astype(f32)
-        last = jnp.concatenate([terms[:, 512:], extra[:, 64:]], axis=1)
-        send_ref[at, 512:SENT] = last.astype(bf16)
-        return 0
-
-    lax.fori_loop(0, 6, weights, 0, unroll=6)
-
-
-def weight_terms(idx, h, dq, line, dgain, acc, keep, got):
+    kept_ref[:, SIDE:] = block[:, :64]
+    for j in range(6):
+        at = slice(128 * j, 128 * j + 128)
+        kept_ref[at, :SIDE] = mm_tn(h_ref[:, at], dq_ref[...])
+
+
+def kept_terms(idx, h, dq, line, dgain, acc):
     return call(
-        terms_kernel,
-        [sds(WIDTH, SENT + LATE)],
-        [smem] + [vmem] * 7,
-        name="weight_terms",
-        mib=14,
-        us=5,
-    )(idx, h, dq, line, dgain, acc, keep, got)[0]
+        kept_kernel,
+        [sds(WIDTH, PART, dtype=f32)],
+        [smem] + [vmem] * 5,
+        name="kept_terms",
+        mib=12,
+        us=4,
+    )(idx, h, dq, line, dgain, acc)[0]
+
+
+def joined_kernel(kept_ref, got_ref, keep_ref, late_ref, out_ref):
+    out_ref[:, :PART] = (kept_ref[...] + got_ref[...].astype(f32)).astype(bf16)
+    out_ref[:, PART:] = (keep_ref[...].astype(f32) + late_ref[...].astype(f32)).astype(bf16)
+
+
+def joined_terms(kept, got, keep, late):
+    return call(
+        joined_kernel, [sds(WIDTH, PART + LATE)], [vmem] * 4, name="joined_terms", mib=8
+    )(kept, got, keep, late)[0]
 
 
 def pair_kernel(idx_ref, own_ref, got_ref, d0_ref, d1_ref, d2_ref, d3_ref):
@@ -754,16 +752,16 @@
             sums = sums + got_ref[48 * f : 48 * f + 48, a:b].astype(f32)
         return sums
 
-    pieces = [total(0, 512)]
-    last = total(512, SENT)
+    pieces = [total(0, 256)]
+    last = total(256, PART)
     lane = iota((48, 128), 1)
     both = last + pltpu.roll(last, 127, 1)
     high = both.astype(bf16).astype(f32)
     rest = pltpu.roll(both - high, 1, 1)
     last = jnp.where(lane < 64, last, jnp.where(lane % 2 == 0, high, rest))
-    pieces += [last, total(SENT, SENT + LATE)]
+    pieces += [last, total(PART, PART + LATE)]
     sums = jnp.concatenate(pieces, axis=1)
-    blank = jnp.zeros((2, SENT + LATE), f32)
+    blank = jnp.zeros((2, PART + LATE), f32)
     rows = []
     for s in range(8):
         rows += [sums[6 * s : 6 * s + 6], blank]
@@ -771,21 +769,23 @@
 
 
 def middle_sums(got):
-    return call(middle_kernel, [sds(64, SENT + LATE)], [vmem], name="middle_sums", mib=8)(got)[0]
+    return call(middle_kernel, [sds(64, PART + LATE)], [vmem], name="middle_sums", mib=8)(got)[0]
 
 
 def sums_kernel(recv_ref, q_ref, k_ref, v_ref, o_ref, router_ref, small_ref):
     got = recv_ref[...].astype(f32)
     parts = [got[8 * s : 8 * s + 8] for s in range(8)]
-    quads = [parts[2 * y] + parts[2 * y + 1] for y in range(4)]
+    quads = [
+        jnp.concatenate([parts[2 * y][:, :256], parts[2 * y + 1][:, :SIDE]], axis=1) for y in range(4)
+    ]
     for m, ref in enumerate((q_ref, k_ref, v_ref)):
         cols = jnp.concatenate([a[:, COLS * m : COLS * m + COLS] for a in quads], axis=1)
         ref[...] = cols[:6].astype(bf16)
     halves = [parts[c] + parts[2 + c] + parts[4 + c] + parts[6 + c] for c in range(2)]
-    o_ref[...] = jnp.concatenate([a[:6, SENT : SENT + HALF] for a in halves], axis=1).astype(bf16)
-    routed = [a[:6, SENT + HALF : SENT + HALF + 64] for a in halves]
+    o_ref[...] = jnp.concatenate([a[:6, PART : PART + HALF] for a in halves], axis=1).astype(bf16)
+    routed = [a[:6, PART + HALF : PART + HALF + 64] for a in halves]
     router_ref[...] = jnp.concatenate(routed, axis=1).astype(bf16)
-    small_ref[...] = halves[0][:, 512:SENT] + halves[1][:, 512:SENT]
+    small_ref[...] = halves[0][:, 256:PART] + halves[1][:, 256:PART]
 
 
 def sums_last(recv):
@@ -822,7 +822,7 @@
     attended = attend(idx, heads, segments.reshape(LEN, 1), blocks)
     more = [more] + [along_y(more, k) for k in (1, 2, 3)]
     more, attended = lax.optimization_barrier((more, attended))
-    wo, router = output_weights(idx, more + [other_core(b) for b in more])
+    wo, router = output_weights(idx, more + [other_core(jnp.concatenate(more, axis=0))])
     o_parts = attended[:4]
     gains, lse, wqkv, band, x_all, qe, ke, v = attended[4:]
     o_parts = [o_parts[0]] + [along_y(o_parts[k], k) for k in (1, 2, 3)]
@@ -837,11 +837,13 @@
     go_parts = [more[0]] + [along_y(more[k], k) for k in (1, 2, 3)]
     keep, give, dgain = more[4:]
     late = other_core(give)
-    own, other, dq_all, line, acc, h = attend_back(
+    own, other, dq_keep, give_terms, line, acc, h = attend_back(
         idx, go_parts, x_all, wqkv, qe, ke, v, band, lse, gains
     )
+    got_terms = other_core(give_terms)
+    kept = kept_terms(idx, h, dq_keep, line, dgain, acc)
+    terms = joined_terms(kept, got_terms, keep, late)
     got = other_core(other)
-    terms = weight_terms(idx, h, dq_all, line, dgain, acc, keep, late)
     d_parts = pair_sum(idx, own, got)
     d_parts = [d_parts[0]] + [along_y(d_parts[k], k) for k in (1, 2, 3)]
     sums = exchange(middle_sums(exchange(terms, "fsdp")), "seq")

time: 203 us -> 201 us (level)
  waiting for transfers between devices: 38.8 us -> 44 us
  starting transfers between devices: 50.8 us -> 46.7 us
  Pallas kernels: 53.7 us -> 50.5 us
    all_to_all x4, waiting for transfers between devices: 33.2 us -> 38.2 us  [exchange(): return lax.all_to_all(v, axes, split_axis=0, concat_axis=0, tiled=True)]
    all_to_all x4, starting transfers between devices: 25.5 us -> 21.8 us  [exchange(): return lax.all_to_all(v, axes, split_axis=0, concat_axis=0, tiled=True)]
    pallas_call x1, Pallas kernels: 13 us -> 9.43 us  [experts(): pl.pallas_call(expert_kernel, out_shape=[sds(LEN, HALF), sds(1, WIDTH, FF...]
    pallas_call x2 -> x3, Pallas kernels: 5.6 us -> 4.88 us  [the longest x1 2.6 us: kept_terms(): call(kept_kernel, [sds(WIDTH, PART, dtype=f32)], [smem] + [vmem] * 5, nam...]
    unnamed x61 -> x69, local copies, waits for them, and re-layouts: 6.25 us -> 6.85 us
    ppermute x10 -> x8, starting transfers between devices: 7.7 us -> 7.25 us  [other_core(): return lax.ppermute(v, 'seq', [(s, s ^ 1) for s in range(8)])]
  transfers between devices with their start and end apart: 29 -> 27, of which waited for: 11 -> 10; matrix products, arithmetic and copies ran while one was open for 1% -> 1% of each run, Pallas kernels for 15% -> 16%
where the time goes in v4:
time: 201 us; the launch traced here: 200 us
  Pallas kernels  50.5 us (25%)
  starting transfers between devices  46.7 us (23%)
  blocking collectives  46 us (23%)
  waiting for transfers between devices  44 us (22%)
  local copies, waits for them, and re-layouts  9.51 us (5%)
    all_to_all x2, blocking collectives, exchange(): return lax.all_to_all(v, axes, split_axis=0, concat_axis=0, tiled=True)  46 us
    all_to_all x4, waiting for transfers between devices, exchange(): return lax.all_to_all(v, axes, split_axis=0, concat_axis=0, tiled=True)  38.2 us
    all_to_all x4, starting transfers between devices, exchange(): return lax.all_to_all(v, axes, split_axis=0, concat_axis=0, tiled=True)  21.8 us
    ppermute x15, starting transfers between devices, along_y(): return lax.ppermute(v, 'seq', [(s, (s + 2 * k) % 8) for s in range(8)])  17.7 us
    pallas_call x1, Pallas kernels, attend(): pl.pallas_call(attend_kernel, out_shape=outs + saved, in_specs=[smem, vme...  12.2 us
    pallas_call x1, Pallas kernels, attend_back(): call(backward_kernel, outs, [smem] + [vmem] * 12, [pltpu.VMEM((4, TOK, CO...  11.3 us
    pallas_call x1, Pallas kernels, experts(): pl.pallas_call(expert_kernel, out_shape=[sds(LEN, HALF), sds(1, WIDTH, FF...  9.43 us
    ppermute x8, starting transfers between devices, other_core(): return lax.ppermute(v, 'seq', [(s, s ^ 1) for s in range(8)])  7.25 us
  transfers between devices with their start and end apart: 27, of which 10 were waited for; matrix products, arithmetic and copies ran while one was open for 1% of the time, Pallas kernels for 16%

profile of v4, /device:TPU:1, one launch (start us, length us, event | category | flops | bytes accessed | tf_op | source)
XLA Modules:
  0.0 199.8 jit_solution(16751777336465338480)
XLA Ops:
  0.7 1.3 maximum_bitcast_fusion.small_ref
  1.9 1.7 pack_weights.1
  3.6 8.4 %all-to-all-start = ((bf16[16,8,2432]{2,1,0:T(8,128)(2,1)}), bf16[16,8,2432]{2,1,0:T(8,128)(2,1)S(1)}, u32[]{:S(2)}, u32[]{:S(2)}) async-start(bf16[16,8,2432]{2,1,0:T(8,128)(2,1)} %bitcast.28), calls=%async_computation | async-start | bytes 1245184 | tf_op jit(solution)/shard_map/all_to_all | solution.py:801
  12.1 1.0 collective-permute-start.3
  13.1 2.7 %collective-permute-start.2 = (bf16[128,768]{1,0:T(8,128)(2,1)S(1)}, bf16[128,768]{1,0:T(8,128)(2,1)S(1)}, u32[]{:S(2)}, u32[]{:S(2)}) collective-permute-start(bf16[128,768]{1,0:T(8,128)(2,1)S(1)} %copy-done.3), channel_id=1, source_target_pairs={{0,6},{1,7},{2,0},{3,1},{4,2},{5,3},{6,4},{7,5},{8,14},{9,15},{10,... | collective-permute-start | bytes 589832 | tf_op jit(solution)/shard_map/ppermute | solution.py:797
  16.2 0.7 collective-permute-start
  16.9 6.6 %all-to-all-done = bf16[16,8,2432]{2,1,0:T(8,128)(2,1)S(1)} async-done(((bf16[16,8,2432]{2,1,0:T(8,128)(2,1)}), bf16[16,8,2432]{2,1,0:T(8,128)(2,1)S(1)}, u32[]{:S(2)}, u32[]{:S(2)}) %all-to-all-start) | async-done | bytes 622624 | tf_op jit(solution)/shard_map/all_to_all | solution.py:801
  23.5 0.8 copy-done.19
  24.3 2.5 %split_weights.1 = (bf16[768,640]{1,0:T(8,128)(2,1)}, bf16[96,896]{1,0:T(8,128)(2,1)}) custom-call(bf16[128,2432]{1,0:T(8,128)(2,1)} %bitcast.27), custom_call_target="tpu_custom_call" | custom-call | flops 2300000000 | bytes 1048576 | tf_op jit(solution)/shard_map/split_weights/pallas_call | solution.py:169
  26.8 1.5 collective-permute-done.refs_1_
  28.4 5.2 %all-to-all-start.1 = ((bf16[8,96,640]{2,1,0:T(8,128)(2,1)}), bf16[8,96,640]{2,1,0:T(8,128)(2,1)S(1)}, u32[]{:S(2)}, u32[]{:S(2)}) async-start(bf16[8,96,640]{2,1,0:T(8,128)(2,1)} %bitcast.26), calls=%async_computation.1 | async-start | bytes 1966080 | tf_op jit(solution)/shard_map/all_to_all | solution.py:801
  34.1 1.0 copy.27.seg_ref
  35.7 12.3 %all-to-all-done.1 = bf16[8,96,640]{2,1,0:T(8,128)(2,1)S(1)} async-done(((bf16[8,96,640]{2,1,0:T(8,128)(2,1)}), bf16[8,96,640]{2,1,0:T(8,128)(2,1)S(1)}, u32[]{:S(2)}, u32[]{:S(2)}) %all-to-all-start.1) | async-done | bytes 983072 | tf_op jit(solution)/shard_map/all_to_all | solution.py:801
  48.0 0.9 collective-permute-start.6
  48.9 1.2 collective-permute-start.5
  51.5 12.2 %attend.1 = (bf16[128,192]{1,0:T(8,128)(2,1)}, bf16[128,192]{1,0:T(8,128)(2,1)}, bf16[128,192]{1,0:T(8,128)(2,1)}, bf16[128,192]{1,0:T(8,128)(2,1)}, f32[8,768]{...) custom-call(s32[2]{0:T(128)} %pad_add_fusion.idx_ref, ...), custom_call_target="tpu_custom_call" | custom-call | flops 16099999744 | bytes 1048576 | tf_op jit(solution)/shard_map/attend/pallas_call | solution.py:343
  63.9 1.5 collective-permute-start.13
  65.6 1.7 collective-permute-start.10
  67.3 2.4 %collective-permute-start.11 = (bf16[128,192]{1,0:T(8,128)(2,1)S(1)}, bf16[128,192]{1,0:T(8,128)(2,1)S(1)}, u32[]{:S(2)}, u32[]{:S(2)}) collective-permute-start(bf16[128,192]{1,0:T(8,128)(2,1)S(1)} %copy-done.30), channel_id=1, source_target_pairs={{0,4},{1,5},{2,6},{3,7},{4,0},{5,1},{6,2},{7,3},{8,12},{9,13},{10,... | collective-permute-start | bytes 147464 | tf_op jit(solution)/shard_map/ppermute | solution.py:797
  69.7 1.2 collective-permute-start.12
  70.9 1.7 output_weights.1
  73.2 2.0 %dispatch.1 = (f32[128,768]{1,0:T(8,128)S(1)}, bf16[128,768]{1,0:T(8,128)(2,1)S(1)}, f32[128,128]{1,0:T(8,128)S(1)}, bf16[2,128,128]{2,1,0:T(8,128)(2,1)S(1)}, bf16[1024,384]{1,0:T(8,128)(2,1)S(1)}) custom-call(s32[2]{0:T(128)S(1)} %copy-done.5, bf16[128,768]{1,0:T(8,128)(2,1)S(1)} %copy-done.4, bf16[128,192]{1,0:T(8,128)(2,1)S(1)} %copy-done.8, ...), custom_call_target="tpu_custom_call" | custom-call | flops 2300000000 | bytes 1048576 | tf_op jit(solution)/shard_map/dispatch/pallas_call | solution.py:403
  75.2 25.4 %all_to_all.67 = bf16[128,8,384]{2,1,0:T(8,128)(2,1)S(1)} all-to-all(bf16[128,8,384]{2,1,0:T(8,128)(2,1)S(1)} %bitcast.19), channel_id=1, replica_groups=mesh['fsdp'=16,'seq'=8] {'fsdp','seq'}, dimensions={0} | all-to-all | bytes 1572864 | tf_op jit(solution)/shard_map/all_to_all | solution.py:801
  100.6 2.3 %copy-done.1 = bf16[1,3072,768]{2,1,0:T(8,128)(2,1)S(1)} copy-done((bf16[1,3072,768]{2,1,0:T(8,128)(2,1)S(1)}, bf16[1,3072,768]{2,1,0:T(8,128)(2,1)}, u32[]{:S(2)}) %copy-start.1) | copy-done | bytes 4718616
  102.9 9.4 %experts.1 = (bf16[1024,384]{1,0:T(8,128)(2,1)S(1)}, bf16[1,768,3072]{2,1,0:T(8,128)(2,1)}, bf16[1,3072,768]{2,1,0:T(8,128)(2,1)}) custom-call(bf16[1024,384]{1,0:T(8,128)(2,1)S(1)} %bitcast.20, bf16[1,768,3072]{2,1,0:T(8,128)(2,1)S(1)} %bitcast.24, bf16[1,3072,768]{2,1,0:T(8,128)(2,1)S(1)} %copy-done.1), custom_call_target="tpu_custom_call" | custom-call | flops 13799999488 | bytes 1048576 | tf_op jit(solution)/shard_map/experts/pallas_call | solution.py:471
  112.4 20.6 %all_to_all.68 = bf16[128,8,384]{2,1,0:T(8,128)(2,1)S(1)} all-to-all(bf16[128,8,384]{2,1,0:T(8,128)(2,1)S(1)} %bitcast.21), channel_id=1, replica_groups=mesh['fsdp'=16,'seq'=8] {'fsdp','seq'}, dimensions={0} | all-to-all | bytes 1572864 | tf_op jit(solution)/shard_map/all_to_all | solution.py:801
  133.0 2.4 %returned.1 = (bf16[128,768]{1,0:T(8,128)(2,1)}, f32[128,768]{1,0:T(8,128)S(1)}, bf16[128,192]{1,0:T(8,128)(2,1)S(1)}, bf16[128,192]{1,0:T(8,128)(2,1)S(1)}, bf1...) custom-call(s32[2]{0:T(128)S(1)} %copy-done.5, ...), custom_call_target="tpu_custom_call" | custom-call | flops 2300000000 | bytes 1048576 | tf_op jit(solution)/shard_map/returned/pallas_call | solution.py:554
  135.5 2.1 %collective-permute-start.15 = (bf16[128,192]{1,0:T(8,128)(2,1)S(1)}, bf16[128,192]{1,0:T(8,128)(2,1)S(1)}, u32[]{:S(2)}, u32[]{:S(2)}) collective-permute-start(bf16[128,192]{1,0:T(8,128)(2,1)S(1)} %get-tuple-element.128), channel_id=1, source_target_pairs={{0,4},{1,5},{2,6},{3,7},{4,0},{5,1},{6,2},{7,3},{8,12},{9,13},{10,... | collective-permute-start | bytes 147464 | tf_op jit(solution)/shard_map/ppermute | solution.py:797
  137.6 0.7 collective-permute-start.16
  138.3 1.6 collective-permute-start.22
  141.4 11.3 %attend_back.1 = (f32[4,128,768]{2,1,0:T(8,128)S(1)}, bf16[4,128,768]{2,1,0:T(8,128)(2,1)S(1)}, bf16[1024,320]{1,0:T(8,128)(2,1)S(1)}, bf16[768,384]{1,0:T(8,128...) custom-call(s32[2]{0:T(128)S(1)} %copy-done.5, ...), custom_call_target="tpu_custom_call" | custom-call | flops 13799999488 | bytes 1048576 | tf_op jit(solution)/shard_map/attend_back/pallas_call | solution.py:641
  152.7 2.5 %collective-permute-start.21 = (bf16[768,384]{1,0:T(8,128)(2,1)S(1)}, bf16[768,384]{1,0:T(8,128)(2,1)S(1)}, u32[]{:S(2)}, u32[]{:S(2)}) collective-permute-start(bf16[768,384]{1,0:T(8,128)(2,1)S(1)} %get-tuple-element.149), channel_id=1, source_target_pairs={{0,1},{1,0},{2,3},{3,2},{4,5},{5,4},{6,7},{7,6},{8,9},{9,8},{10,11... | collective-permute-start | bytes 1769480 | tf_op jit(solution)/shard_map/ppermute | solution.py:805
  155.2 2.6 %kept_terms.1.kept_ref = f32[768,384]{1,0:T(8,128)S(1)} custom-call(s32[2]{0:T(128)S(1)} %copy-done.5, bf16[1024,768]{1,0:T(8,128)(2,1)S(1)} %get-tuple-element.144.h_ref, bf16[1024,320]{1,0:T(8,128)(2,1)S(1)} %get-tuple-element.145.dq_ref, f32[8,768]{1,0:T(8,128)S(1)} %get-tuple-element.146.line_ref, f32[8,768]{1,0:T(8,128)S(1)} %get-tuple-element.147.dgain_ref, ...), custom_call_target="tpu_custom_call" | custom-call | flops 4600000000 | bytes 1048576 | tf_op jit(solution)/shard_map/kept_terms/pallas_call | solution.py:700
  157.8 1.4 joined_terms.1
  159.2 3.7 %all-to-all-start.4 = ((bf16[16,48,896]{2,1,0:T(8,128)(2,1)}), bf16[16,48,896]{2,1,0:T(8,128)(2,1)S(1)}, u32[]{:S(2)}, u32[]{:S(2)}) async-start(bf16[16,48,896]{2,1,0:T(8,128)(2,1)} %bitcast.12), calls=%async_computation.4 | async-start | bytes 2752512 | tf_op jit(solution)/shard_map/all_to_all | solution.py:801
  163.0 2.3 %collective-permute-done.17.got_ref = bf16[4,128,768]{2,1,0:T(8,128)(2,1)S(1)} collective-permute-done((bf16[4,128,768]{2,1,0:T(8,128)(2,1)S(1)}, bf16[4,128,768]{2,1,0:T(8,128)(2,1)S(1)}, u32[]{:S(2)}, u32[]{:S(2)}) %collective-permute-start.17) | collective-permute-done | bytes 786464 | tf_op jit(solution)/shard_map/ppermute | solution.py:805
  165.2 1.4 copy-done.7
  167.3 1.1 collective-permute-start.18
  168.4 2.2 %collective-permute-start.19 = (bf16[128,768]{1,0:T(8,128)(2,1)S(1)}, bf16[128,768]{1,0:T(8,128)(2,1)S(1)}, u32[]{:S(2)}, u32[]{:S(2)}) collective-permute-start(bf16[128,768]{1,0:T(8,128)(2,1)S(1)} %get-tuple-element.141), channel_id=1, source_target_pairs={{0,4},{1,5},{2,6},{3,7},{4,0},{5,1},{6,2},{7,3},{8,12},{9,13},{10,... | collective-permute-start | bytes 589832 | tf_op jit(solution)/shard_map/ppermute | solution.py:797
  170.9 16.0 %all-to-all-done.4 = bf16[16,48,896]{2,1,0:T(8,128)(2,1)S(1)} async-done(((bf16[16,48,896]{2,1,0:T(8,128)(2,1)}), bf16[16,48,896]{2,1,0:T(8,128)(2,1)S(1)}, u32[]{:S(2)}, u32[]{:S(2)}) %all-to-all-start.4) | async-done | bytes 1376288 | tf_op jit(solution)/shard_map/all_to_all | solution.py:801
  186.9 0.9 middle_sums.1
  187.8 4.4 %all-to-all-start.5 = ((bf16[8,8,896]{2,1,0:T(8,128)(2,1)}), bf16[8,8,896]{2,1,0:T(8,128)(2,1)S(1)}, u32[]{:S(2)}, u32[]{:S(2)}) async-start(bf16[8,8,896]{2,1,0:T(8,128)(2,1)} %bitcast.14), calls=%async_computation.5 | async-start | bytes 229376 | tf_op jit(solution)/shard_map/all_to_all | solution.py:801
  192.3 0.7 copy-done.10
  193.1 1.0 tokens_last.1
  194.1 3.3 %all-to-all-done.5 = bf16[8,8,896]{2,1,0:T(8,128)(2,1)S(1)} async-done(((bf16[8,8,896]{2,1,0:T(8,128)(2,1)}), bf16[8,8,896]{2,1,0:T(8,128)(2,1)S(1)}, u32[]{:S(2)}, u32[]{:S(2)}) %all-to-all-start.5) | async-done | bytes 114720 | tf_op jit(solution)/shard_map/all_to_all | solution.py:801
  197.4 0.7 sums_last.1
  198.3 0.7 slice_reduce_fusion.2
  199.1 0.7 slice_reduce_fusion
  (103 shorter events, 6.3 us)
Async XLA Ops:
  1.9 10.1 %copy-start.3 = (bf16[128,768]{1,0:T(8,128)(2,1)S(1)}, bf16[128,768]{1,0:T(8,128)(2,1)}, u32[]{:S(2)}) copy-start(bf16[128,768]{1,0:T(8,128)(2,1)} %x_ref.3) | copy-start | bytes 589828
  3.6 19.9 %all-to-all-start = ((bf16[16,8,2432]{2,1,0:T(8,128)(2,1)}), bf16[16,8,2432]{2,1,0:T(8,128)(2,1)S(1)}, u32[]{:S(2)}, u32[]{:S(2)}) async-start(bf16[16,8,2432]{2,1,0:T(8,128)(2,1)} %bitcast.28), calls=%async_computation | async-start | bytes 1245184 | tf_op jit(solution)/shard_map/all_to_all | solution.py:801
  12.1 14.7 %collective-permute-start.3 = (bf16[128,768]{1,0:T(8,128)(2,1)S(1)}, bf16[128,768]{1,0:T(8,128)(2,1)S(1)}, u32[]{:S(2)}, u32[]{:S(2)}) collective-permute-start(bf16[128,768]{1,0:T(8,128)(2,1)S(1)} %copy-done.3), channel_id=1, source_target_pairs={{0,1},{1,0},{2,3},{3,2},{4,5},{5,4},{6,7},{7,6},{8,9},{9,8},{10,11... | collective-permute-start | bytes 589832 | tf_op jit(solution)/shard_map/ppermute | solution.py:805
  13.1 13.7 %collective-permute-start.2 = (bf16[128,768]{1,0:T(8,128)(2,1)S(1)}, bf16[128,768]{1,0:T(8,128)(2,1)S(1)}, u32[]{:S(2)}, u32[]{:S(2)}) collective-permute-start(bf16[128,768]{1,0:T(8,128)(2,1)S(1)} %copy-done.3), channel_id=1, source_target_pairs={{0,6},{1,7},{2,0},{3,1},{4,2},{5,3},{6,4},{7,5},{8,14},{9,15},{10,... | collective-permute-start | bytes 589832 | tf_op jit(solution)/shard_map/ppermute | solution.py:797
  15.8 11.0 %collective-permute-start.1 = (bf16[128,768]{1,0:T(8,128)(2,1)S(1)}, bf16[128,768]{1,0:T(8,128)(2,1)S(1)}, u32[]{:S(2)}, u32[]{:S(2)}) collective-permute-start(bf16[128,768]{1,0:T(8,128)(2,1)S(1)} %copy-done.3), channel_id=1, source_target_pairs={{0,4},{1,5},{2,6},{3,7},{4,0},{5,1},{6,2},{7,3},{8,12},{9,13},{10,... | collective-permute-start | bytes 589832 | tf_op jit(solution)/shard_map/ppermute | solution.py:797
  16.2 12.2 %collective-permute-start = (bf16[128,768]{1,0:T(8,128)(2,1)S(1)}, bf16[128,768]{1,0:T(8,128)(2,1)S(1)}, u32[]{:S(2)}, u32[]{:S(2)}) collective-permute-start(bf16[128,768]{1,0:T(8,128)(2,1)S(1)} %copy-done.3), channel_id=1, source_target_pairs={{0,2},{1,3},{2,4},{3,5},{4,6},{5,7},{6,0},{7,1},{8,10},{9,11},{10,... | collective-permute-start | bytes 589832 | tf_op jit(solution)/shard_map/ppermute | solution.py:797
  26.8 7.3 %copy-start.20 = (s32[1,1024]{1,0:T(1,128)S(1)}, s32[1,1024]{1,0:T(1,128)}, u32[]{:S(2)}) copy-start(s32[1,1024]{1,0:T(1,128)} %param.15) | copy-start | bytes 12292
  26.8 21.2 %copy-start = (bf16[96,896]{1,0:T(8,128)(2,1)S(1)}, bf16[96,896]{1,0:T(8,128)(2,1)}, u32[]{:S(2)}) copy-start(bf16[96,896]{1,0:T(8,128)(2,1)} %get-tuple-element.112.refs_0_) | copy-start | bytes 516100
  26.8 23.3 %copy-start.22 = (bf16[128,768]{1,0:T(8,128)(2,1)}, bf16[128,768]{1,0:T(8,128)(2,1)S(1)}, u32[]{:S(2)}) copy-start(bf16[128,768]{1,0:T(8,128)(2,1)S(1)} %collective-permute-done.3.refs_4_) | copy-start | bytes 589828
  26.8 23.3 %copy-start.23 = (bf16[128,768]{1,0:T(8,128)(2,1)}, bf16[128,768]{1,0:T(8,128)(2,1)S(1)}, u32[]{:S(2)}) copy-start(bf16[128,768]{1,0:T(8,128)(2,1)S(1)} %collective-permute-done.2.refs_3_) | copy-start | bytes 589828
  26.8 23.3 %copy-start.24 = (bf16[128,768]{1,0:T(8,128)(2,1)}, bf16[128,768]{1,0:T(8,128)(2,1)S(1)}, u32[]{:S(2)}) copy-start(bf16[128,768]{1,0:T(8,128)(2,1)S(1)} %collective-permute-done.1.refs_2_) | copy-start | bytes 589828
  28.4 21.8 %copy-start.25 = (bf16[128,768]{1,0:T(8,128)(2,1)}, bf16[128,768]{1,0:T(8,128)(2,1)S(1)}, u32[]{:S(2)}) copy-start(bf16[128,768]{1,0:T(8,128)(2,1)S(1)} %collective-permute-done.refs_1_) | copy-start | bytes 589828
  28.4 19.6 %all-to-all-start.1 = ((bf16[8,96,640]{2,1,0:T(8,128)(2,1)}), bf16[8,96,640]{2,1,0:T(8,128)(2,1)S(1)}, u32[]{:S(2)}, u32[]{:S(2)}) async-start(bf16[8,96,640]{2,1,0:T(8,128)(2,1)} %bitcast.26), calls=%async_computation.1 | async-start | bytes 1966080 | tf_op jit(solution)/shard_map/all_to_all | solution.py:801
  33.6 16.5 %collective-permute-start.7 = (bf16[128,768]{1,0:T(8,128)(2,1)S(1)}, bf16[128,768]{1,0:T(8,128)(2,1)S(1)}, u32[]{:S(2)}, u32[]{:S(2)}) collective-permute-start(bf16[128,768]{1,0:T(8,128)(2,1)S(1)} %collective-permute-done.refs_1_), channel_id=1, source_target_pairs={{0,1},{1,0},{2,3},{3,2},{4,5},{5,4},{6,7},{7,6},{8,9},{9,8},{10,11... | collective-permute-start | bytes 589832 | tf_op jit(solution)/shard_map/ppermute | solution.py:805
  33.6 16.5 %collective-permute-start.8 = (bf16[128,768]{1,0:T(8,128)(2,1)S(1)}, bf16[128,768]{1,0:T(8,128)(2,1)S(1)}, u32[]{:S(2)}, u32[]{:S(2)}) collective-permute-start(bf16[128,768]{1,0:T(8,128)(2,1)S(1)} %collective-permute-done.1.refs_2_), channel_id=1, source_target_pairs={{0,1},{1,0},{2,3},{3,2},{4,5},{5,4},{6,7},{7,6},{8,9},{9,8},{10,11... | collective-permute-start | bytes 589832 | tf_op jit(solution)/shard_map/ppermute | solution.py:805
  34.1 16.0 %collective-permute-start.9 = (bf16[128,768]{1,0:T(8,128)(2,1)S(1)}, bf16[128,768]{1,0:T(8,128)(2,1)S(1)}, u32[]{:S(2)}, u32[]{:S(2)}) collective-permute-start(bf16[128,768]{1,0:T(8,128)(2,1)S(1)} %collective-permute-done.2.refs_3_), channel_id=1, source_target_pairs={{0,1},{1,0},{2,3},{3,2},{4,5},{5,4},{6,7},{7,6},{8,9},{9,8},{10,11... | collective-permute-start | bytes 589832 | tf_op jit(solution)/shard_map/ppermute | solution.py:805
  48.0 15.8 %collective-permute-start.6 = (bf16[96,896]{1,0:T(8,128)(2,1)S(1)}, bf16[96,896]{1,0:T(8,128)(2,1)S(1)}, u32[]{:S(2)}, u32[]{:S(2)}) collective-permute-start(bf16[96,896]{1,0:T(8,128)(2,1)S(1)} %copy-done), channel_id=1, source_target_pairs={{0,6},{1,7},{2,0},{3,1},{4,2},{5,3},{6,4},{7,5},{8,14},{9,15},{10,... | collective-permute-start | bytes 516104 | tf_op jit(solution)/shard_map/ppermute | solution.py:797
  48.9 14.9 %collective-permute-start.5 = (bf16[96,896]{1,0:T(8,128)(2,1)S(1)}, bf16[96,896]{1,0:T(8,128)(2,1)S(1)}, u32[]{:S(2)}, u32[]{:S(2)}) collective-permute-start(bf16[96,896]{1,0:T(8,128)(2,1)S(1)} %copy-done), channel_id=1, source_target_pairs={{0,4},{1,5},{2,6},{3,7},{4,0},{5,1},{6,2},{7,3},{8,12},{9,13},{10,... | collective-permute-start | bytes 516104 | tf_op jit(solution)/shard_map/ppermute | solution.py:797
  50.1 13.7 %collective-permute-start.4 = (bf16[96,896]{1,0:T(8,128)(2,1)S(1)}, bf16[96,896]{1,0:T(8,128)(2,1)S(1)}, u32[]{:S(2)}, u32[]{:S(2)}) collective-permute-start(bf16[96,896]{1,0:T(8,128)(2,1)S(1)} %copy-done), channel_id=1, source_target_pairs={{0,2},{1,3},{2,4},{3,5},{4,6},{5,7},{6,0},{7,1},{8,10},{9,11},{10,... | collective-permute-start | bytes 516104 | tf_op jit(solution)/shard_map/ppermute | solution.py:797
  63.8 7.1 %copy-start.5 = (s32[2]{0:T(128)S(1)}, s32[2]{0:T(128)}, u32[]{:S(2)}) copy-start(s32[2]{0:T(128)} %pad_add_fusion.idx_ref) | copy-start | bytes 28
  63.9 7.0 %collective-permute-start.13 = (bf16[384,896]{1,0:T(8,128)(2,1)S(1)}, bf16[384,896]{1,0:T(8,128)(2,1)S(1)}, u32[]{:S(2)}, u32[]{:S(2)}) collective-permute-start(bf16[384,896]{1,0:T(8,128)(2,1)S(1)} %pad_maximum_fusion), channel_id=1, source_target_pairs={{0,1},{1,0},{2,3},{3,2},{4,5},{5,4},{6,7},{7,6},{8,9},{9,8},{10,11... | collective-permute-start | bytes 2064392 | tf_op jit(solution)/shard_map/ppermute | solution.py:805
  65.5 7.6 %copy-start.2 = (bf16[128,768]{1,0:T(8,128)(2,1)S(1)}, bf16[128,768]{1,0:T(8,128)(2,1)}, u32[]{:S(2)}) copy-start(bf16[128,768]{1,0:T(8,128)(2,1)} %cot_ref.3) | copy-start | bytes 589828
  65.5 7.6 %copy-start.4 = (bf16[128,768]{1,0:T(8,128)(2,1)S(1)}, bf16[128,768]{1,0:T(8,128)(2,1)}, u32[]{:S(2)}) copy-start(bf16[128,768]{1,0:T(8,128)(2,1)} %x_ref.3) | copy-start | bytes 589828
  65.6 7.6 %copy-start.8 = (bf16[128,192]{1,0:T(8,128)(2,1)S(1)}, bf16[128,192]{1,0:T(8,128)(2,1)}, u32[]{:S(2)}) copy-start(bf16[128,192]{1,0:T(8,128)(2,1)} %get-tuple-element.108.o0_ref) | copy-start | bytes 147460
  65.6 7.6 %copy-start.9 = (f32[8,768]{1,0:T(8,128)S(1)}, f32[8,768]{1,0:T(8,128)}, u32[]{:S(2)}) copy-start(f32[8,768]{1,0:T(8,128)} %get-tuple-element.118.gain_ref) | copy-start | bytes 73732
  65.6 7.0 %collective-permute-start.10 = (bf16[128,192]{1,0:T(8,128)(2,1)S(1)}, bf16[128,192]{1,0:T(8,128)(2,1)S(1)}, u32[]{:S(2)}, u32[]{:S(2)}) collective-permute-start(bf16[128,192]{1,0:T(8,128)(2,1)S(1)} %copy-done.31), channel_id=1, source_target_pairs={{0,2},{1,3},{2,4},{3,5},{4,6},{5,7},{6,0},{7,1},{8,10},{9,11},{10,... | collective-permute-start | bytes 147464 | tf_op jit(solution)/shard_map/ppermute | solution.py:797
  67.3 5.3 %collective-permute-start.11 = (bf16[128,192]{1,0:T(8,128)(2,1)S(1)}, bf16[128,192]{1,0:T(8,128)(2,1)S(1)}, u32[]{:S(2)}, u32[]{:S(2)}) collective-permute-start(bf16[128,192]{1,0:T(8,128)(2,1)S(1)} %copy-done.30), channel_id=1, source_target_pairs={{0,4},{1,5},{2,6},{3,7},{4,0},{5,1},{6,2},{7,3},{8,12},{9,13},{10,... | collective-permute-start | bytes 147464 | tf_op jit(solution)/shard_map/ppermute | solution.py:797
  69.7 3.4 %collective-permute-start.12 = (bf16[128,192]{1,0:T(8,128)(2,1)S(1)}, bf16[128,192]{1,0:T(8,128)(2,1)S(1)}, u32[]{:S(2)}, u32[]{:S(2)}) collective-permute-start(bf16[128,192]{1,0:T(8,128)(2,1)S(1)} %copy-done.29), channel_id=1, source_target_pairs={{0,6},{1,7},{2,0},{3,1},{4,2},{5,3},{6,4},{7,5},{8,14},{9,15},{10,... | collective-permute-start | bytes 147464 | tf_op jit(solution)/shard_map/ppermute | solution.py:797
  73.1 27.5 %slice-start = ((s8[4718592]{0:T(1024)(128)(4,1)}), s8[4194304]{0:T(1024)(128)(4,1)S(1)}, s32[]{:S(2)}) async-start(s8[4718592]{0:T(1024)(128)(4,1)} %bitcast.23), calls=%async_computation.6 | async-start | bytes 8388608
  73.1 27.5 %slice-start.1 = ((s8[4718592]{0:T(1024)(128)(4,1)}), s8[524288]{0:T(1024)(128)(4,1)S(1)}, s32[]{:S(2)}) async-start(s8[4718592]{0:T(1024)(128)(4,1)} %bitcast.23), calls=%async_computation.7 | async-start | bytes 1048576
  133.0 8.4 %copy-start.11 = (bf16[1024,768]{1,0:T(8,128)(2,1)S(1)}, bf16[1024,768]{1,0:T(8,128)(2,1)}, u32[]{:S(2)}) copy-start(bf16[1024,768]{1,0:T(8,128)(2,1)} %get-tuple-element.130.x_ref) | copy-start | bytes 4718596
  133.0 8.4 %copy-start.12 = (bf16[768,576]{1,0:T(8,128)(2,1)S(1)}, bf16[768,576]{1,0:T(8,128)(2,1)}, u32[]{:S(2)}) copy-start(bf16[768,576]{1,0:T(8,128)(2,1)} %get-tuple-element.131.wqkv_ref) | copy-start | bytes 2654212
  133.0 8.4 %copy-start.13 = (f32[3,128,640]{2,1,0:T(8,128)S(1)}, f32[3,128,640]{2,1,0:T(8,128)}, u32[]{:S(2)}) copy-start(f32[3,128,640]{2,1,0:T(8,128)} %get-tuple-element.135.band_ref) | copy-start | bytes 2949124
  133.0 8.4 %copy-start.14 = (bf16[1024,384]{1,0:T(8,128)(2,1)S(1)}, bf16[1024,384]{1,0:T(8,128)(2,1)}, u32[]{:S(2)}) copy-start(bf16[1024,384]{1,0:T(8,128)(2,1)} %get-tuple-element.132.qe_ref) | copy-start | bytes 2359300
  133.0 8.4 %copy-start.15 = (bf16[1024,384]{1,0:T(8,128)(2,1)S(1)}, bf16[1024,384]{1,0:T(8,128)(2,1)}, u32[]{:S(2)}) copy-start(bf16[1024,384]{1,0:T(8,128)(2,1)} %get-tuple-element.133.ke_ref) | copy-start | bytes 2359300
  133.0 8.4 %copy-start.16 = (bf16[1024,192]{1,0:T(8,128)(2,1)S(1)}, bf16[1024,192]{1,0:T(8,128)(2,1)}, u32[]{:S(2)}) copy-start(bf16[1024,192]{1,0:T(8,128)(2,1)} %get-tuple-element.134.v_ref) | copy-start | bytes 1179652
  133.0 8.4 %copy-start.17 = (f32[4,128,128]{2,1,0:T(8,128)S(1)}, f32[4,128,128]{2,1,0:T(8,128)}, u32[]{:S(2)}) copy-start(f32[4,128,128]{2,1,0:T(8,128)} %get-tuple-element.136.lse_ref) | copy-start | bytes 786436
  135.5 4.7 %collective-permute-start.14 = (bf16[128,192]{1,0:T(8,128)(2,1)S(1)}, bf16[128,192]{1,0:T(8,128)(2,1)S(1)}, u32[]{:S(2)}, u32[]{:S(2)}) collective-permute-start(bf16[128,192]{1,0:T(8,128)(2,1)S(1)} %get-tuple-element.127), channel_id=1, source_target_pairs={{0,2},{1,3},{2,4},{3,5},{4,6},{5,7},{6,0},{7,1},{8,10},{9,11},{10,... | collective-permute-start | bytes 147464 | tf_op jit(solution)/shard_map/ppermute | solution.py:797
  135.5 5.3 %collective-permute-start.15 = (bf16[128,192]{1,0:T(8,128)(2,1)S(1)}, bf16[128,192]{1,0:T(8,128)(2,1)S(1)}, u32[]{:S(2)}, u32[]{:S(2)}) collective-permute-start(bf16[128,192]{1,0:T(8,128)(2,1)S(1)} %get-tuple-element.128), channel_id=1, source_target_pairs={{0,4},{1,5},{2,6},{3,7},{4,0},{5,1},{6,2},{7,3},{8,12},{9,13},{10,... | collective-permute-start | bytes 147464 | tf_op jit(solution)/shard_map/ppermute | solution.py:797
  137.6 3.8 %collective-permute-start.16 = (bf16[128,192]{1,0:T(8,128)(2,1)S(1)}, bf16[128,192]{1,0:T(8,128)(2,1)S(1)}, u32[]{:S(2)}, u32[]{:S(2)}) collective-permute-start(bf16[128,192]{1,0:T(8,128)(2,1)S(1)} %get-tuple-element.129), channel_id=1, source_target_pairs={{0,6},{1,7},{2,0},{3,1},{4,2},{5,3},{6,4},{7,5},{8,14},{9,15},{10,... | collective-permute-start | bytes 147464 | tf_op jit(solution)/shard_map/ppermute | solution.py:797
  138.3 19.5 %collective-permute-start.22 = (bf16[768,512]{1,0:T(8,128)(2,1)S(1)}, bf16[768,512]{1,0:T(8,128)(2,1)S(1)}, u32[]{:S(2)}, u32[]{:S(2)}) collective-permute-start(bf16[768,512]{1,0:T(8,128)(2,1)S(1)} %get-tuple-element.151), channel_id=1, source_target_pairs={{0,1},{1,0},{2,3},{3,2},{4,5},{5,4},{6,7},{7,6},{8,9},{9,8},{10,11... | collective-permute-start | bytes 2359304 | tf_op jit(solution)/shard_map/ppermute | solution.py:805
  152.7 5.1 %collective-permute-start.21 = (bf16[768,384]{1,0:T(8,128)(2,1)S(1)}, bf16[768,384]{1,0:T(8,128)(2,1)S(1)}, u32[]{:S(2)}, u32[]{:S(2)}) collective-permute-start(bf16[768,384]{1,0:T(8,128)(2,1)S(1)} %get-tuple-element.149), channel_id=1, source_target_pairs={{0,1},{1,0},{2,3},{3,2},{4,5},{5,4},{6,7},{7,6},{8,9},{9,8},{10,11... | collective-permute-start | bytes 1769480 | tf_op jit(solution)/shard_map/ppermute | solution.py:805
  159.2 27.8 %all-to-all-start.4 = ((bf16[16,48,896]{2,1,0:T(8,128)(2,1)}), bf16[16,48,896]{2,1,0:T(8,128)(2,1)S(1)}, u32[]{:S(2)}, u32[]{:S(2)}) async-start(bf16[16,48,896]{2,1,0:T(8,128)(2,1)} %bitcast.12), calls=%async_computation.4 | async-start | bytes 2752512 | tf_op jit(solution)/shard_map/all_to_all | solution.py:801
  162.9 2.4 %collective-permute-start.17 = (bf16[4,128,768]{2,1,0:T(8,128)(2,1)S(1)}, bf16[4,128,768]{2,1,0:T(8,128)(2,1)S(1)}, u32[]{:S(2)}, u32[]{:S(2)}) collective-permute-start(bf16[4,128,768]{2,1,0:T(8,128)(2,1)S(1)} %get-tuple-element.138), channel_id=1, source_target_pairs={{0,1},{1,0},{2,3},{3,2},{4,5},{5,4},{6,7},{7,6},{8,9},{9,8},{10,11... | collective-permute-start | bytes 2359304 | tf_op jit(solution)/shard_map/ppermute | solution.py:805
  167.3 25.0 %collective-permute-start.18 = (bf16[128,768]{1,0:T(8,128)(2,1)S(1)}, bf16[128,768]{1,0:T(8,128)(2,1)S(1)}, u32[]{:S(2)}, u32[]{:S(2)}) collective-permute-start(bf16[128,768]{1,0:T(8,128)(2,1)S(1)} %get-tuple-element.140), channel_id=1, source_target_pairs={{0,2},{1,3},{2,4},{3,5},{4,6},{5,7},{6,0},{7,1},{8,10},{9,11},{10,... | collective-permute-start | bytes 589832 | tf_op jit(solution)/shard_map/ppermute | solution.py:797
  168.4 23.9 %collective-permute-start.19 = (bf16[128,768]{1,0:T(8,128)(2,1)S(1)}, bf16[128,768]{1,0:T(8,128)(2,1)S(1)}, u32[]{:S(2)}, u32[]{:S(2)}) collective-permute-start(bf16[128,768]{1,0:T(8,128)(2,1)S(1)} %get-tuple-element.141), channel_id=1, source_target_pairs={{0,4},{1,5},{2,6},{3,7},{4,0},{5,1},{6,2},{7,3},{8,12},{9,13},{10,... | collective-permute-start | bytes 589832 | tf_op jit(solution)/shard_map/ppermute | solution.py:797
  170.7 21.6 %collective-permute-start.20 = (bf16[128,768]{1,0:T(8,128)(2,1)S(1)}, bf16[128,768]{1,0:T(8,128)(2,1)S(1)}, u32[]{:S(2)}, u32[]{:S(2)}) collective-permute-start(bf16[128,768]{1,0:T(8,128)(2,1)S(1)} %get-tuple-element.142), channel_id=1, source_target_pairs={{0,6},{1,7},{2,0},{3,1},{4,2},{5,3},{6,4},{7,5},{8,14},{9,15},{10,... | collective-permute-start | bytes 589832 | tf_op jit(solution)/shard_map/ppermute | solution.py:797
  187.8 9.6 %all-to-all-start.5 = ((bf16[8,8,896]{2,1,0:T(8,128)(2,1)}), bf16[8,8,896]{2,1,0:T(8,128)(2,1)S(1)}, u32[]{:S(2)}, u32[]{:S(2)}) async-start(bf16[8,8,896]{2,1,0:T(8,128)(2,1)} %bitcast.14), calls=%async_computation.5 | async-start | bytes 229376 | tf_op jit(solution)/shard_map/all_to_all | solution.py:801
  (13 other events, 27.6 us)

commit v5 on v4

--- a/solution.py
+++ b/solution.py
@@ -25,7 +25,7 @@
 SIDE = 320
 PART = 384
 LATE = 512
-FF_TILE = 768
+FF_TILE = 512
 PROJ = 512
 eps = 1e-06
 bucket_edges = (12, 16, 23, 32, 46, 64, 91)
@@ -843,8 +843,8 @@
     got_terms = other_core(give_terms)
     kept = kept_terms(idx, h, dq_keep, line, dgain, acc)
     terms = joined_terms(kept, got_terms, keep, late)
-    got = other_core(other)
-    d_parts = pair_sum(idx, own, got)
+    d_parts = pair_sum(idx, own, other_core(other))
+    terms, d_parts = lax.optimization_barrier((terms, d_parts))
     d_parts = [d_parts[0]] + [along_y(d_parts[k], k) for k in (1, 2, 3)]
     sums = exchange(middle_sums(exchange(terms, "fsdp")), "seq")
     dq, dk, dv, do, dr, small = sums_last(sums)

time: 201 us -> 201 us (level)
    ppermute x8, waiting for transfers between devices: 2.28 us -> 0.02 us  [other_core(): return lax.ppermute(v, 'seq', [(s, s ^ 1) for s in range(8)])]
    all_to_all x4, waiting for transfers between devices: 38.2 us -> 40.4 us  [exchange(): return lax.all_to_all(v, axes, split_axis=0, concat_axis=0, tiled=True)]
    unnamed x69 -> x67, local copies, waits for them, and re-layouts: 6.85 us -> 6.44 us
  transfers between devices with their start and end apart: 27 -> 27, of which waited for: 10 -> 9; matrix products, arithmetic and copies ran while one was open for 1% -> 1% of each run, Pallas kernels for 16% -> 17%
where the time goes in v5:
time: 201 us; the launch traced here: 200 us
  Pallas kernels  50.6 us (25%)
  starting transfers between devices  47.1 us (23%)
  blocking collectives  46 us (23%)
  waiting for transfers between devices  44 us (22%)
  local copies, waits for them, and re-layouts  9.11 us (5%)
    all_to_all x2, blocking collectives, exchange(): return lax.all_to_all(v, axes, split_axis=0, concat_axis=0, tiled=True)  46 us
    all_to_all x4, waiting for transfers between devices, exchange(): return lax.all_to_all(v, axes, split_axis=0, concat_axis=0, tiled=True)  40.4 us
    all_to_all x4, starting transfers between devices, exchange(): return lax.all_to_all(v, axes, split_axis=0, concat_axis=0, tiled=True)  22.2 us
    ppermute x15, starting transfers between devices, along_y(): return lax.ppermute(v, 'seq', [(s, (s + 2 * k) % 8) for s in range(8)])  17.6 us
    pallas_call x1, Pallas kernels, attend(): pl.pallas_call(attend_kernel, out_shape=outs + saved, in_specs=[smem, vme...  12.2 us
    pallas_call x1, Pallas kernels, attend_back(): call(backward_kernel, outs, [smem] + [vmem] * 12, [pltpu.VMEM((4, TOK, CO...  11.7 us
    pallas_call x1, Pallas kernels, experts(): pl.pallas_call(expert_kernel, out_shape=[sds(LEN, HALF), sds(1, WIDTH, FF...  9.01 us
    ppermute x8, starting transfers between devices, other_core(): return lax.ppermute(v, 'seq', [(s, s ^ 1) for s in range(8)])  7.21 us
  transfers between devices with their start and end apart: 27, of which 9 were waited for; matrix products, arithmetic and copies ran while one was open for 1% of the time, Pallas kernels for 17%

profile of v5, /device:TPU:1, one launch (start us, length us, event | category | flops | bytes accessed | tf_op | source)
XLA Modules:
  0.0 199.9 jit_solution(7454867028625724563)
XLA Ops:
  0.7 1.3 maximum_bitcast_fusion.small_ref
  1.9 1.7 pack_weights.1
  3.6 8.4 %all-to-all-start = ((bf16[16,8,2432]{2,1,0:T(8,128)(2,1)}), bf16[16,8,2432]{2,1,0:T(8,128)(2,1)S(1)}, u32[]{:S(2)}, u32[]{:S(2)}) async-start(bf16[16,8,2432]{2,1,0:T(8,128)(2,1)} %bitcast.28), calls=%async_computation | async-start | bytes 1245184 | tf_op jit(solution)/shard_map/all_to_all | solution.py:801
  12.1 1.0 collective-permute-start.3
  13.1 2.7 %collective-permute-start.2 = (bf16[128,768]{1,0:T(8,128)(2,1)S(1)}, bf16[128,768]{1,0:T(8,128)(2,1)S(1)}, u32[]{:S(2)}, u32[]{:S(2)}) collective-permute-start(bf16[128,768]{1,0:T(8,128)(2,1)S(1)} %copy-done.3), channel_id=1, source_target_pairs={{0,6},{1,7},{2,0},{3,1},{4,2},{5,3},{6,4},{7,5},{8,14},{9,15},{10,... | collective-permute-start | bytes 589832 | tf_op jit(solution)/shard_map/ppermute | solution.py:797
  16.2 0.7 collective-permute-start
  16.9 6.6 %all-to-all-done = bf16[16,8,2432]{2,1,0:T(8,128)(2,1)S(1)} async-done(((bf16[16,8,2432]{2,1,0:T(8,128)(2,1)}), bf16[16,8,2432]{2,1,0:T(8,128)(2,1)S(1)}, u32[]{:S(2)}, u32[]{:S(2)}) %all-to-all-start) | async-done | bytes 622624 | tf_op jit(solution)/shard_map/all_to_all | solution.py:801
  23.5 0.8 copy-done.18
  24.3 2.5 %split_weights.1 = (bf16[768,640]{1,0:T(8,128)(2,1)}, bf16[96,896]{1,0:T(8,128)(2,1)}) custom-call(bf16[128,2432]{1,0:T(8,128)(2,1)} %bitcast.27), custom_call_target="tpu_custom_call" | custom-call | flops 2300000000 | bytes 1048576 | tf_op jit(solution)/shard_map/split_weights/pallas_call | solution.py:169
  26.8 1.5 collective-permute-done.refs_1_
  28.4 5.2 %all-to-all-start.1 = ((bf16[8,96,640]{2,1,0:T(8,128)(2,1)}), bf16[8,96,640]{2,1,0:T(8,128)(2,1)S(1)}, u32[]{:S(2)}, u32[]{:S(2)}) async-start(bf16[8,96,640]{2,1,0:T(8,128)(2,1)} %bitcast.26), calls=%async_computation.1 | async-start | bytes 1966080 | tf_op jit(solution)/shard_map/all_to_all | solution.py:801
  34.1 1.0 copy.27.seg_ref
  35.7 12.3 %all-to-all-done.1 = bf16[8,96,640]{2,1,0:T(8,128)(2,1)S(1)} async-done(((bf16[8,96,640]{2,1,0:T(8,128)(2,1)}), bf16[8,96,640]{2,1,0:T(8,128)(2,1)S(1)}, u32[]{:S(2)}, u32[]{:S(2)}) %all-to-all-start.1) | async-done | bytes 983072 | tf_op jit(solution)/shard_map/all_to_all | solution.py:801
  48.0 0.9 collective-permute-start.6
  48.9 1.2 collective-permute-start.5
  51.5 12.2 %attend.1 = (bf16[128,192]{1,0:T(8,128)(2,1)}, bf16[128,192]{1,0:T(8,128)(2,1)}, bf16[128,192]{1,0:T(8,128)(2,1)}, bf16[128,192]{1,0:T(8,128)(2,1)}, f32[8,768]{...) custom-call(s32[2]{0:T(128)} %pad_add_fusion.idx_ref, ...), custom_call_target="tpu_custom_call" | custom-call | flops 16099999744 | bytes 1048576 | tf_op jit(solution)/shard_map/attend/pallas_call | solution.py:343
  63.9 1.5 collective-permute-start.13
  65.6 1.7 collective-permute-start.10
  67.3 2.4 %collective-permute-start.11 = (bf16[128,192]{1,0:T(8,128)(2,1)S(1)}, bf16[128,192]{1,0:T(8,128)(2,1)S(1)}, u32[]{:S(2)}, u32[]{:S(2)}) collective-permute-start(bf16[128,192]{1,0:T(8,128)(2,1)S(1)} %copy-done.29), channel_id=1, source_target_pairs={{0,4},{1,5},{2,6},{3,7},{4,0},{5,1},{6,2},{7,3},{8,12},{9,13},{10,... | collective-permute-start | bytes 147464 | tf_op jit(solution)/shard_map/ppermute | solution.py:797
  69.7 1.2 collective-permute-start.12
  70.9 1.7 output_weights.1
  73.1 2.0 %dispatch.1 = (f32[128,768]{1,0:T(8,128)S(1)}, bf16[128,768]{1,0:T(8,128)(2,1)S(1)}, f32[128,128]{1,0:T(8,128)S(1)}, bf16[2,128,128]{2,1,0:T(8,128)(2,1)S(1)}, bf16[1024,384]{1,0:T(8,128)(2,1)S(1)}) custom-call(s32[2]{0:T(128)S(1)} %copy-done.5, bf16[128,768]{1,0:T(8,128)(2,1)S(1)} %copy-done.4, bf16[128,192]{1,0:T(8,128)(2,1)S(1)} %copy-done.8, ...), custom_call_target="tpu_custom_call" | custom-call | flops 2300000000 | bytes 1048576 | tf_op jit(solution)/shard_map/dispatch/pallas_call | solution.py:403
  75.2 25.4 %all_to_all.67 = bf16[128,8,384]{2,1,0:T(8,128)(2,1)S(1)} all-to-all(bf16[128,8,384]{2,1,0:T(8,128)(2,1)S(1)} %bitcast.19), channel_id=1, replica_groups=mesh['fsdp'=16,'seq'=8] {'fsdp','seq'}, dimensions={0} | all-to-all | bytes 1572864 | tf_op jit(solution)/shard_map/all_to_all | solution.py:801
  100.6 2.3 %copy-done.1 = bf16[1,3072,768]{2,1,0:T(8,128)(2,1)S(1)} copy-done((bf16[1,3072,768]{2,1,0:T(8,128)(2,1)S(1)}, bf16[1,3072,768]{2,1,0:T(8,128)(2,1)}, u32[]{:S(2)}) %copy-start.1) | copy-done | bytes 4718616
  102.9 9.0 %experts.1 = (bf16[1024,384]{1,0:T(8,128)(2,1)S(1)}, bf16[1,768,3072]{2,1,0:T(8,128)(2,1)}, bf16[1,3072,768]{2,1,0:T(8,128)(2,1)}) custom-call(bf16[1024,384]{1,0:T(8,128)(2,1)S(1)} %bitcast.20, bf16[1,768,3072]{2,1,0:T(8,128)(2,1)S(1)} %bitcast.24, bf16[1,3072,768]{2,1,0:T(8,128)(2,1)S(1)} %copy-done.1), custom_call_target="tpu_custom_call" | custom-call | flops 13799999488 | bytes 1048576 | tf_op jit(solution)/shard_map/experts/pallas_call | solution.py:471
  112.0 20.6 %all_to_all.68 = bf16[128,8,384]{2,1,0:T(8,128)(2,1)S(1)} all-to-all(bf16[128,8,384]{2,1,0:T(8,128)(2,1)S(1)} %bitcast.21), channel_id=1, replica_groups=mesh['fsdp'=16,'seq'=8] {'fsdp','seq'}, dimensions={0} | all-to-all | bytes 1572864 | tf_op jit(solution)/shard_map/all_to_all | solution.py:801
  132.6 2.4 %returned.1 = (bf16[128,768]{1,0:T(8,128)(2,1)}, f32[128,768]{1,0:T(8,128)S(1)}, bf16[128,192]{1,0:T(8,128)(2,1)S(1)}, bf16[128,192]{1,0:T(8,128)(2,1)S(1)}, bf1...) custom-call(s32[2]{0:T(128)S(1)} %copy-done.5, ...), custom_call_target="tpu_custom_call" | custom-call | flops 2300000000 | bytes 1048576 | tf_op jit(solution)/shard_map/returned/pallas_call | solution.py:554
  135.0 2.1 %collective-permute-start.15 = (bf16[128,192]{1,0:T(8,128)(2,1)S(1)}, bf16[128,192]{1,0:T(8,128)(2,1)S(1)}, u32[]{:S(2)}, u32[]{:S(2)}) collective-permute-start(bf16[128,192]{1,0:T(8,128)(2,1)S(1)} %get-tuple-element.133), channel_id=1, source_target_pairs={{0,4},{1,5},{2,6},{3,7},{4,0},{5,1},{6,2},{7,3},{8,12},{9,13},{10,... | collective-permute-start | bytes 147464 | tf_op jit(solution)/shard_map/ppermute | solution.py:797
  137.1 0.8 collective-permute-start.16
  137.9 1.6 collective-permute-start.18
  141.0 11.7 %attend_back.1 = (f32[4,128,768]{2,1,0:T(8,128)S(1)}, bf16[4,128,768]{2,1,0:T(8,128)(2,1)S(1)}, bf16[1024,320]{1,0:T(8,128)(2,1)S(1)}, bf16[768,384]{1,0:T(8,128...) custom-call(s32[2]{0:T(128)S(1)} %copy-done.5, ...), custom_call_target="tpu_custom_call" | custom-call | flops 13799999488 | bytes 1048576 | tf_op jit(solution)/shard_map/attend_back/pallas_call | solution.py:641
  152.7 2.4 %collective-permute-start.17 = (bf16[768,384]{1,0:T(8,128)(2,1)S(1)}, bf16[768,384]{1,0:T(8,128)(2,1)S(1)}, u32[]{:S(2)}, u32[]{:S(2)}) collective-permute-start(bf16[768,384]{1,0:T(8,128)(2,1)S(1)} %get-tuple-element.147), channel_id=1, source_target_pairs={{0,1},{1,0},{2,3},{3,2},{4,5},{5,4},{6,7},{7,6},{8,9},{9,8},{10,11... | collective-permute-start | bytes 1769480 | tf_op jit(solution)/shard_map/ppermute | solution.py:805
  155.2 2.7 %kept_terms.1.kept_ref = f32[768,384]{1,0:T(8,128)S(1)} custom-call(s32[2]{0:T(128)S(1)} %copy-done.5, bf16[1024,768]{1,0:T(8,128)(2,1)S(1)} %get-tuple-element.142.h_ref, bf16[1024,320]{1,0:T(8,128)(2,1)S(1)} %get-tuple-element.143.dq_ref, f32[8,768]{1,0:T(8,128)S(1)} %get-tuple-element.144.line_ref, f32[8,768]{1,0:T(8,128)S(1)} %get-tuple-element.145.dgain_ref, ...), custom_call_target="tpu_custom_call" | custom-call | flops 4600000000 | bytes 1048576 | tf_op jit(solution)/shard_map/kept_terms/pallas_call | solution.py:700
  157.9 1.4 joined_terms.1
  159.3 0.7 pair_sum.1
  160.0 0.7 copy-done.6
  160.8 3.7 %all-to-all-start.4 = ((bf16[16,48,896]{2,1,0:T(8,128)(2,1)}), bf16[16,48,896]{2,1,0:T(8,128)(2,1)S(1)}, u32[]{:S(2)}, u32[]{:S(2)}) async-start(bf16[16,48,896]{2,1,0:T(8,128)(2,1)} %bitcast.12), calls=%async_computation.4 | async-start | bytes 2752512 | tf_op jit(solution)/shard_map/all_to_all | solution.py:801
  164.5 1.1 collective-permute-start.20
  165.6 2.2 %collective-permute-start.21 = (bf16[128,768]{1,0:T(8,128)(2,1)S(1)}, bf16[128,768]{1,0:T(8,128)(2,1)S(1)}, u32[]{:S(2)}, u32[]{:S(2)}) collective-permute-start(bf16[128,768]{1,0:T(8,128)(2,1)S(1)} %get-tuple-element.158), channel_id=1, source_target_pairs={{0,4},{1,5},{2,6},{3,7},{4,0},{5,1},{6,2},{7,3},{8,12},{9,13},{10,... | collective-permute-start | bytes 589832 | tf_op jit(solution)/shard_map/ppermute | solution.py:797
  168.1 18.5 %all-to-all-done.4 = bf16[16,48,896]{2,1,0:T(8,128)(2,1)S(1)} async-done(((bf16[16,48,896]{2,1,0:T(8,128)(2,1)}), bf16[16,48,896]{2,1,0:T(8,128)(2,1)S(1)}, u32[]{:S(2)}, u32[]{:S(2)}) %all-to-all-start.4) | async-done | bytes 1376288 | tf_op jit(solution)/shard_map/all_to_all | solution.py:801
  186.6 0.9 middle_sums.1
  187.5 4.9 %all-to-all-start.5 = ((bf16[8,8,896]{2,1,0:T(8,128)(2,1)}), bf16[8,8,896]{2,1,0:T(8,128)(2,1)S(1)}, u32[]{:S(2)}, u32[]{:S(2)}) async-start(bf16[8,8,896]{2,1,0:T(8,128)(2,1)} %bitcast.14), calls=%async_computation.5 | async-start | bytes 229376 | tf_op jit(solution)/shard_map/all_to_all | solution.py:801
  192.4 1.0 copy-done.7
  193.4 1.0 tokens_last.1
  194.4 3.1 %all-to-all-done.5 = bf16[8,8,896]{2,1,0:T(8,128)(2,1)S(1)} async-done(((bf16[8,8,896]{2,1,0:T(8,128)(2,1)}), bf16[8,8,896]{2,1,0:T(8,128)(2,1)S(1)}, u32[]{:S(2)}, u32[]{:S(2)}) %all-to-all-start.5) | async-done | bytes 114720 | tf_op jit(solution)/shard_map/all_to_all | solution.py:801
  197.5 0.7 sums_last.1
  198.5 0.7 slice_reduce_fusion.2
  199.2 0.7 slice_reduce_fusion
  (101 shorter events, 5.6 us)
Async XLA Ops:
  1.9 10.1 %copy-start.3 = (bf16[128,768]{1,0:T(8,128)(2,1)S(1)}, bf16[128,768]{1,0:T(8,128)(2,1)}, u32[]{:S(2)}) copy-start(bf16[128,768]{1,0:T(8,128)(2,1)} %x_ref.3) | copy-start | bytes 589828
  3.6 19.9 %all-to-all-start = ((bf16[16,8,2432]{2,1,0:T(8,128)(2,1)}), bf16[16,8,2432]{2,1,0:T(8,128)(2,1)S(1)}, u32[]{:S(2)}, u32[]{:S(2)}) async-start(bf16[16,8,2432]{2,1,0:T(8,128)(2,1)} %bitcast.28), calls=%async_computation | async-start | bytes 1245184 | tf_op jit(solution)/shard_map/all_to_all | solution.py:801
  12.1 14.7 %collective-permute-start.3 = (bf16[128,768]{1,0:T(8,128)(2,1)S(1)}, bf16[128,768]{1,0:T(8,128)(2,1)S(1)}, u32[]{:S(2)}, u32[]{:S(2)}) collective-permute-start(bf16[128,768]{1,0:T(8,128)(2,1)S(1)} %copy-done.3), channel_id=1, source_target_pairs={{0,1},{1,0},{2,3},{3,2},{4,5},{5,4},{6,7},{7,6},{8,9},{9,8},{10,11... | collective-permute-start | bytes 589832 | tf_op jit(solution)/shard_map/ppermute | solution.py:805
  13.1 13.7 %collective-permute-start.2 = (bf16[128,768]{1,0:T(8,128)(2,1)S(1)}, bf16[128,768]{1,0:T(8,128)(2,1)S(1)}, u32[]{:S(2)}, u32[]{:S(2)}) collective-permute-start(bf16[128,768]{1,0:T(8,128)(2,1)S(1)} %copy-done.3), channel_id=1, source_target_pairs={{0,6},{1,7},{2,0},{3,1},{4,2},{5,3},{6,4},{7,5},{8,14},{9,15},{10,... | collective-permute-start | bytes 589832 | tf_op jit(solution)/shard_map/ppermute | solution.py:797
  15.8 11.0 %collective-permute-start.1 = (bf16[128,768]{1,0:T(8,128)(2,1)S(1)}, bf16[128,768]{1,0:T(8,128)(2,1)S(1)}, u32[]{:S(2)}, u32[]{:S(2)}) collective-permute-start(bf16[128,768]{1,0:T(8,128)(2,1)S(1)} %copy-done.3), channel_id=1, source_target_pairs={{0,4},{1,5},{2,6},{3,7},{4,0},{5,1},{6,2},{7,3},{8,12},{9,13},{10,... | collective-permute-start | bytes 589832 | tf_op jit(solution)/shard_map/ppermute | solution.py:797
  16.2 12.2 %collective-permute-start = (bf16[128,768]{1,0:T(8,128)(2,1)S(1)}, bf16[128,768]{1,0:T(8,128)(2,1)S(1)}, u32[]{:S(2)}, u32[]{:S(2)}) collective-permute-start(bf16[128,768]{1,0:T(8,128)(2,1)S(1)} %copy-done.3), channel_id=1, source_target_pairs={{0,2},{1,3},{2,4},{3,5},{4,6},{5,7},{6,0},{7,1},{8,10},{9,11},{10,... | collective-permute-start | bytes 589832 | tf_op jit(solution)/shard_map/ppermute | solution.py:797
  26.8 7.3 %copy-start.19 = (s32[1,1024]{1,0:T(1,128)S(1)}, s32[1,1024]{1,0:T(1,128)}, u32[]{:S(2)}) copy-start(s32[1,1024]{1,0:T(1,128)} %param.15) | copy-start | bytes 12292
  26.8 21.2 %copy-start = (bf16[96,896]{1,0:T(8,128)(2,1)S(1)}, bf16[96,896]{1,0:T(8,128)(2,1)}, u32[]{:S(2)}) copy-start(bf16[96,896]{1,0:T(8,128)(2,1)} %get-tuple-element.117.refs_0_) | copy-start | bytes 516100
  26.8 23.3 %copy-start.21 = (bf16[128,768]{1,0:T(8,128)(2,1)}, bf16[128,768]{1,0:T(8,128)(2,1)S(1)}, u32[]{:S(2)}) copy-start(bf16[128,768]{1,0:T(8,128)(2,1)S(1)} %collective-permute-done.3.refs_4_) | copy-start | bytes 589828
  26.8 23.3 %copy-start.22 = (bf16[128,768]{1,0:T(8,128)(2,1)}, bf16[128,768]{1,0:T(8,128)(2,1)S(1)}, u32[]{:S(2)}) copy-start(bf16[128,768]{1,0:T(8,128)(2,1)S(1)} %collective-permute-done.2.refs_3_) | copy-start | bytes 589828
  26.8 23.3 %copy-start.23 = (bf16[128,768]{1,0:T(8,128)(2,1)}, bf16[128,768]{1,0:T(8,128)(2,1)S(1)}, u32[]{:S(2)}) copy-start(bf16[128,768]{1,0:T(8,128)(2,1)S(1)} %collective-permute-done.1.refs_2_) | copy-start | bytes 589828
  28.4 21.8 %copy-start.24 = (bf16[128,768]{1,0:T(8,128)(2,1)}, bf16[128,768]{1,0:T(8,128)(2,1)S(1)}, u32[]{:S(2)}) copy-start(bf16[128,768]{1,0:T(8,128)(2,1)S(1)} %collective-permute-done.refs_1_) | copy-start | bytes 589828
  28.4 19.6 %all-to-all-start.1 = ((bf16[8,96,640]{2,1,0:T(8,128)(2,1)}), bf16[8,96,640]{2,1,0:T(8,128)(2,1)S(1)}, u32[]{:S(2)}, u32[]{:S(2)}) async-start(bf16[8,96,640]{2,1,0:T(8,128)(2,1)} %bitcast.26), calls=%async_computation.1 | async-start | bytes 1966080 | tf_op jit(solution)/shard_map/all_to_all | solution.py:801
  33.6 16.5 %collective-permute-start.7 = (bf16[128,768]{1,0:T(8,128)(2,1)S(1)}, bf16[128,768]{1,0:T(8,128)(2,1)S(1)}, u32[]{:S(2)}, u32[]{:S(2)}) collective-permute-start(bf16[128,768]{1,0:T(8,128)(2,1)S(1)} %collective-permute-done.refs_1_), channel_id=1, source_target_pairs={{0,1},{1,0},{2,3},{3,2},{4,5},{5,4},{6,7},{7,6},{8,9},{9,8},{10,11... | collective-permute-start | bytes 589832 | tf_op jit(solution)/shard_map/ppermute | solution.py:805
  33.6 16.5 %collective-permute-start.8 = (bf16[128,768]{1,0:T(8,128)(2,1)S(1)}, bf16[128,768]{1,0:T(8,128)(2,1)S(1)}, u32[]{:S(2)}, u32[]{:S(2)}) collective-permute-start(bf16[128,768]{1,0:T(8,128)(2,1)S(1)} %collective-permute-done.1.refs_2_), channel_id=1, source_target_pairs={{0,1},{1,0},{2,3},{3,2},{4,5},{5,4},{6,7},{7,6},{8,9},{9,8},{10,11... | collective-permute-start | bytes 589832 | tf_op jit(solution)/shard_map/ppermute | solution.py:805
  34.1 16.0 %collective-permute-start.9 = (bf16[128,768]{1,0:T(8,128)(2,1)S(1)}, bf16[128,768]{1,0:T(8,128)(2,1)S(1)}, u32[]{:S(2)}, u32[]{:S(2)}) collective-permute-start(bf16[128,768]{1,0:T(8,128)(2,1)S(1)} %collective-permute-done.2.refs_3_), channel_id=1, source_target_pairs={{0,1},{1,0},{2,3},{3,2},{4,5},{5,4},{6,7},{7,6},{8,9},{9,8},{10,11... | collective-permute-start | bytes 589832 | tf_op jit(solution)/shard_map/ppermute | solution.py:805
  48.0 15.8 %collective-permute-start.6 = (bf16[96,896]{1,0:T(8,128)(2,1)S(1)}, bf16[96,896]{1,0:T(8,128)(2,1)S(1)}, u32[]{:S(2)}, u32[]{:S(2)}) collective-permute-start(bf16[96,896]{1,0:T(8,128)(2,1)S(1)} %copy-done), channel_id=1, source_target_pairs={{0,6},{1,7},{2,0},{3,1},{4,2},{5,3},{6,4},{7,5},{8,14},{9,15},{10,... | collective-permute-start | bytes 516104 | tf_op jit(solution)/shard_map/ppermute | solution.py:797
  48.9 14.9 %collective-permute-start.5 = (bf16[96,896]{1,0:T(8,128)(2,1)S(1)}, bf16[96,896]{1,0:T(8,128)(2,1)S(1)}, u32[]{:S(2)}, u32[]{:S(2)}) collective-permute-start(bf16[96,896]{1,0:T(8,128)(2,1)S(1)} %copy-done), channel_id=1, source_target_pairs={{0,4},{1,5},{2,6},{3,7},{4,0},{5,1},{6,2},{7,3},{8,12},{9,13},{10,... | collective-permute-start | bytes 516104 | tf_op jit(solution)/shard_map/ppermute | solution.py:797
  50.1 13.7 %collective-permute-start.4 = (bf16[96,896]{1,0:T(8,128)(2,1)S(1)}, bf16[96,896]{1,0:T(8,128)(2,1)S(1)}, u32[]{:S(2)}, u32[]{:S(2)}) collective-permute-start(bf16[96,896]{1,0:T(8,128)(2,1)S(1)} %copy-done), channel_id=1, source_target_pairs={{0,2},{1,3},{2,4},{3,5},{4,6},{5,7},{6,0},{7,1},{8,10},{9,11},{10,... | collective-permute-start | bytes 516104 | tf_op jit(solution)/shard_map/ppermute | solution.py:797
  63.8 7.1 %copy-start.5 = (s32[2]{0:T(128)S(1)}, s32[2]{0:T(128)}, u32[]{:S(2)}) copy-start(s32[2]{0:T(128)} %pad_add_fusion.idx_ref) | copy-start | bytes 28
  63.9 7.0 %collective-permute-start.13 = (bf16[384,896]{1,0:T(8,128)(2,1)S(1)}, bf16[384,896]{1,0:T(8,128)(2,1)S(1)}, u32[]{:S(2)}, u32[]{:S(2)}) collective-permute-start(bf16[384,896]{1,0:T(8,128)(2,1)S(1)} %pad_maximum_fusion), channel_id=1, source_target_pairs={{0,1},{1,0},{2,3},{3,2},{4,5},{5,4},{6,7},{7,6},{8,9},{9,8},{10,11... | collective-permute-start | bytes 2064392 | tf_op jit(solution)/shard_map/ppermute | solution.py:805
  65.5 7.6 %copy-start.2 = (bf16[128,768]{1,0:T(8,128)(2,1)S(1)}, bf16[128,768]{1,0:T(8,128)(2,1)}, u32[]{:S(2)}) copy-start(bf16[128,768]{1,0:T(8,128)(2,1)} %cot_ref.3) | copy-start | bytes 589828
  65.5 7.6 %copy-start.4 = (bf16[128,768]{1,0:T(8,128)(2,1)S(1)}, bf16[128,768]{1,0:T(8,128)(2,1)}, u32[]{:S(2)}) copy-start(bf16[128,768]{1,0:T(8,128)(2,1)} %x_ref.3) | copy-start | bytes 589828
  65.6 7.6 %copy-start.8 = (bf16[128,192]{1,0:T(8,128)(2,1)S(1)}, bf16[128,192]{1,0:T(8,128)(2,1)}, u32[]{:S(2)}) copy-start(bf16[128,192]{1,0:T(8,128)(2,1)} %get-tuple-element.113.o0_ref) | copy-start | bytes 147460
  65.6 7.6 %copy-start.9 = (f32[8,768]{1,0:T(8,128)S(1)}, f32[8,768]{1,0:T(8,128)}, u32[]{:S(2)}) copy-start(f32[8,768]{1,0:T(8,128)} %get-tuple-element.123.gain_ref) | copy-start | bytes 73732
  65.6 7.0 %collective-permute-start.10 = (bf16[128,192]{1,0:T(8,128)(2,1)S(1)}, bf16[128,192]{1,0:T(8,128)(2,1)S(1)}, u32[]{:S(2)}, u32[]{:S(2)}) collective-permute-start(bf16[128,192]{1,0:T(8,128)(2,1)S(1)} %copy-done.30), channel_id=1, source_target_pairs={{0,2},{1,3},{2,4},{3,5},{4,6},{5,7},{6,0},{7,1},{8,10},{9,11},{10,... | collective-permute-start | bytes 147464 | tf_op jit(solution)/shard_map/ppermute | solution.py:797
  67.3 5.3 %collective-permute-start.11 = (bf16[128,192]{1,0:T(8,128)(2,1)S(1)}, bf16[128,192]{1,0:T(8,128)(2,1)S(1)}, u32[]{:S(2)}, u32[]{:S(2)}) collective-permute-start(bf16[128,192]{1,0:T(8,128)(2,1)S(1)} %copy-done.29), channel_id=1, source_target_pairs={{0,4},{1,5},{2,6},{3,7},{4,0},{5,1},{6,2},{7,3},{8,12},{9,13},{10,... | collective-permute-start | bytes 147464 | tf_op jit(solution)/shard_map/ppermute | solution.py:797
  69.7 3.4 %collective-permute-start.12 = (bf16[128,192]{1,0:T(8,128)(2,1)S(1)}, bf16[128,192]{1,0:T(8,128)(2,1)S(1)}, u32[]{:S(2)}, u32[]{:S(2)}) collective-permute-start(bf16[128,192]{1,0:T(8,128)(2,1)S(1)} %copy-done.28), channel_id=1, source_target_pairs={{0,6},{1,7},{2,0},{3,1},{4,2},{5,3},{6,4},{7,5},{8,14},{9,15},{10,... | collective-permute-start | bytes 147464 | tf_op jit(solution)/shard_map/ppermute | solution.py:797
  73.1 27.5 %slice-start = ((s8[4718592]{0:T(1024)(128)(4,1)}), s8[4194304]{0:T(1024)(128)(4,1)S(1)}, s32[]{:S(2)}) async-start(s8[4718592]{0:T(1024)(128)(4,1)} %bitcast.23), calls=%async_computation.6 | async-start | bytes 8388608
  73.1 27.5 %slice-start.1 = ((s8[4718592]{0:T(1024)(128)(4,1)}), s8[524288]{0:T(1024)(128)(4,1)S(1)}, s32[]{:S(2)}) async-start(s8[4718592]{0:T(1024)(128)(4,1)} %bitcast.23), calls=%async_computation.7 | async-start | bytes 1048576
  132.6 8.4 %copy-start.10 = (bf16[1024,768]{1,0:T(8,128)(2,1)S(1)}, bf16[1024,768]{1,0:T(8,128)(2,1)}, u32[]{:S(2)}) copy-start(bf16[1024,768]{1,0:T(8,128)(2,1)} %get-tuple-element.135.x_ref) | copy-start | bytes 4718596
  132.6 8.4 %copy-start.11 = (bf16[768,576]{1,0:T(8,128)(2,1)S(1)}, bf16[768,576]{1,0:T(8,128)(2,1)}, u32[]{:S(2)}) copy-start(bf16[768,576]{1,0:T(8,128)(2,1)} %get-tuple-element.136.wqkv_ref) | copy-start | bytes 2654212
  132.6 8.4 %copy-start.12 = (f32[3,128,640]{2,1,0:T(8,128)S(1)}, f32[3,128,640]{2,1,0:T(8,128)}, u32[]{:S(2)}) copy-start(f32[3,128,640]{2,1,0:T(8,128)} %get-tuple-element.140.band_ref) | copy-start | bytes 2949124
  132.6 8.4 %copy-start.13 = (bf16[1024,384]{1,0:T(8,128)(2,1)S(1)}, bf16[1024,384]{1,0:T(8,128)(2,1)}, u32[]{:S(2)}) copy-start(bf16[1024,384]{1,0:T(8,128)(2,1)} %get-tuple-element.137.qe_ref) | copy-start | bytes 2359300
  132.6 8.4 %copy-start.14 = (bf16[1024,384]{1,0:T(8,128)(2,1)S(1)}, bf16[1024,384]{1,0:T(8,128)(2,1)}, u32[]{:S(2)}) copy-start(bf16[1024,384]{1,0:T(8,128)(2,1)} %get-tuple-element.138.ke_ref) | copy-start | bytes 2359300
  132.6 8.4 %copy-start.15 = (bf16[1024,192]{1,0:T(8,128)(2,1)S(1)}, bf16[1024,192]{1,0:T(8,128)(2,1)}, u32[]{:S(2)}) copy-start(bf16[1024,192]{1,0:T(8,128)(2,1)} %get-tuple-element.139.v_ref) | copy-start | bytes 1179652
  132.6 8.4 %copy-start.16 = (f32[4,128,128]{2,1,0:T(8,128)S(1)}, f32[4,128,128]{2,1,0:T(8,128)}, u32[]{:S(2)}) copy-start(f32[4,128,128]{2,1,0:T(8,128)} %get-tuple-element.141.lse_ref) | copy-start | bytes 786436
  135.0 4.7 %collective-permute-start.14 = (bf16[128,192]{1,0:T(8,128)(2,1)S(1)}, bf16[128,192]{1,0:T(8,128)(2,1)S(1)}, u32[]{:S(2)}, u32[]{:S(2)}) collective-permute-start(bf16[128,192]{1,0:T(8,128)(2,1)S(1)} %get-tuple-element.132), channel_id=1, source_target_pairs={{0,2},{1,3},{2,4},{3,5},{4,6},{5,7},{6,0},{7,1},{8,10},{9,11},{10,... | collective-permute-start | bytes 147464 | tf_op jit(solution)/shard_map/ppermute | solution.py:797
  135.0 5.3 %collective-permute-start.15 = (bf16[128,192]{1,0:T(8,128)(2,1)S(1)}, bf16[128,192]{1,0:T(8,128)(2,1)S(1)}, u32[]{:S(2)}, u32[]{:S(2)}) collective-permute-start(bf16[128,192]{1,0:T(8,128)(2,1)S(1)} %get-tuple-element.133), channel_id=1, source_target_pairs={{0,4},{1,5},{2,6},{3,7},{4,0},{5,1},{6,2},{7,3},{8,12},{9,13},{10,... | collective-permute-start | bytes 147464 | tf_op jit(solution)/shard_map/ppermute | solution.py:797
  137.1 3.8 %collective-permute-start.16 = (bf16[128,192]{1,0:T(8,128)(2,1)S(1)}, bf16[128,192]{1,0:T(8,128)(2,1)S(1)}, u32[]{:S(2)}, u32[]{:S(2)}) collective-permute-start(bf16[128,192]{1,0:T(8,128)(2,1)S(1)} %get-tuple-element.134), channel_id=1, source_target_pairs={{0,6},{1,7},{2,0},{3,1},{4,2},{5,3},{6,4},{7,5},{8,14},{9,15},{10,... | collective-permute-start | bytes 147464 | tf_op jit(solution)/shard_map/ppermute | solution.py:797
  137.9 20.0 %collective-permute-start.18 = (bf16[768,512]{1,0:T(8,128)(2,1)S(1)}, bf16[768,512]{1,0:T(8,128)(2,1)S(1)}, u32[]{:S(2)}, u32[]{:S(2)}) collective-permute-start(bf16[768,512]{1,0:T(8,128)(2,1)S(1)} %get-tuple-element.149), channel_id=1, source_target_pairs={{0,1},{1,0},{2,3},{3,2},{4,5},{5,4},{6,7},{7,6},{8,9},{9,8},{10,11... | collective-permute-start | bytes 2359304 | tf_op jit(solution)/shard_map/ppermute | solution.py:805
  152.7 5.2 %collective-permute-start.17 = (bf16[768,384]{1,0:T(8,128)(2,1)S(1)}, bf16[768,384]{1,0:T(8,128)(2,1)S(1)}, u32[]{:S(2)}, u32[]{:S(2)}) collective-permute-start(bf16[768,384]{1,0:T(8,128)(2,1)S(1)} %get-tuple-element.147), channel_id=1, source_target_pairs={{0,1},{1,0},{2,3},{3,2},{4,5},{5,4},{6,7},{7,6},{8,9},{9,8},{10,11... | collective-permute-start | bytes 1769480 | tf_op jit(solution)/shard_map/ppermute | solution.py:805
  155.1 4.2 %collective-permute-start.19 = (bf16[4,128,768]{2,1,0:T(8,128)(2,1)S(1)}, bf16[4,128,768]{2,1,0:T(8,128)(2,1)S(1)}, u32[]{:S(2)}, u32[]{:S(2)}) collective-permute-start(bf16[4,128,768]{2,1,0:T(8,128)(2,1)S(1)} %get-tuple-element.151), channel_id=1, source_target_pairs={{0,1},{1,0},{2,3},{3,2},{4,5},{5,4},{6,7},{7,6},{8,9},{9,8},{10,11... | collective-permute-start | bytes 2359304 | tf_op jit(solution)/shard_map/ppermute | solution.py:805
  160.8 25.8 %all-to-all-start.4 = ((bf16[16,48,896]{2,1,0:T(8,128)(2,1)}), bf16[16,48,896]{2,1,0:T(8,128)(2,1)S(1)}, u32[]{:S(2)}, u32[]{:S(2)}) async-start(bf16[16,48,896]{2,1,0:T(8,128)(2,1)} %bitcast.12), calls=%async_computation.4 | async-start | bytes 2752512 | tf_op jit(solution)/shard_map/all_to_all | solution.py:801
  164.5 27.9 %collective-permute-start.20 = (bf16[128,768]{1,0:T(8,128)(2,1)S(1)}, bf16[128,768]{1,0:T(8,128)(2,1)S(1)}, u32[]{:S(2)}, u32[]{:S(2)}) collective-permute-start(bf16[128,768]{1,0:T(8,128)(2,1)S(1)} %get-tuple-element.157), channel_id=1, source_target_pairs={{0,2},{1,3},{2,4},{3,5},{4,6},{5,7},{6,0},{7,1},{8,10},{9,11},{10,... | collective-permute-start | bytes 589832 | tf_op jit(solution)/shard_map/ppermute | solution.py:797
  165.6 26.8 %collective-permute-start.21 = (bf16[128,768]{1,0:T(8,128)(2,1)S(1)}, bf16[128,768]{1,0:T(8,128)(2,1)S(1)}, u32[]{:S(2)}, u32[]{:S(2)}) collective-permute-start(bf16[128,768]{1,0:T(8,128)(2,1)S(1)} %get-tuple-element.158), channel_id=1, source_target_pairs={{0,4},{1,5},{2,6},{3,7},{4,0},{5,1},{6,2},{7,3},{8,12},{9,13},{10,... | collective-permute-start | bytes 589832 | tf_op jit(solution)/shard_map/ppermute | solution.py:797
  167.8 24.6 %collective-permute-start.22 = (bf16[128,768]{1,0:T(8,128)(2,1)S(1)}, bf16[128,768]{1,0:T(8,128)(2,1)S(1)}, u32[]{:S(2)}, u32[]{:S(2)}) collective-permute-start(bf16[128,768]{1,0:T(8,128)(2,1)S(1)} %get-tuple-element.159), channel_id=1, source_target_pairs={{0,6},{1,7},{2,0},{3,1},{4,2},{5,3},{6,4},{7,5},{8,14},{9,15},{10,... | collective-permute-start | bytes 589832 | tf_op jit(solution)/shard_map/ppermute | solution.py:797
  187.5 10.0 %all-to-all-start.5 = ((bf16[8,8,896]{2,1,0:T(8,128)(2,1)}), bf16[8,8,896]{2,1,0:T(8,128)(2,1)S(1)}, u32[]{:S(2)}, u32[]{:S(2)}) async-start(bf16[8,8,896]{2,1,0:T(8,128)(2,1)} %bitcast.14), calls=%async_computation.5 | async-start | bytes 229376 | tf_op jit(solution)/shard_map/all_to_all | solution.py:801
  (12 other events, 22.1 us)
